TPU v7x, 32 devices: a whole 2x2x4 slice. The times are simulated.
32 devices in a mesh: case: 2 (over y), ax: 16 (over z, x, core).
Axes of the slice: x: 2, y: 2, z: 4, core: 2. Of those that a mesh axis runs over, the one named last changes fastest.
Arguments:
- checkpoint: float32 [32, 384, 1536], P(('case', 'ax')), parts along dimension 0, may hold values from -6 to 6
- cotangent: float32 [32, 384, 1536], P(('case', 'ax')), parts along dimension 0, may hold values from -6 to 6
- amplitudes: float32 [512], P('case'), parts along dimension 0, may hold values from -6 to 6
- patch_ids: int32 [32, 1536], P(('case', 'ax')), parts along dimension 0, may hold values from 0 to 255
- substep: int32 [2], P('case'), parts along dimension 0, may hold values from 0 to 2
- axial_speed: float32 [384], replicated, may hold values from 0.5 to 1.5
- radial_diffusion: float32 [384], replicated, may hold values from 0.05 to 0.3
- azimuth_diffusion: float32 [384], replicated, may hold values from 0.05 to 0.3
Outputs:
- advanced: float32 [32, 384, 1536], P(('case', 'ax')), parts along dimension 0
- adjoint_state: float32 [32, 384, 1536], P(('case', 'ax')), parts along dimension 0
- actuation_grad: float32 [512], P('case'), parts along dimension 0
There are 2 independent parts, one for each index of `case`. A program takes and returns all parts, laid end to end along the dimension named above; an argument that names none is the same for every part. Nothing has to cross between parts.
All inputs are finite; a program needn't handle non-finite values.
Results may differ from a plain program's by a relative error of at most 0.00002.
Values sent between devices are 32-bit elements; how exact they have to be, the bound alone decides.
No kernel may reach another device: no remote copies, remote signals or barrier semaphores. Data moves between devices by JAX's collectives and lax.ppermute only.
A program may use at most 64 MiB of HBM per device.

v0:
```python
import math

import jax
import jax.numpy as jnp
from jax import lax
from jax.experimental import pallas as pl
from jax.experimental.pallas import tpu as pltpu
from jax.sharding import PartitionSpec as P

time_step = 0.6
dissipation = 2.0

STATE_PARTS = 48
STATE_CUTS = (0, 33, 44, 48)
LOCAL_ROWS = 64
ADD_ROWS = 88
SUB = 8


def section_size(substep):
    section_table = jnp.array([1.0 / 3.0, 15.0 / 16.0, 8.0 / 15.0], jnp.float32) * time_step
    selector = (jnp.arange(3, dtype=jnp.int32) == substep[0]).astype(jnp.float32)
    return jnp.sum(section_table * selector)


def on_pairs(count):
    return [(i, i ^ 1) for i in range(count)]


def off_pairs(count):
    return [(i, (i + 1) % count if i % 2 else (i - 1) % count) for i in range(count)]


def cell_sum(value, axis):
    count = lax.axis_size(axis)
    direct = [i for i in range(count) if i % 4 in (1, 2)]
    turning = [i for i in range(count) if i % 4 in (0, 3)]
    place = lax.axis_index(axis) % 4
    turns = (place == 0) | (place == 3)
    value = value + lax.ppermute(value, axis, [(i, i ^ 1) for i in range(count)])
    for n in range(2, count.bit_length() - 1):
        value = value + lax.ppermute(value, axis, [(i, i ^ (1 << n)) for i in direct])
    given = lax.ppermute(value, axis, [(i, i ^ 1) for i in direct])
    value = given + lax.ppermute(given, axis, [(i, i ^ 3) for i in turning])
    return jnp.where(turns, value, lax.ppermute(value, axis, [(i, i ^ 1) for i in turning]))


def wall_kernel(ids, amplitudes, edge, wall, bins):
    patches, cells = amplitudes.shape[1], ids.shape[1]
    patch = lax.broadcasted_iota(jnp.int32, (patches, cells), 0)
    hit = jnp.where(patch == ids[...], 1.0, 0.0).astype(jnp.float32)
    values = jnp.broadcast_to(amplitudes[...], (SUB, patches))
    wall[...] = lax.dot_general(
        values,
        hit,
        (((1,), (0,)), ((), ())),
        precision=lax.Precision.HIGHEST,
        preferred_element_type=jnp.float32,
    )[:1]
    bins[...] = lax.dot_general(
        edge[0],
        hit,
        (((1,), (1,)), ((), ())),
        precision=lax.Precision.HIGHEST,
        preferred_element_type=jnp.float32,
    )[SUB - 1 :]


def wall_and_bins(patch_ids, amplitudes, cotangent):
    rows, cells = cotangent.shape[1:]
    patches = amplitudes.shape[0]
    return pl.pallas_call(
        wall_kernel,
        grid=(1,),
        out_shape=(
            jax.ShapeDtypeStruct((1, cells), jnp.float32),
            jax.ShapeDtypeStruct((1, patches), jnp.float32),
        ),
        in_specs=[
            pl.BlockSpec((1, cells), lambda i: (0, 0)),
            pl.BlockSpec((1, patches), lambda i: (0, 0)),
            pl.BlockSpec((1, SUB, cells), lambda i: (0, rows // SUB - 1, 0)),
        ],
        out_specs=(
            pl.BlockSpec((1, cells), lambda i: (0, 0)),
            pl.BlockSpec((1, patches), lambda i: (0, 0)),
        ),
        compiler_params=pltpu.CompilerParams(vmem_limit_bytes=40 << 20),
    )(patch_ids, amplitudes[None], cotangent)


def local_kernel(scal, q, q_up, q_down, q_near, c, c_up, c_down, c_near, c_far, wall, coef, q_out, c_out):
    block, width = q.shape[1:]
    step, side = scal[0], scal[1]
    here, last = pl.program_id(0), pl.num_programs(0) - 1
    u, rd, ad = coef[:, 0:1], coef[:, 1:2], coef[:, 2:3]
    row = lax.broadcasted_iota(jnp.int32, (block, 1), 0)

    def around(x, up, down):
        above = jnp.where(row == 0, up, pltpu.roll(x, 1, 0))
        below = jnp.where(row == block - 1, down, pltpu.roll(x, block - 1, 0))
        return above, below

    def sides(x):
        return pltpu.roll(x, 1, 1) + pltpu.roll(x, width - 1, 1)

    x = q[0]
    first_row = pltpu.roll(x[:1], width // 2, 1)
    up = jnp.where(here == 0, first_row, q_up[0, SUB - 1 :])
    down = jnp.where(here == last, wall[...], q_down[0, :1])
    above, below = around(x, up, down)
    near = q_near[0]
    axial = near - (0.5 * side) * (near * (u + 0.5 * near)) - dissipation * x
    q_out[0] = x + step * (
        axial + rd * (above + below - 2.0 * x) + ad * (sides(x) - 2.0 * x)
    )

    y = c[0]
    weighted = rd * y
    before, after = coef_rows(coef)
    first_row = pltpu.roll(weighted[:1], width // 2, 1)
    up = jnp.where(here == 0, first_row, before * c_up[0, SUB - 1 :])
    down = jnp.where(here == last, 0.0, after * c_down[0, :1])
    above, below = around(weighted, up, down)
    slope = (0.5 * side) * (u + x)
    axial = c_near[0] * (1.0 + slope) + c_far[0] * (1.0 - slope) - dissipation * y
    c_out[0] = y + step * (
        axial + (above + below - 2.0 * weighted) + ad * (sides(y) - 2.0 * y)
    )


def coef_rows(coef):
    return coef[0:1, 3:4], coef[0:1, 4:5]


def local_parts(scal, q, q_near, c, c_near, c_far, wall, coef):
    rows, width = q.shape[1:]
    block = math.gcd(LOCAL_ROWS, rows)
    tiles, total = block // SUB, rows // SUB
    full = pl.BlockSpec((1, block, width), lambda i: (0, i, 0))
    up = pl.BlockSpec((1, SUB, width), lambda i: (0, jnp.maximum(i * tiles - 1, 0), 0))
    down = pl.BlockSpec((1, SUB, width), lambda i: (0, jnp.minimum((i + 1) * tiles, total - 1), 0))
    rd = coef[:, 1]
    before, after = jnp.roll(rd, 1), jnp.roll(rd, -block)
    coef = jnp.concatenate([coef, before[:, None], after[:, None]], axis=1)
    shape = jax.ShapeDtypeStruct(q.shape, q.dtype)
    return pl.pallas_call(
        local_kernel,
        grid=(rows // block,),
        out_shape=(shape, shape),
        in_specs=[pl.BlockSpec(memory_space=pltpu.SMEM)]
        + [full, up, down, full] * 2
        + [full]
        + [pl.BlockSpec((1, width), lambda i: (0, 0))]
        + [pl.BlockSpec((block, coef.shape[1]), lambda i: (i, 0))],
        out_specs=(full, full),
        compiler_params=pltpu.CompilerParams(vmem_limit_bytes=40 << 20),
        cost_estimate=pl.CostEstimate(
            flops=50 * rows * width, bytes_accessed=4 * rows * width * 7, transcendentals=0
        ),
    )(scal, q, q, q, q_near, c, c, c, c_near, c_far, wall, coef)


def state_far(scal, base, far, coef, out):
    step, side = scal[0], scal[1]
    x = far[0]
    out[0] = base[0] + step * (x + (0.5 * side) * (x * (coef[:, 0:1] + 0.5 * x)))


def add_rows(scal, base, part, coef, start):
    rows, width = part.shape[1:]
    whole = rows <= ADD_ROWS and start % rows == 0
    block = rows if whole else math.gcd(ADD_ROWS, rows, start)
    first = start // block
    full = pl.BlockSpec((1, block, width), lambda i: (0, first + i, 0))
    piece = pl.BlockSpec((1, block, width), lambda i: (0, i, 0))
    column = pl.BlockSpec((block, coef.shape[1]), lambda i: (first + i, 0))
    return pl.pallas_call(
        state_far,
        grid=(rows // block,),
        out_shape=jax.ShapeDtypeStruct(base.shape, base.dtype),
        in_specs=[pl.BlockSpec(memory_space=pltpu.SMEM), full, piece, column],
        out_specs=full,
        input_output_aliases={1: 0},
        compiler_params=pltpu.CompilerParams(vmem_limit_bytes=40 << 20),
        cost_estimate=pl.CostEstimate(
            flops=10 * rows * width, bytes_accessed=4 * rows * width * 3, transcendentals=0
        ),
    )(scal, base, part, coef)


def local(
    checkpoint,
    cotangent,
    amplitudes,
    patch_ids,
    substep,
    axial_speed,
    radial_diffusion,
    azimuth_diffusion,
):
    count = lax.axis_size("ax")
    rows = checkpoint.shape[1]
    patches = amplitudes.shape[0]
    near, far = on_pairs(count), off_pairs(count)
    cot_far_rows = lax.ppermute(cotangent, "ax", far)
    cot_near_rows = lax.ppermute(cotangent, "ax", near)
    state_near_rows = lax.ppermute(checkpoint, "ax", near)

    wall, binned = wall_and_bins(patch_ids, amplitudes, cotangent)
    if count & (count - 1) or count < 4:
        binned = lax.psum(binned, "ax")
    else:
        binned = cell_sum(binned, "ax")

    late, binned = lax.optimization_barrier((checkpoint, binned))
    edges = [rows * n // STATE_PARTS for n in STATE_CUTS]
    state_far_rows = [
        lax.ppermute(late[:, low:high], "ax", far) for low, high in zip(edges, edges[1:])
    ]

    step_size = section_size(substep)
    side = 1.0 - 2.0 * (lax.axis_index("ax") % 2).astype(jnp.float32)
    total_cells = checkpoint.shape[0] * count * checkpoint.shape[2]
    norm_factor = (patches / total_cells) ** 0.5
    gradient = (step_size * radial_diffusion[-1] * norm_factor) * binned[0]
    scal = jnp.stack([step_size, side])
    coef = jnp.stack([axial_speed, radial_diffusion, azimuth_diffusion], axis=1)

    cot_far_rows, cot_near_rows, state_near_rows = lax.optimization_barrier(
        (cot_far_rows, cot_near_rows, state_near_rows)
    )
    advanced, adjoint = local_parts(
        scal, checkpoint, state_near_rows, cotangent, cot_near_rows, cot_far_rows, wall, coef
    )
    for low, part in zip(edges, state_far_rows):
        advanced = add_rows(scal, advanced, part, coef, low)
    return (advanced, adjoint, gradient)


def solution(mesh):
    placed = (
        P(("case", "ax"), None, None),
        P(("case", "ax"), None, None),
        P("case"),
        P(("case", "ax"), None),
        P("case"),
        P(),
        P(),
        P(),
    )
    return jax.shard_map(
        local,
        mesh=mesh,
        in_specs=placed,
        out_specs=(P(("case", "ax"), None, None), P(("case", "ax"), None, None), P("case")),
        check_vma=False,
    )
```

profile of v0, /device:TPU:1, one launch (start us, length us, event | category | flops | bytes accessed | tf_op | source)
XLA Modules:
  0.0 107.6 jit_solution(17518416405576973177)
XLA Ops:
  0.6 0.0 copy-start
  0.6 2.7 %collective-permute-start = (f32[1,384,1536]{2,1,0:T(8,128)}, f32[1,384,1536]{2,1,0:T(8,128)}, u32[]{:S(2)}, u32[]{:S(2)}) collective-permute-start(f32[1,384,1536]{2,1,0:T(8,128)} %c_down.1), channel_id=1, source_target_pairs={{0,15},{1,2},{2,1},{3,4},{4,3},{5,6},{6,5},{7,8},{8,7},{9,10},{10,... | collective-permute-start | bytes 7077896 | tf_op jit(solution)/shard_map/ppermute | solution.py:206
  3.3 2.9 %collective-permute-start.1 = (f32[1,384,1536]{2,1,0:T(8,128)}, f32[1,384,1536]{2,1,0:T(8,128)}, u32[]{:S(2)}, u32[]{:S(2)}) collective-permute-start(f32[1,384,1536]{2,1,0:T(8,128)} %c_down.1), channel_id=1, source_target_pairs={{0,1},{1,0},{2,3},{3,2},{4,5},{5,4},{6,7},{7,6},{8,9},{9,8},{10,11... | collective-permute-start | bytes 7077896 | tf_op jit(solution)/shard_map/ppermute | solution.py:207
  6.2 0.0 collective-permute-start.2
  6.2 1.7 %copy-done.1 = f32[1,384,1536]{2,1,0:T(8,128)S(1)} copy-done((f32[1,384,1536]{2,1,0:T(8,128)S(1)}, f32[1,384,1536]{2,1,0:T(8,128)}, u32[]{:S(2)}) %copy-start.1) | copy-done | bytes 2359320
  7.9 0.7 copy-done.3
  8.5 0.7 copy-done.4
  9.2 2.2 %shard_map.112 = (f32[1,1536]{1,0:T(1,128)S(1)}, f32[1,256]{1,0:T(1,128)S(1)}) custom-call(s32[1,1536]{1,0:T(1,128)S(1)} %copy-done.3, f32[1,256]{1,0:T(1,128)S(1)} %bitcast.8, f32[1,384,1536]{2,1,0:T(8,128)S(1)} %copy-done.1), custom_call_target="tpu_custom_call" | custom-call | tf_op jit(solution)/shard_map/pallas_call | solution.py:72
  11.4 0.5 collective-permute-start.3
  12.0 1.8 %collective-permute-done.3 = f32[1,256]{1,0:T(1,128)S(1)} collective-permute-done((f32[1,256]{1,0:T(1,128)S(1)}, f32[1,256]{1,0:T(1,128)S(1)}, u32[]{:S(2)}, u32[]{:S(2)}) %collective-permute-start.3) | collective-permute-done | bytes 1056 | tf_op jit(solution)/shard_map/ppermute | solution.py:40
  13.7 1.9 %collective-permute-start.4 = (f32[1,256]{1,0:T(1,128)S(1)}, f32[1,256]{1,0:T(1,128)S(1)}, u32[]{:S(2)}, u32[]{:S(2)}) collective-permute-start(f32[1,256]{1,0:T(1,128)S(1)} %add.21), channel_id=1, source_target_pairs={{1,5},{2,6},{5,1},{6,2},{9,13},{10,14},{13,9},{14,10},{17,21},{18,... | collective-permute-start | bytes 3080 | tf_op jit(solution)/shard_map/ppermute | solution.py:42
  15.6 2.9 %collective-permute-done.4 = f32[1,256]{1,0:T(1,128)S(1)} collective-permute-done((f32[1,256]{1,0:T(1,128)S(1)}, f32[1,256]{1,0:T(1,128)S(1)}, u32[]{:S(2)}, u32[]{:S(2)}) %collective-permute-start.4) | collective-permute-done | bytes 1056 | tf_op jit(solution)/shard_map/ppermute | solution.py:42
  18.5 1.9 %collective-permute-start.5 = (f32[1,256]{1,0:T(1,128)S(1)}, f32[1,256]{1,0:T(1,128)S(1)}, u32[]{:S(2)}, u32[]{:S(2)}) collective-permute-start(f32[1,256]{1,0:T(1,128)S(1)} %add.22), channel_id=1, source_target_pairs={{1,9},{2,10},{5,13},{6,14},{9,1},{10,2},{13,5},{14,6},{17,25},{18,... | collective-permute-start | bytes 3080 | tf_op jit(solution)/shard_map/ppermute | solution.py:42
  20.4 3.8 %collective-permute-done.5 = f32[1,256]{1,0:T(1,128)S(1)} collective-permute-done((f32[1,256]{1,0:T(1,128)S(1)}, f32[1,256]{1,0:T(1,128)S(1)}, u32[]{:S(2)}, u32[]{:S(2)}) %collective-permute-start.5) | collective-permute-done | bytes 1056 | tf_op jit(solution)/shard_map/ppermute | solution.py:42
  24.2 1.3 %collective-permute-start.6 = (f32[1,256]{1,0:T(1,128)S(1)}, f32[1,256]{1,0:T(1,128)S(1)}, u32[]{:S(2)}, u32[]{:S(2)}) collective-permute-start(f32[1,256]{1,0:T(1,128)S(1)} %add.23), channel_id=1, source_target_pairs={{1,0},{2,3},{5,4},{6,7},{9,8},{10,11},{13,12},{14,15},{17,16},{18,... | collective-permute-start | bytes 3080 | tf_op jit(solution)/shard_map/ppermute | solution.py:43
  25.5 0.8 collective-permute-done.6
  26.3 0.6 collective-permute-start.7
  26.9 0.0 collective-permute-done.7
  27.0 1.3 %collective-permute-start.8 = (f32[1,256]{1,0:T(1,128)S(1)}, f32[1,256]{1,0:T(1,128)S(1)}, u32[]{:S(2)}, u32[]{:S(2)}) collective-permute-start(f32[1,256]{1,0:T(1,128)S(1)} %add.24), channel_id=1, source_target_pairs={{0,1},{3,2},{4,5},{7,6},{8,9},{11,10},{12,13},{15,14},{16,17},{19,... | collective-permute-start | bytes 3080 | tf_op jit(solution)/shard_map/ppermute | solution.py:45
  28.3 6.7 %collective-permute-done.8 = f32[1,256]{1,0:T(1,128)S(1)} collective-permute-done((f32[1,256]{1,0:T(1,128)S(1)}, f32[1,256]{1,0:T(1,128)S(1)}, u32[]{:S(2)}, u32[]{:S(2)}) %collective-permute-start.8) | collective-permute-done | bytes 1056 | tf_op jit(solution)/shard_map/ppermute | solution.py:45
  35.0 0.0 copy-done
  35.0 1.4 %slice.30 = f32[1,264,1536]{2,1,0:T(8,128)} slice(f32[1,384,1536]{2,1,0:T(8,128)S(1)} %copy-done), slice={[0:1], [0:264], [0:1536]} | slice | bytes 3244032 | tf_op jit(solution)/shard_map/slice | solution.py:219
  36.4 0.0 collective-permute-start.9
  36.4 0.0 copy-done.5
  36.4 0.6 slice.26
  37.0 0.1 slice.28
  37.7 0.0 copy-done.6
  37.8 0.6 pad_maximum_fusion.1
  38.4 0.1 pad_maximum_fusion.2
  38.5 0.1 copy.23.coef
  38.7 0.9 slice.31
  39.5 1.7 %collective-permute-start.10 = (f32[1,88,1536]{2,1,0:T(8,128)}, f32[1,88,1536]{2,1,0:T(8,128)S(1)}, u32[]{:S(2)}, u32[]{:S(2)}) collective-permute-start(f32[1,88,1536]{2,1,0:T(8,128)} %slice.31), channel_id=1, source_target_pairs={{0,15},{1,2},{2,1},{3,4},{4,3},{5,6},{6,5},{7,8},{8,7},{9,10},{10,... | collective-permute-start | bytes 1622024 | tf_op jit(solution)/shard_map/ppermute | solution.py:219
  41.3 0.1 copy.24.coef
  41.4 0.6 fusion
  43.2 0.7 pad_maximum_fusion.3.scal
  44.0 36.7 %collective-permute-done.c_far = f32[1,384,1536]{2,1,0:T(8,128)} collective-permute-done((f32[1,384,1536]{2,1,0:T(8,128)}, f32[1,384,1536]{2,1,0:T(8,128)}, u32[]{:S(2)}, u32[]{:S(2)}) %collective-permute-start) | collective-permute-done | bytes 2359328 | tf_op jit(solution)/shard_map/ppermute | solution.py:206
  80.7 1.7 %collective-permute-start.11 = (f32[1,32,1536]{2,1,0:T(8,128)S(1)}, f32[1,32,1536]{2,1,0:T(8,128)S(1)}, u32[]{:S(2)}, u32[]{:S(2)}) collective-permute-start(f32[1,32,1536]{2,1,0:T(8,128)S(1)} %slice.32), channel_id=1, source_target_pairs={{0,15},{1,2},{2,1},{3,4},{4,3},{5,6},{6,5},{7,8},{8,7},{9,10},{10,... | collective-permute-start | bytes 589832 | tf_op jit(solution)/shard_map/ppermute | solution.py:219
  82.5 0.6 broadcast_multiply_fusion
  83.0 0.0 collective-permute-done.1.c_near
  83.0 0.0 collective-permute-done.2.q_near
  83.0 1.7 %copy-done.2 = f32[1,384,1536]{2,1,0:T(8,128)S(1)} copy-done((f32[1,384,1536]{2,1,0:T(8,128)S(1)}, f32[1,384,1536]{2,1,0:T(8,128)}, u32[]{:S(2)}) %copy-start.2) | copy-done | bytes 2359320
  84.7 8.2 %shard_map.113 = (f32[1,384,1536]{2,1,0:T(8,128)}, f32[1,384,1536]{2,1,0:T(8,128)}) custom-call(f32[2]{0:T(128)S(1)} %pad_maximum_fusion.3.scal, f32[1,384,1536]{2,1,0:T(8,128)S(1)} %copy-done, f32[1,384,1536]{2,1,0:T(8,128)S(1)} %copy-done, f32[1,384,1536]{2,1,0:T(8,128)S(1)} %copy-done, f32[1,384,1536]{2,1,0:T(8,128)} %collective-permute-done.2.q_near, ...), custom_call_target="tpu_custom_call" | custom-call | flops 29491200 | bytes 16515072 | tf_op jit(solution)/shard_map/pallas_call | solution.py:147
  92.9 5.2 %collective-permute-done.9.far = f32[1,264,1536]{2,1,0:T(8,128)} collective-permute-done((f32[1,264,1536]{2,1,0:T(8,128)}, f32[1,264,1536]{2,1,0:T(8,128)}, u32[]{:S(2)}, u32[]{:S(2)}) %collective-permute-start.9) | collective-permute-done | bytes 1622048 | tf_op jit(solution)/shard_map/ppermute | solution.py:219
  98.1 4.1 %shard_map.114.base = f32[1,384,1536]{2,1,0:T(8,128)} custom-call(f32[2]{0:T(128)S(1)} %pad_maximum_fusion.3.scal, f32[1,384,1536]{2,1,0:T(8,128)} %get-tuple-element.16.base, f32[1,264,1536]{2,1,0:T(8,128)} %collective-permute-done.9.far, f32[384,3]{1,0:T(8,128)S(1)} %copy.24.coef), custom_call_target="tpu_custom_call", output_to_operand_aliasing={{}: (1, {})} | custom-call | flops 4055040 | bytes 4866048 | tf_op jit(solution)/shard_map/pallas_call | solution.py:178
  102.2 1.6 %collective-permute-done.10.far = f32[1,88,1536]{2,1,0:T(8,128)S(1)} collective-permute-done((f32[1,88,1536]{2,1,0:T(8,128)}, f32[1,88,1536]{2,1,0:T(8,128)S(1)}, u32[]{:S(2)}, u32[]{:S(2)}) %collective-permute-start.10) | collective-permute-done | bytes 540704 | tf_op jit(solution)/shard_map/ppermute | solution.py:219
  103.8 2.0 %shard_map.115.base = f32[1,384,1536]{2,1,0:T(8,128)} custom-call(f32[2]{0:T(128)S(1)} %pad_maximum_fusion.3.scal, f32[1,384,1536]{2,1,0:T(8,128)} %shard_map.114.base, f32[1,88,1536]{2,1,0:T(8,128)S(1)} %collective-permute-done.10.far, f32[384,3]{1,0:T(8,128)S(1)} %copy.24.coef), custom_call_target="tpu_custom_call", output_to_operand_aliasing={{}: (1, {})} | custom-call | flops 1351680 | bytes 1622016 | tf_op jit(solution)/shard_map/pallas_call | solution.py:178
  105.8 0.1 collective-permute-done.11.far
  105.9 1.7 %shard_map.116 = f32[1,384,1536]{2,1,0:T(8,128)} custom-call(f32[2]{0:T(128)S(1)} %pad_maximum_fusion.3.scal, f32[1,384,1536]{2,1,0:T(8,128)} %shard_map.115.base, f32[1,32,1536]{2,1,0:T(8,128)S(1)} %collective-permute-done.11.far, f32[384,3]{1,0:T(8,128)S(1)} %copy.24.coef), custom_call_target="tpu_custom_call", output_to_operand_aliasing={{}: (1, {})} | custom-call | flops 491520 | bytes 589824 | tf_op jit(solution)/shard_map/pallas_call | solution.py:178
  (24 shorter events, 0.1 us)
Async XLA Ops:
  0.6 34.4 %copy-start = (f32[1,384,1536]{2,1,0:T(8,128)S(1)}, f32[1,384,1536]{2,1,0:T(8,128)}, u32[]{:S(2)}) copy-start(f32[1,384,1536]{2,1,0:T(8,128)} %q_down.1) | copy-start | bytes 7077892
  0.6 80.1 %collective-permute-start = (f32[1,384,1536]{2,1,0:T(8,128)}, f32[1,384,1536]{2,1,0:T(8,128)}, u32[]{:S(2)}, u32[]{:S(2)}) collective-permute-start(f32[1,384,1536]{2,1,0:T(8,128)} %c_down.1), channel_id=1, source_target_pairs={{0,15},{1,2},{2,1},{3,4},{4,3},{5,6},{6,5},{7,8},{8,7},{9,10},{10,... | collective-permute-start | bytes 7077896 | tf_op jit(solution)/shard_map/ppermute | solution.py:206
  3.3 79.7 %collective-permute-start.1 = (f32[1,384,1536]{2,1,0:T(8,128)}, f32[1,384,1536]{2,1,0:T(8,128)}, u32[]{:S(2)}, u32[]{:S(2)}) collective-permute-start(f32[1,384,1536]{2,1,0:T(8,128)} %c_down.1), channel_id=1, source_target_pairs={{0,1},{1,0},{2,3},{3,2},{4,5},{5,4},{6,7},{7,6},{8,9},{9,8},{10,11... | collective-permute-start | bytes 7077896 | tf_op jit(solution)/shard_map/ppermute | solution.py:207
  6.2 76.9 %collective-permute-start.2 = (f32[1,384,1536]{2,1,0:T(8,128)}, f32[1,384,1536]{2,1,0:T(8,128)}, u32[]{:S(2)}, u32[]{:S(2)}) collective-permute-start(f32[1,384,1536]{2,1,0:T(8,128)} %q_down.1), channel_id=1, source_target_pairs={{0,1},{1,0},{2,3},{3,2},{4,5},{5,4},{6,7},{7,6},{8,9},{9,8},{10,11... | collective-permute-start | bytes 7077896 | tf_op jit(solution)/shard_map/ppermute | solution.py:208
  6.2 1.7 %copy-start.1 = (f32[1,384,1536]{2,1,0:T(8,128)S(1)}, f32[1,384,1536]{2,1,0:T(8,128)}, u32[]{:S(2)}) copy-start(f32[1,384,1536]{2,1,0:T(8,128)} %c_down.1) | copy-start | bytes 7077892
  7.9 0.7 copy-start.3
  8.5 0.7 copy-start.4
  9.2 27.2 %copy-start.5 = (f32[384]{0:T(512)S(1)}, f32[384]{0:T(512)}, u32[]{:S(2)}) copy-start(f32[384]{0:T(512)} %param.15) | copy-start | bytes 4612
  9.2 28.5 %copy-start.6 = (f32[384]{0:T(512)S(1)}, f32[384]{0:T(512)}, u32[]{:S(2)}) copy-start(f32[384]{0:T(512)} %param.14) | copy-start | bytes 4612
  9.2 28.5 %copy-start.7 = (f32[384]{0:T(512)S(1)}, f32[384]{0:T(512)}, u32[]{:S(2)}) copy-start(f32[384]{0:T(512)} %param.16) | copy-start | bytes 4612
  11.4 2.3 %collective-permute-start.3 = (f32[1,256]{1,0:T(1,128)S(1)}, f32[1,256]{1,0:T(1,128)S(1)}, u32[]{:S(2)}, u32[]{:S(2)}) collective-permute-start(f32[1,256]{1,0:T(1,128)S(1)} %get-tuple-element.17), channel_id=1, source_target_pairs={{0,1},{1,0},{2,3},{3,2},{4,5},{5,4},{6,7},{7,6},{8,9},{9,8},{10,11... | collective-permute-start | bytes 3080 | tf_op jit(solution)/shard_map/ppermute | solution.py:40
  13.7 4.8 %collective-permute-start.4 = (f32[1,256]{1,0:T(1,128)S(1)}, f32[1,256]{1,0:T(1,128)S(1)}, u32[]{:S(2)}, u32[]{:S(2)}) collective-permute-start(f32[1,256]{1,0:T(1,128)S(1)} %add.21), channel_id=1, source_target_pairs={{1,5},{2,6},{5,1},{6,2},{9,13},{10,14},{13,9},{14,10},{17,21},{18,... | collective-permute-start | bytes 3080 | tf_op jit(solution)/shard_map/ppermute | solution.py:42
  18.5 5.7 %collective-permute-start.5 = (f32[1,256]{1,0:T(1,128)S(1)}, f32[1,256]{1,0:T(1,128)S(1)}, u32[]{:S(2)}, u32[]{:S(2)}) collective-permute-start(f32[1,256]{1,0:T(1,128)S(1)} %add.22), channel_id=1, source_target_pairs={{1,9},{2,10},{5,13},{6,14},{9,1},{10,2},{13,5},{14,6},{17,25},{18,... | collective-permute-start | bytes 3080 | tf_op jit(solution)/shard_map/ppermute | solution.py:42
  24.2 2.1 %collective-permute-start.6 = (f32[1,256]{1,0:T(1,128)S(1)}, f32[1,256]{1,0:T(1,128)S(1)}, u32[]{:S(2)}, u32[]{:S(2)}) collective-permute-start(f32[1,256]{1,0:T(1,128)S(1)} %add.23), channel_id=1, source_target_pairs={{1,0},{2,3},{5,4},{6,7},{9,8},{10,11},{13,12},{14,15},{17,16},{18,... | collective-permute-start | bytes 3080 | tf_op jit(solution)/shard_map/ppermute | solution.py:43
  26.3 0.7 collective-permute-start.7
  27.0 8.1 %collective-permute-start.8 = (f32[1,256]{1,0:T(1,128)S(1)}, f32[1,256]{1,0:T(1,128)S(1)}, u32[]{:S(2)}, u32[]{:S(2)}) collective-permute-start(f32[1,256]{1,0:T(1,128)S(1)} %add.24), channel_id=1, source_target_pairs={{0,1},{3,2},{4,5},{7,6},{8,9},{11,10},{12,13},{15,14},{16,17},{19,... | collective-permute-start | bytes 3080 | tf_op jit(solution)/shard_map/ppermute | solution.py:45
  35.0 6.4 %copy-start.8 = (f32[3]{0:T(128)S(1)}, f32[3]{0:T(128)}, u32[]{:S(2)}) copy-start(f32[3]{0:T(128)} %constant.47) | copy-start | bytes 40
  36.4 61.7 %collective-permute-start.9 = (f32[1,264,1536]{2,1,0:T(8,128)}, f32[1,264,1536]{2,1,0:T(8,128)}, u32[]{:S(2)}, u32[]{:S(2)}) collective-permute-start(f32[1,264,1536]{2,1,0:T(8,128)} %slice.30), channel_id=1, source_target_pairs={{0,15},{1,2},{2,1},{3,4},{4,3},{5,6},{6,5},{7,8},{8,7},{9,10},{10,... | collective-permute-start | bytes 4866056 | tf_op jit(solution)/shard_map/ppermute | solution.py:219
  39.5 64.3 %collective-permute-start.10 = (f32[1,88,1536]{2,1,0:T(8,128)}, f32[1,88,1536]{2,1,0:T(8,128)S(1)}, u32[]{:S(2)}, u32[]{:S(2)}) collective-permute-start(f32[1,88,1536]{2,1,0:T(8,128)} %slice.31), channel_id=1, source_target_pairs={{0,15},{1,2},{2,1},{3,4},{4,3},{5,6},{6,5},{7,8},{8,7},{9,10},{10,... | collective-permute-start | bytes 1622024 | tf_op jit(solution)/shard_map/ppermute | solution.py:219
  80.7 25.2 %collective-permute-start.11 = (f32[1,32,1536]{2,1,0:T(8,128)S(1)}, f32[1,32,1536]{2,1,0:T(8,128)S(1)}, u32[]{:S(2)}, u32[]{:S(2)}) collective-permute-start(f32[1,32,1536]{2,1,0:T(8,128)S(1)} %slice.32), channel_id=1, source_target_pairs={{0,15},{1,2},{2,1},{3,4},{4,3},{5,6},{6,5},{7,8},{8,7},{9,10},{10,... | collective-permute-start | bytes 589832 | tf_op jit(solution)/shard_map/ppermute | solution.py:219
  83.0 1.7 %copy-start.2 = (f32[1,384,1536]{2,1,0:T(8,128)S(1)}, f32[1,384,1536]{2,1,0:T(8,128)}, u32[]{:S(2)}) copy-start(f32[1,384,1536]{2,1,0:T(8,128)} %c_down.1) | copy-start | bytes 7077892
where the time goes:
time: 108 us
  waiting for transfers between devices  59.6 us (55%)
  Pallas kernels  18.2 us (17%)
  starting transfers between devices  16.6 us (15%)
  local copies, waits for them, and re-layouts  7.93 us (7%)
  between operations  2.68 us (2%)
  other arithmetic  2.62 us (2%)
    ppermute x1, waiting for transfers between devices, local(): cot_far_rows = lax.ppermute(cotangent, 'ax', far)  36.7 us
    pallas_call x1, Pallas kernels, local_parts(): pl.pallas_call(local_kernel, grid=(rows // block,), out_shape=(shape, sha...  8.21 us
    pallas_call x3, Pallas kernels, add_rows(): pl.pallas_call(state_far, grid=(rows // block,), out_shape=jax.ShapeDtype...  7.84 us
    ppermute x3, waiting for transfers between devices, local(): lax.ppermute(late[:, low:high], 'ax', far)  6.88 us
    ppermute x1, waiting for transfers between devices, cell_sum(): lax.ppermute(value, axis, [(i, i ^ 1) for i in turning])  6.74 us
    ppermute x2, waiting for transfers between devices, cell_sum(): value = value + lax.ppermute(value, axis, [(i, i ^ 1 << n) for i in direct])  6.62 us
    unnamed x18, local copies, waits for them, and re-layouts  4.72 us
    ppermute x2, starting transfers between devices, cell_sum(): value = value + lax.ppermute(value, axis, [(i, i ^ 1 << n) for i in direct])  3.82 us
  transfers between devices with their start and end apart: 12, of which 9 were waited for; matrix products, arithmetic and copies ran while one was open for 5% of the time, Pallas kernels for 15%

commit v1 on v0

--- a/solution.py
+++ b/solution.py
@@ -161,32 +161,71 @@
     )(scal, q, q, q, q_near, c, c, c, c_near, c_far, wall, coef)
 
 
-def state_far(scal, base, far, coef, out):
-    step, side = scal[0], scal[1]
+def state_far(base, far, weight, out):
     x = far[0]
-    out[0] = base[0] + step * (x + (0.5 * side) * (x * (coef[:, 0:1] + 0.5 * x)))
-
-
-def add_rows(scal, base, part, coef, start):
+    out[0] = base[0] + x * (weight[:, 0:1] + weight[:, 1:2] * x)
+
+
+def add_rows(base, part, weight, start):
     rows, width = part.shape[1:]
     whole = rows <= ADD_ROWS and start % rows == 0
     block = rows if whole else math.gcd(ADD_ROWS, rows, start)
     first = start // block
     full = pl.BlockSpec((1, block, width), lambda i: (0, first + i, 0))
     piece = pl.BlockSpec((1, block, width), lambda i: (0, i, 0))
-    column = pl.BlockSpec((block, coef.shape[1]), lambda i: (first + i, 0))
+    column = pl.BlockSpec((block, weight.shape[1]), lambda i: (first + i, 0))
     return pl.pallas_call(
         state_far,
         grid=(rows // block,),
         out_shape=jax.ShapeDtypeStruct(base.shape, base.dtype),
-        in_specs=[pl.BlockSpec(memory_space=pltpu.SMEM), full, piece, column],
+        in_specs=[full, piece, column],
         out_specs=full,
-        input_output_aliases={1: 0},
+        input_output_aliases={0: 0},
         compiler_params=pltpu.CompilerParams(vmem_limit_bytes=40 << 20),
         cost_estimate=pl.CostEstimate(
             flops=10 * rows * width, bytes_accessed=4 * rows * width * 3, transcendentals=0
         ),
-    )(scal, base, part, coef)
+    )(base, part, weight)
+
+
+def last_rows(base, part, weight):
+    rows, width = part.shape[1:]
+    start = base.shape[1] - rows
+
+    def kernel(base, far, weight, out, have, x, w, sems):
+        here = pl.ds(start, rows)
+        copies = [
+            pltpu.make_async_copy(base.at[0, here], have, sems.at[0]),
+            pltpu.make_async_copy(far.at[0], x, sems.at[1]),
+            pltpu.make_async_copy(weight.at[here], w, sems.at[2]),
+        ]
+        for copy in copies:
+            copy.start()
+        for copy in copies:
+            copy.wait()
+        have[...] = have[...] + x[...] * (w[:, 0:1] + w[:, 1:2] * x[...])
+        back = pltpu.make_async_copy(have, out.at[0, here], sems.at[3])
+        back.start()
+        back.wait()
+
+    anywhere = pl.BlockSpec(memory_space=pl.ANY)
+    return pl.pallas_call(
+        kernel,
+        out_shape=jax.ShapeDtypeStruct(base.shape, base.dtype),
+        in_specs=[anywhere] * 3,
+        out_specs=anywhere,
+        scratch_shapes=[
+            pltpu.VMEM((rows, width), jnp.float32),
+            pltpu.VMEM((rows, width), jnp.float32),
+            pltpu.VMEM((rows, weight.shape[1]), jnp.float32),
+            pltpu.SemaphoreType.DMA((4,)),
+        ],
+        input_output_aliases={0: 0},
+        compiler_params=pltpu.CompilerParams(vmem_limit_bytes=40 << 20),
+        cost_estimate=pl.CostEstimate(
+            flops=10 * rows * width, bytes_accessed=4 * rows * width * 3, transcendentals=0
+        ),
+    )(base, part, weight)
 
 
 def local(
@@ -226,6 +265,10 @@
     gradient = (step_size * radial_diffusion[-1] * norm_factor) * binned[0]
     scal = jnp.stack([step_size, side])
     coef = jnp.stack([axial_speed, radial_diffusion, azimuth_diffusion], axis=1)
+    half = 0.5 * side * step_size
+    weight = jnp.stack(
+        [step_size + half * axial_speed, jnp.broadcast_to(0.5 * half, axial_speed.shape)], axis=1
+    )
 
     cot_far_rows, cot_near_rows, state_near_rows = lax.optimization_barrier(
         (cot_far_rows, cot_near_rows, state_near_rows)
@@ -233,8 +276,9 @@
     advanced, adjoint = local_parts(
         scal, checkpoint, state_near_rows, cotangent, cot_near_rows, cot_far_rows, wall, coef
     )
-    for low, part in zip(edges, state_far_rows):
-        advanced = add_rows(scal, advanced, part, coef, low)
+    for low, part in zip(edges, state_far_rows[:-1]):
+        advanced = add_rows(advanced, part, weight, low)
+    advanced = last_rows(advanced, state_far_rows[-1], weight)
     return (advanced, adjoint, gradient)
 
 

time: 108 us -> 108 us (level)
  waiting for transfers between devices: 59.6 us -> 58.3 us
    pallas_call x3 -> x2, Pallas kernels: 7.84 us -> 6.04 us  [add_rows(): pl.pallas_call(state_far, grid=(rows // block,), out_shape=jax.ShapeDtype...]
    pallas_call x0 -> x1, Pallas kernels: none -> 1.74 us  [last_rows(): pl.pallas_call(kernel, out_shape=jax.ShapeDtypeStruct(base.shape, base.dt...]
    ppermute x1, waiting for transfers between devices: 36.7 us -> 35.5 us  [local(): cot_far_rows = lax.ppermute(cotangent, 'ax', far)]
  transfers between devices with their start and end apart: 12 -> 12, of which waited for: 9 -> 9; matrix products, arithmetic and copies ran while one was open for 5% -> 6% of each run, Pallas kernels for 15% -> 15%
where the time goes in v1:
time: 108 us
  waiting for transfers between devices  58.3 us (54%)
  Pallas kernels  18.2 us (17%)
  starting transfers between devices  16.6 us (15%)
  local copies, waits for them, and re-layouts  7.91 us (7%)
  between operations  3.36 us (3%)
  other arithmetic  3.26 us (3%)
    ppermute x1, waiting for transfers between devices, local(): cot_far_rows = lax.ppermute(cotangent, 'ax', far)  35.5 us
    pallas_call x1, Pallas kernels, local_parts(): pl.pallas_call(local_kernel, grid=(rows // block,), out_shape=(shape, sha...  8.21 us
    ppermute x3, waiting for transfers between devices, local(): lax.ppermute(late[:, low:high], 'ax', far)  6.95 us
    ppermute x1, waiting for transfers between devices, cell_sum(): lax.ppermute(value, axis, [(i, i ^ 1) for i in turning])  6.74 us
    ppermute x2, waiting for transfers between devices, cell_sum(): value = value + lax.ppermute(value, axis, [(i, i ^ 1 << n) for i in direct])  6.62 us
    pallas_call x2, Pallas kernels, add_rows(): pl.pallas_call(state_far, grid=(rows // block,), out_shape=jax.ShapeDtype...  6.04 us
    unnamed x18, local copies, waits for them, and re-layouts  4.72 us
    ppermute x2, starting transfers between devices, cell_sum(): value = value + lax.ppermute(value, axis, [(i, i ^ 1 << n) for i in direct])  3.82 us
  transfers between devices with their start and end apart: 12, of which 9 were waited for; matrix products, arithmetic and copies ran while one was open for 6% of the time, Pallas kernels for 15%

profile of v1, /device:TPU:1, one launch (start us, length us, event | category | flops | bytes accessed | tf_op | source)
XLA Modules:
  0.0 107.6 jit_solution(12624891714597666511)
XLA Ops:
  0.6 0.0 copy-start
  0.6 2.7 %collective-permute-start = (f32[1,384,1536]{2,1,0:T(8,128)}, f32[1,384,1536]{2,1,0:T(8,128)}, u32[]{:S(2)}, u32[]{:S(2)}) collective-permute-start(f32[1,384,1536]{2,1,0:T(8,128)} %c_down.1), channel_id=1, source_target_pairs={{0,15},{1,2},{2,1},{3,4},{4,3},{5,6},{6,5},{7,8},{8,7},{9,10},{10,... | collective-permute-start | bytes 7077896 | tf_op jit(solution)/shard_map/ppermute | solution.py:245
  3.3 2.9 %collective-permute-start.1 = (f32[1,384,1536]{2,1,0:T(8,128)}, f32[1,384,1536]{2,1,0:T(8,128)}, u32[]{:S(2)}, u32[]{:S(2)}) collective-permute-start(f32[1,384,1536]{2,1,0:T(8,128)} %c_down.1), channel_id=1, source_target_pairs={{0,1},{1,0},{2,3},{3,2},{4,5},{5,4},{6,7},{7,6},{8,9},{9,8},{10,11... | collective-permute-start | bytes 7077896 | tf_op jit(solution)/shard_map/ppermute | solution.py:246
  6.2 0.0 collective-permute-start.2
  6.2 1.7 %copy-done.1 = f32[1,384,1536]{2,1,0:T(8,128)S(1)} copy-done((f32[1,384,1536]{2,1,0:T(8,128)S(1)}, f32[1,384,1536]{2,1,0:T(8,128)}, u32[]{:S(2)}) %copy-start.1) | copy-done | bytes 2359320
  7.9 0.7 copy-done.3
  8.5 0.7 copy-done.4
  9.2 2.2 %shard_map.112 = (f32[1,1536]{1,0:T(1,128)S(1)}, f32[1,256]{1,0:T(1,128)S(1)}) custom-call(s32[1,1536]{1,0:T(1,128)S(1)} %copy-done.3, f32[1,256]{1,0:T(1,128)S(1)} %bitcast.8, f32[1,384,1536]{2,1,0:T(8,128)S(1)} %copy-done.1), custom_call_target="tpu_custom_call" | custom-call | tf_op jit(solution)/shard_map/pallas_call | solution.py:72
  11.4 0.5 collective-permute-start.3
  12.0 1.8 %collective-permute-done.3 = f32[1,256]{1,0:T(1,128)S(1)} collective-permute-done((f32[1,256]{1,0:T(1,128)S(1)}, f32[1,256]{1,0:T(1,128)S(1)}, u32[]{:S(2)}, u32[]{:S(2)}) %collective-permute-start.3) | collective-permute-done | bytes 1056 | tf_op jit(solution)/shard_map/ppermute | solution.py:40
  13.7 1.9 %collective-permute-start.4 = (f32[1,256]{1,0:T(1,128)S(1)}, f32[1,256]{1,0:T(1,128)S(1)}, u32[]{:S(2)}, u32[]{:S(2)}) collective-permute-start(f32[1,256]{1,0:T(1,128)S(1)} %add.29), channel_id=1, source_target_pairs={{1,5},{2,6},{5,1},{6,2},{9,13},{10,14},{13,9},{14,10},{17,21},{18,... | collective-permute-start | bytes 3080 | tf_op jit(solution)/shard_map/ppermute | solution.py:42
  15.6 2.9 %collective-permute-done.4 = f32[1,256]{1,0:T(1,128)S(1)} collective-permute-done((f32[1,256]{1,0:T(1,128)S(1)}, f32[1,256]{1,0:T(1,128)S(1)}, u32[]{:S(2)}, u32[]{:S(2)}) %collective-permute-start.4) | collective-permute-done | bytes 1056 | tf_op jit(solution)/shard_map/ppermute | solution.py:42
  18.5 1.9 %collective-permute-start.5 = (f32[1,256]{1,0:T(1,128)S(1)}, f32[1,256]{1,0:T(1,128)S(1)}, u32[]{:S(2)}, u32[]{:S(2)}) collective-permute-start(f32[1,256]{1,0:T(1,128)S(1)} %add.30), channel_id=1, source_target_pairs={{1,9},{2,10},{5,13},{6,14},{9,1},{10,2},{13,5},{14,6},{17,25},{18,... | collective-permute-start | bytes 3080 | tf_op jit(solution)/shard_map/ppermute | solution.py:42
  20.4 3.8 %collective-permute-done.5 = f32[1,256]{1,0:T(1,128)S(1)} collective-permute-done((f32[1,256]{1,0:T(1,128)S(1)}, f32[1,256]{1,0:T(1,128)S(1)}, u32[]{:S(2)}, u32[]{:S(2)}) %collective-permute-start.5) | collective-permute-done | bytes 1056 | tf_op jit(solution)/shard_map/ppermute | solution.py:42
  24.2 1.3 %collective-permute-start.6 = (f32[1,256]{1,0:T(1,128)S(1)}, f32[1,256]{1,0:T(1,128)S(1)}, u32[]{:S(2)}, u32[]{:S(2)}) collective-permute-start(f32[1,256]{1,0:T(1,128)S(1)} %add.31), channel_id=1, source_target_pairs={{1,0},{2,3},{5,4},{6,7},{9,8},{10,11},{13,12},{14,15},{17,16},{18,... | collective-permute-start | bytes 3080 | tf_op jit(solution)/shard_map/ppermute | solution.py:43
  25.5 0.8 collective-permute-done.6
  26.3 0.6 collective-permute-start.7
  26.9 0.0 collective-permute-done.7
  27.0 1.3 %collective-permute-start.8 = (f32[1,256]{1,0:T(1,128)S(1)}, f32[1,256]{1,0:T(1,128)S(1)}, u32[]{:S(2)}, u32[]{:S(2)}) collective-permute-start(f32[1,256]{1,0:T(1,128)S(1)} %add.32), channel_id=1, source_target_pairs={{0,1},{3,2},{4,5},{7,6},{8,9},{11,10},{12,13},{15,14},{16,17},{19,... | collective-permute-start | bytes 3080 | tf_op jit(solution)/shard_map/ppermute | solution.py:45
  28.3 6.7 %collective-permute-done.8 = f32[1,256]{1,0:T(1,128)S(1)} collective-permute-done((f32[1,256]{1,0:T(1,128)S(1)}, f32[1,256]{1,0:T(1,128)S(1)}, u32[]{:S(2)}, u32[]{:S(2)}) %collective-permute-start.8) | collective-permute-done | bytes 1056 | tf_op jit(solution)/shard_map/ppermute | solution.py:45
  35.0 0.0 copy-done
  35.0 1.4 %slice.30 = f32[1,264,1536]{2,1,0:T(8,128)} slice(f32[1,384,1536]{2,1,0:T(8,128)S(1)} %copy-done), slice={[0:1], [0:264], [0:1536]} | slice | bytes 3244032 | tf_op jit(solution)/shard_map/slice | solution.py:258
  36.4 0.0 collective-permute-start.9
  36.4 0.6 slice.26
  37.0 0.1 slice.28
  37.7 0.0 copy-done.7
  37.8 0.6 pad_maximum_fusion
  38.4 0.1 pad_maximum_fusion.1
  38.5 0.1 copy.21.coef
  38.7 0.6 fusion
  39.9 0.9 slice.31
  40.8 1.7 %collective-permute-start.10 = (f32[1,88,1536]{2,1,0:T(8,128)}, f32[1,88,1536]{2,1,0:T(8,128)S(1)}, u32[]{:S(2)}, u32[]{:S(2)}) collective-permute-start(f32[1,88,1536]{2,1,0:T(8,128)} %slice.31), channel_id=1, source_target_pairs={{0,15},{1,2},{2,1},{3,4},{4,3},{5,6},{6,5},{7,8},{8,7},{9,10},{10,... | collective-permute-start | bytes 1622024 | tf_op jit(solution)/shard_map/ppermute | solution.py:258
  42.5 0.6 multiply_add_fusion
  43.2 0.1 stack.32
  44.5 0.7 pad_maximum_fusion.2.scal
  45.3 35.5 %collective-permute-done.c_far = f32[1,384,1536]{2,1,0:T(8,128)} collective-permute-done((f32[1,384,1536]{2,1,0:T(8,128)}, f32[1,384,1536]{2,1,0:T(8,128)}, u32[]{:S(2)}, u32[]{:S(2)}) %collective-permute-start) | collective-permute-done | bytes 2359328 | tf_op jit(solution)/shard_map/ppermute | solution.py:245
  80.7 1.7 %collective-permute-start.11 = (f32[1,32,1536]{2,1,0:T(8,128)S(1)}, f32[1,32,1536]{2,1,0:T(8,128)S(1)}, u32[]{:S(2)}, u32[]{:S(2)}) collective-permute-start(f32[1,32,1536]{2,1,0:T(8,128)S(1)} %slice.32), channel_id=1, source_target_pairs={{0,15},{1,2},{2,1},{3,4},{4,3},{5,6},{6,5},{7,8},{8,7},{9,10},{10,... | collective-permute-start | bytes 589832 | tf_op jit(solution)/shard_map/ppermute | solution.py:258
  82.5 0.6 broadcast_multiply_fusion
  83.0 0.0 collective-permute-done.1.c_near
  83.0 0.0 collective-permute-done.2.q_near
  83.0 1.7 %copy-done.2 = f32[1,384,1536]{2,1,0:T(8,128)S(1)} copy-done((f32[1,384,1536]{2,1,0:T(8,128)S(1)}, f32[1,384,1536]{2,1,0:T(8,128)}, u32[]{:S(2)}) %copy-start.2) | copy-done | bytes 2359320
  84.7 8.2 %shard_map.113 = (f32[1,384,1536]{2,1,0:T(8,128)}, f32[1,384,1536]{2,1,0:T(8,128)}) custom-call(f32[2]{0:T(128)S(1)} %pad_maximum_fusion.2.scal, f32[1,384,1536]{2,1,0:T(8,128)S(1)} %copy-done, f32[1,384,1536]{2,1,0:T(8,128)S(1)} %copy-done, f32[1,384,1536]{2,1,0:T(8,128)S(1)} %copy-done, f32[1,384,1536]{2,1,0:T(8,128)} %collective-permute-done.2.q_near, ...), custom_call_target="tpu_custom_call" | custom-call | flops 29491200 | bytes 16515072 | tf_op jit(solution)/shard_map/pallas_call | solution.py:147
  92.9 5.2 %collective-permute-done.9.far = f32[1,264,1536]{2,1,0:T(8,128)} collective-permute-done((f32[1,264,1536]{2,1,0:T(8,128)}, f32[1,264,1536]{2,1,0:T(8,128)}, u32[]{:S(2)}, u32[]{:S(2)}) %collective-permute-start.9) | collective-permute-done | bytes 1622048 | tf_op jit(solution)/shard_map/ppermute | solution.py:258
  98.1 4.0 %shard_map.114.base = f32[1,384,1536]{2,1,0:T(8,128)} custom-call(f32[1,384,1536]{2,1,0:T(8,128)} %get-tuple-element.16.base, f32[1,264,1536]{2,1,0:T(8,128)} %collective-permute-done.9.far, f32[384,2]{1,0:T(8,128)S(1)} %stack.31.weight), custom_call_target="tpu_custom_call", output_to_operand_aliasing={{}: (0, {})} | custom-call | flops 4055040 | bytes 4866048 | tf_op jit(solution)/shard_map/pallas_call | solution.py:177
  102.1 1.7 %collective-permute-done.10.far = f32[1,88,1536]{2,1,0:T(8,128)S(1)} collective-permute-done((f32[1,88,1536]{2,1,0:T(8,128)}, f32[1,88,1536]{2,1,0:T(8,128)S(1)}, u32[]{:S(2)}, u32[]{:S(2)}) %collective-permute-start.10) | collective-permute-done | bytes 540704 | tf_op jit(solution)/shard_map/ppermute | solution.py:258
  103.8 2.0 %shard_map.115.base = f32[1,384,1536]{2,1,0:T(8,128)} custom-call(f32[1,384,1536]{2,1,0:T(8,128)} %shard_map.114.base, f32[1,88,1536]{2,1,0:T(8,128)S(1)} %collective-permute-done.10.far, f32[384,2]{1,0:T(8,128)S(1)} %stack.31.weight), custom_call_target="tpu_custom_call", output_to_operand_aliasing={{}: (0, {})} | custom-call | flops 1351680 | bytes 1622016 | tf_op jit(solution)/shard_map/pallas_call | solution.py:177
  105.8 0.1 collective-permute-done.11.far
  105.9 1.7 %shard_map.116 = f32[1,384,1536]{2,1,0:T(8,128)} custom-call(f32[1,384,1536]{2,1,0:T(8,128)} %shard_map.115.base, f32[1,32,1536]{2,1,0:T(8,128)S(1)} %collective-permute-done.11.far, f32[384,2]{1,0:T(8,128)S(1)} %stack.31.weight), custom_call_target="tpu_custom_call", output_to_operand_aliasing={{}: (0, {})} | custom-call | flops 491520 | bytes 589824 | tf_op jit(solution)/shard_map/pallas_call | solution.py:212
  (25 shorter events, 0.1 us)
Async XLA Ops:
  0.6 34.4 %copy-start = (f32[1,384,1536]{2,1,0:T(8,128)S(1)}, f32[1,384,1536]{2,1,0:T(8,128)}, u32[]{:S(2)}) copy-start(f32[1,384,1536]{2,1,0:T(8,128)} %q_down.1) | copy-start | bytes 7077892
  0.6 80.1 %collective-permute-start = (f32[1,384,1536]{2,1,0:T(8,128)}, f32[1,384,1536]{2,1,0:T(8,128)}, u32[]{:S(2)}, u32[]{:S(2)}) collective-permute-start(f32[1,384,1536]{2,1,0:T(8,128)} %c_down.1), channel_id=1, source_target_pairs={{0,15},{1,2},{2,1},{3,4},{4,3},{5,6},{6,5},{7,8},{8,7},{9,10},{10,... | collective-permute-start | bytes 7077896 | tf_op jit(solution)/shard_map/ppermute | solution.py:245
  3.3 79.7 %collective-permute-start.1 = (f32[1,384,1536]{2,1,0:T(8,128)}, f32[1,384,1536]{2,1,0:T(8,128)}, u32[]{:S(2)}, u32[]{:S(2)}) collective-permute-start(f32[1,384,1536]{2,1,0:T(8,128)} %c_down.1), channel_id=1, source_target_pairs={{0,1},{1,0},{2,3},{3,2},{4,5},{5,4},{6,7},{7,6},{8,9},{9,8},{10,11... | collective-permute-start | bytes 7077896 | tf_op jit(solution)/shard_map/ppermute | solution.py:246
  6.2 76.9 %collective-permute-start.2 = (f32[1,384,1536]{2,1,0:T(8,128)}, f32[1,384,1536]{2,1,0:T(8,128)}, u32[]{:S(2)}, u32[]{:S(2)}) collective-permute-start(f32[1,384,1536]{2,1,0:T(8,128)} %q_down.1), channel_id=1, source_target_pairs={{0,1},{1,0},{2,3},{3,2},{4,5},{5,4},{6,7},{7,6},{8,9},{9,8},{10,11... | collective-permute-start | bytes 7077896 | tf_op jit(solution)/shard_map/ppermute | solution.py:247
  6.2 1.7 %copy-start.1 = (f32[1,384,1536]{2,1,0:T(8,128)S(1)}, f32[1,384,1536]{2,1,0:T(8,128)}, u32[]{:S(2)}) copy-start(f32[1,384,1536]{2,1,0:T(8,128)} %c_down.1) | copy-start | bytes 7077892
  7.9 0.7 copy-start.3
  8.5 0.7 copy-start.4
  9.2 27.2 %copy-start.5 = (f32[384]{0:T(512)S(1)}, f32[384]{0:T(512)}, u32[]{:S(2)}) copy-start(f32[384]{0:T(512)} %param.15) | copy-start | bytes 4612
  9.2 28.5 %copy-start.6 = (f32[384]{0:T(512)S(1)}, f32[384]{0:T(512)}, u32[]{:S(2)}) copy-start(f32[384]{0:T(512)} %param.14) | copy-start | bytes 4612
  9.2 28.5 %copy-start.7 = (f32[384]{0:T(512)S(1)}, f32[384]{0:T(512)}, u32[]{:S(2)}) copy-start(f32[384]{0:T(512)} %param.16) | copy-start | bytes 4612
  11.4 27.2 %copy-start.8 = (f32[3]{0:T(128)S(1)}, f32[3]{0:T(128)}, u32[]{:S(2)}) copy-start(f32[3]{0:T(128)} %constant.51) | copy-start | bytes 40
  11.4 2.3 %collective-permute-start.3 = (f32[1,256]{1,0:T(1,128)S(1)}, f32[1,256]{1,0:T(1,128)S(1)}, u32[]{:S(2)}, u32[]{:S(2)}) collective-permute-start(f32[1,256]{1,0:T(1,128)S(1)} %get-tuple-element.17), channel_id=1, source_target_pairs={{0,1},{1,0},{2,3},{3,2},{4,5},{5,4},{6,7},{7,6},{8,9},{9,8},{10,11... | collective-permute-start | bytes 3080 | tf_op jit(solution)/shard_map/ppermute | solution.py:40
  13.7 4.8 %collective-permute-start.4 = (f32[1,256]{1,0:T(1,128)S(1)}, f32[1,256]{1,0:T(1,128)S(1)}, u32[]{:S(2)}, u32[]{:S(2)}) collective-permute-start(f32[1,256]{1,0:T(1,128)S(1)} %add.29), channel_id=1, source_target_pairs={{1,5},{2,6},{5,1},{6,2},{9,13},{10,14},{13,9},{14,10},{17,21},{18,... | collective-permute-start | bytes 3080 | tf_op jit(solution)/shard_map/ppermute | solution.py:42
  18.5 5.7 %collective-permute-start.5 = (f32[1,256]{1,0:T(1,128)S(1)}, f32[1,256]{1,0:T(1,128)S(1)}, u32[]{:S(2)}, u32[]{:S(2)}) collective-permute-start(f32[1,256]{1,0:T(1,128)S(1)} %add.30), channel_id=1, source_target_pairs={{1,9},{2,10},{5,13},{6,14},{9,1},{10,2},{13,5},{14,6},{17,25},{18,... | collective-permute-start | bytes 3080 | tf_op jit(solution)/shard_map/ppermute | solution.py:42
  24.2 2.1 %collective-permute-start.6 = (f32[1,256]{1,0:T(1,128)S(1)}, f32[1,256]{1,0:T(1,128)S(1)}, u32[]{:S(2)}, u32[]{:S(2)}) collective-permute-start(f32[1,256]{1,0:T(1,128)S(1)} %add.31), channel_id=1, source_target_pairs={{1,0},{2,3},{5,4},{6,7},{9,8},{10,11},{13,12},{14,15},{17,16},{18,... | collective-permute-start | bytes 3080 | tf_op jit(solution)/shard_map/ppermute | solution.py:43
  26.3 0.7 collective-permute-start.7
  27.0 8.1 %collective-permute-start.8 = (f32[1,256]{1,0:T(1,128)S(1)}, f32[1,256]{1,0:T(1,128)S(1)}, u32[]{:S(2)}, u32[]{:S(2)}) collective-permute-start(f32[1,256]{1,0:T(1,128)S(1)} %add.32), channel_id=1, source_target_pairs={{0,1},{3,2},{4,5},{7,6},{8,9},{11,10},{12,13},{15,14},{16,17},{19,... | collective-permute-start | bytes 3080 | tf_op jit(solution)/shard_map/ppermute | solution.py:45
  36.4 61.7 %collective-permute-start.9 = (f32[1,264,1536]{2,1,0:T(8,128)}, f32[1,264,1536]{2,1,0:T(8,128)}, u32[]{:S(2)}, u32[]{:S(2)}) collective-permute-start(f32[1,264,1536]{2,1,0:T(8,128)} %slice.30), channel_id=1, source_target_pairs={{0,15},{1,2},{2,1},{3,4},{4,3},{5,6},{6,5},{7,8},{8,7},{9,10},{10,... | collective-permute-start | bytes 4866056 | tf_op jit(solution)/shard_map/ppermute | solution.py:258
  40.8 63.0 %collective-permute-start.10 = (f32[1,88,1536]{2,1,0:T(8,128)}, f32[1,88,1536]{2,1,0:T(8,128)S(1)}, u32[]{:S(2)}, u32[]{:S(2)}) collective-permute-start(f32[1,88,1536]{2,1,0:T(8,128)} %slice.31), channel_id=1, source_target_pairs={{0,15},{1,2},{2,1},{3,4},{4,3},{5,6},{6,5},{7,8},{8,7},{9,10},{10,... | collective-permute-start | bytes 1622024 | tf_op jit(solution)/shard_map/ppermute | solution.py:258
  80.7 25.2 %collective-permute-start.11 = (f32[1,32,1536]{2,1,0:T(8,128)S(1)}, f32[1,32,1536]{2,1,0:T(8,128)S(1)}, u32[]{:S(2)}, u32[]{:S(2)}) collective-permute-start(f32[1,32,1536]{2,1,0:T(8,128)S(1)} %slice.32), channel_id=1, source_target_pairs={{0,15},{1,2},{2,1},{3,4},{4,3},{5,6},{6,5},{7,8},{8,7},{9,10},{10,... | collective-permute-start | bytes 589832 | tf_op jit(solution)/shard_map/ppermute | solution.py:258
  83.0 1.7 %copy-start.2 = (f32[1,384,1536]{2,1,0:T(8,128)S(1)}, f32[1,384,1536]{2,1,0:T(8,128)}, u32[]{:S(2)}) copy-start(f32[1,384,1536]{2,1,0:T(8,128)} %c_down.1) | copy-start | bytes 7077892

commit v2 on v1

--- a/solution.py
+++ b/solution.py
@@ -188,44 +188,30 @@
     )(base, part, weight)
 
 
-def last_rows(base, part, weight):
+def put_rows(out, base, part, weight, start):
     rows, width = part.shape[1:]
-    start = base.shape[1] - rows
-
-    def kernel(base, far, weight, out, have, x, w, sems):
-        here = pl.ds(start, rows)
-        copies = [
-            pltpu.make_async_copy(base.at[0, here], have, sems.at[0]),
-            pltpu.make_async_copy(far.at[0], x, sems.at[1]),
-            pltpu.make_async_copy(weight.at[here], w, sems.at[2]),
-        ]
-        for copy in copies:
-            copy.start()
-        for copy in copies:
-            copy.wait()
-        have[...] = have[...] + x[...] * (w[:, 0:1] + w[:, 1:2] * x[...])
-        back = pltpu.make_async_copy(have, out.at[0, here], sems.at[3])
-        back.start()
-        back.wait()
+
+    def kernel(base, far, weight, before, out, fresh, sem):
+        x = far[0]
+        of_row = weight[pl.ds(start, rows), :]
+        fresh[...] = base[0] + x * (of_row[:, 0:1] + of_row[:, 1:2] * x)
+        store = pltpu.make_async_copy(fresh, out.at[0, pl.ds(start, rows)], sem)
+        store.start()
+        store.wait()
 
     anywhere = pl.BlockSpec(memory_space=pl.ANY)
     return pl.pallas_call(
         kernel,
-        out_shape=jax.ShapeDtypeStruct(base.shape, base.dtype),
-        in_specs=[anywhere] * 3,
+        out_shape=jax.ShapeDtypeStruct(out.shape, out.dtype),
+        in_specs=[pl.BlockSpec(memory_space=pltpu.VMEM)] * 3 + [anywhere],
         out_specs=anywhere,
-        scratch_shapes=[
-            pltpu.VMEM((rows, width), jnp.float32),
-            pltpu.VMEM((rows, width), jnp.float32),
-            pltpu.VMEM((rows, weight.shape[1]), jnp.float32),
-            pltpu.SemaphoreType.DMA((4,)),
-        ],
-        input_output_aliases={0: 0},
+        scratch_shapes=[pltpu.VMEM((rows, width), jnp.float32), pltpu.SemaphoreType.DMA],
+        input_output_aliases={3: 0},
         compiler_params=pltpu.CompilerParams(vmem_limit_bytes=40 << 20),
         cost_estimate=pl.CostEstimate(
             flops=10 * rows * width, bytes_accessed=4 * rows * width * 3, transcendentals=0
         ),
-    )(base, part, weight)
+    )(base, part, weight, out)
 
 
 def local(
@@ -276,9 +262,11 @@
     advanced, adjoint = local_parts(
         scal, checkpoint, state_near_rows, cotangent, cot_near_rows, cot_far_rows, wall, coef
     )
-    for low, part in zip(edges, state_far_rows[:-1]):
-        advanced = add_rows(advanced, part, weight, low)
-    advanced = last_rows(advanced, state_far_rows[-1], weight)
+    bases = [advanced[:, low:high] for low, high in zip(edges[1:], edges[2:])]
+    advanced, *bases = lax.optimization_barrier((advanced, *bases))
+    advanced = add_rows(advanced, state_far_rows[0], weight, 0)
+    for low, base, part in zip(edges[1:], bases, state_far_rows[1:]):
+        advanced = put_rows(advanced, base, part, weight, low)
     return (advanced, adjoint, gradient)
 
 

time: 108 us -> 107 us (level)
  local copies, waits for them, and re-layouts: 7.91 us -> 9.94 us
  Pallas kernels: 18.2 us -> 16.2 us
    slice x0 -> x2, local copies, waits for them, and re-layouts: none -> 2.03 us  [local(): bases = [advanced[:, low:high] for low, high in zip(edges[1:], edges[2:])]]
    pallas_call x2 -> x1, Pallas kernels: 6.04 us -> 4.02 us  [add_rows(): pl.pallas_call(state_far, grid=(rows // block,), out_shape=jax.ShapeDtype...]
  transfers between devices with their start and end apart: 12 -> 12, of which waited for: 9 -> 9; matrix products, arithmetic and copies ran while one was open for 6% -> 8% of each run, Pallas kernels for 15% -> 14%
where the time goes in v2:
time: 107 us
  waiting for transfers between devices  57.3 us (54%)
  starting transfers between devices  16.6 us (16%)
  Pallas kernels  16.2 us (15%)
  local copies, waits for them, and re-layouts  9.94 us (9%)
  between operations  3.35 us (3%)
  other arithmetic  3.26 us (3%)
    ppermute x1, waiting for transfers between devices, local(): cot_far_rows = lax.ppermute(cotangent, 'ax', far)  35.5 us
    pallas_call x1, Pallas kernels, local_parts(): pl.pallas_call(local_kernel, grid=(rows // block,), out_shape=(shape, sha...  8.21 us
    ppermute x1, waiting for transfers between devices, cell_sum(): lax.ppermute(value, axis, [(i, i ^ 1) for i in turning])  6.74 us
    ppermute x2, waiting for transfers between devices, cell_sum(): value = value + lax.ppermute(value, axis, [(i, i ^ 1 << n) for i in direct])  6.62 us
    ppermute x3, waiting for transfers between devices, local(): lax.ppermute(late[:, low:high], 'ax', far)  5.94 us
    unnamed x18, local copies, waits for them, and re-layouts  4.72 us
    pallas_call x1, Pallas kernels, add_rows(): pl.pallas_call(state_far, grid=(rows // block,), out_shape=jax.ShapeDtype...  4.02 us
    ppermute x2, starting transfers between devices, cell_sum(): value = value + lax.ppermute(value, axis, [(i, i ^ 1 << n) for i in direct])  3.82 us
  transfers between devices with their start and end apart: 12, of which 9 were waited for; matrix products, arithmetic and copies ran while one was open for 8% of the time, Pallas kernels for 14%

profile of v2, /device:TPU:1, one launch (start us, length us, event | category | flops | bytes accessed | tf_op | source)
XLA Modules:
  0.0 106.7 jit_solution(2248545796980458004)
XLA Ops:
  0.6 0.0 copy-start
  0.6 2.7 %collective-permute-start = (f32[1,384,1536]{2,1,0:T(8,128)}, f32[1,384,1536]{2,1,0:T(8,128)}, u32[]{:S(2)}, u32[]{:S(2)}) collective-permute-start(f32[1,384,1536]{2,1,0:T(8,128)} %c_down.1), channel_id=1, source_target_pairs={{0,15},{1,2},{2,1},{3,4},{4,3},{5,6},{6,5},{7,8},{8,7},{9,10},{10,... | collective-permute-start | bytes 7077896 | tf_op jit(solution)/shard_map/ppermute | solution.py:231
  3.3 2.9 %collective-permute-start.1 = (f32[1,384,1536]{2,1,0:T(8,128)}, f32[1,384,1536]{2,1,0:T(8,128)}, u32[]{:S(2)}, u32[]{:S(2)}) collective-permute-start(f32[1,384,1536]{2,1,0:T(8,128)} %c_down.1), channel_id=1, source_target_pairs={{0,1},{1,0},{2,3},{3,2},{4,5},{5,4},{6,7},{7,6},{8,9},{9,8},{10,11... | collective-permute-start | bytes 7077896 | tf_op jit(solution)/shard_map/ppermute | solution.py:232
  6.2 0.0 collective-permute-start.2
  6.2 1.7 %copy-done.1 = f32[1,384,1536]{2,1,0:T(8,128)S(1)} copy-done((f32[1,384,1536]{2,1,0:T(8,128)S(1)}, f32[1,384,1536]{2,1,0:T(8,128)}, u32[]{:S(2)}) %copy-start.1) | copy-done | bytes 2359320
  7.9 0.7 copy-done.3
  8.5 0.7 copy-done.4
  9.2 2.2 %shard_map.112 = (f32[1,1536]{1,0:T(1,128)S(1)}, f32[1,256]{1,0:T(1,128)S(1)}) custom-call(s32[1,1536]{1,0:T(1,128)S(1)} %copy-done.3, f32[1,256]{1,0:T(1,128)S(1)} %bitcast.8, f32[1,384,1536]{2,1,0:T(8,128)S(1)} %copy-done.1), custom_call_target="tpu_custom_call" | custom-call | tf_op jit(solution)/shard_map/pallas_call | solution.py:72
  11.4 0.5 collective-permute-start.3
  12.0 1.8 %collective-permute-done.3 = f32[1,256]{1,0:T(1,128)S(1)} collective-permute-done((f32[1,256]{1,0:T(1,128)S(1)}, f32[1,256]{1,0:T(1,128)S(1)}, u32[]{:S(2)}, u32[]{:S(2)}) %collective-permute-start.3) | collective-permute-done | bytes 1056 | tf_op jit(solution)/shard_map/ppermute | solution.py:40
  13.7 1.9 %collective-permute-start.4 = (f32[1,256]{1,0:T(1,128)S(1)}, f32[1,256]{1,0:T(1,128)S(1)}, u32[]{:S(2)}, u32[]{:S(2)}) collective-permute-start(f32[1,256]{1,0:T(1,128)S(1)} %add.29), channel_id=1, source_target_pairs={{1,5},{2,6},{5,1},{6,2},{9,13},{10,14},{13,9},{14,10},{17,21},{18,... | collective-permute-start | bytes 3080 | tf_op jit(solution)/shard_map/ppermute | solution.py:42
  15.6 2.9 %collective-permute-done.4 = f32[1,256]{1,0:T(1,128)S(1)} collective-permute-done((f32[1,256]{1,0:T(1,128)S(1)}, f32[1,256]{1,0:T(1,128)S(1)}, u32[]{:S(2)}, u32[]{:S(2)}) %collective-permute-start.4) | collective-permute-done | bytes 1056 | tf_op jit(solution)/shard_map/ppermute | solution.py:42
  18.5 1.9 %collective-permute-start.5 = (f32[1,256]{1,0:T(1,128)S(1)}, f32[1,256]{1,0:T(1,128)S(1)}, u32[]{:S(2)}, u32[]{:S(2)}) collective-permute-start(f32[1,256]{1,0:T(1,128)S(1)} %add.30), channel_id=1, source_target_pairs={{1,9},{2,10},{5,13},{6,14},{9,1},{10,2},{13,5},{14,6},{17,25},{18,... | collective-permute-start | bytes 3080 | tf_op jit(solution)/shard_map/ppermute | solution.py:42
  20.4 3.8 %collective-permute-done.5 = f32[1,256]{1,0:T(1,128)S(1)} collective-permute-done((f32[1,256]{1,0:T(1,128)S(1)}, f32[1,256]{1,0:T(1,128)S(1)}, u32[]{:S(2)}, u32[]{:S(2)}) %collective-permute-start.5) | collective-permute-done | bytes 1056 | tf_op jit(solution)/shard_map/ppermute | solution.py:42
  24.2 1.3 %collective-permute-start.6 = (f32[1,256]{1,0:T(1,128)S(1)}, f32[1,256]{1,0:T(1,128)S(1)}, u32[]{:S(2)}, u32[]{:S(2)}) collective-permute-start(f32[1,256]{1,0:T(1,128)S(1)} %add.31), channel_id=1, source_target_pairs={{1,0},{2,3},{5,4},{6,7},{9,8},{10,11},{13,12},{14,15},{17,16},{18,... | collective-permute-start | bytes 3080 | tf_op jit(solution)/shard_map/ppermute | solution.py:43
  25.5 0.8 collective-permute-done.6
  26.3 0.6 collective-permute-start.7
  26.9 0.0 collective-permute-done.7
  27.0 1.3 %collective-permute-start.8 = (f32[1,256]{1,0:T(1,128)S(1)}, f32[1,256]{1,0:T(1,128)S(1)}, u32[]{:S(2)}, u32[]{:S(2)}) collective-permute-start(f32[1,256]{1,0:T(1,128)S(1)} %add.32), channel_id=1, source_target_pairs={{0,1},{3,2},{4,5},{7,6},{8,9},{11,10},{12,13},{15,14},{16,17},{19,... | collective-permute-start | bytes 3080 | tf_op jit(solution)/shard_map/ppermute | solution.py:45
  28.3 6.7 %collective-permute-done.8 = f32[1,256]{1,0:T(1,128)S(1)} collective-permute-done((f32[1,256]{1,0:T(1,128)S(1)}, f32[1,256]{1,0:T(1,128)S(1)}, u32[]{:S(2)}, u32[]{:S(2)}) %collective-permute-start.8) | collective-permute-done | bytes 1056 | tf_op jit(solution)/shard_map/ppermute | solution.py:45
  35.0 1.4 %slice.40 = f32[1,264,1536]{2,1,0:T(8,128)} slice(f32[1,384,1536]{2,1,0:T(8,128)S(1)} %copy-done), slice={[0:1], [0:264], [0:1536]} | slice | bytes 3244032 | tf_op jit(solution)/shard_map/slice | solution.py:244
  36.4 0.0 collective-permute-start.11
  36.4 0.6 slice.32
  37.0 0.1 slice.34
  37.7 0.6 pad_maximum_fusion
  38.3 0.1 pad_maximum_fusion.1
  38.5 0.1 copy.21.coef
  38.6 0.6 fusion
  39.9 0.9 slice.39
  40.8 1.7 %collective-permute-start.10 = (f32[1,88,1536]{2,1,0:T(8,128)}, f32[1,88,1536]{2,1,0:T(8,128)S(1)}, u32[]{:S(2)}, u32[]{:S(2)}) collective-permute-start(f32[1,88,1536]{2,1,0:T(8,128)} %slice.39), channel_id=1, source_target_pairs={{0,15},{1,2},{2,1},{3,4},{4,3},{5,6},{6,5},{7,8},{8,7},{9,10},{10,... | collective-permute-start | bytes 1622024 | tf_op jit(solution)/shard_map/ppermute | solution.py:244
  42.5 0.6 multiply_add_fusion
  43.2 0.1 stack.32
  44.5 0.7 pad_maximum_fusion.2.scal
  45.3 35.5 %collective-permute-done.c_far = f32[1,384,1536]{2,1,0:T(8,128)} collective-permute-done((f32[1,384,1536]{2,1,0:T(8,128)}, f32[1,384,1536]{2,1,0:T(8,128)}, u32[]{:S(2)}, u32[]{:S(2)}) %collective-permute-start) | collective-permute-done | bytes 2359328 | tf_op jit(solution)/shard_map/ppermute | solution.py:231
  80.7 1.7 %collective-permute-start.9 = (f32[1,32,1536]{2,1,0:T(8,128)S(1)}, f32[1,32,1536]{2,1,0:T(8,128)S(1)}, u32[]{:S(2)}, u32[]{:S(2)}) collective-permute-start(f32[1,32,1536]{2,1,0:T(8,128)S(1)} %slice.38), channel_id=1, source_target_pairs={{0,15},{1,2},{2,1},{3,4},{4,3},{5,6},{6,5},{7,8},{8,7},{9,10},{10,... | collective-permute-start | bytes 589832 | tf_op jit(solution)/shard_map/ppermute | solution.py:244
  82.5 0.6 broadcast_multiply_fusion
  83.0 0.0 collective-permute-done.1.c_near
  83.0 0.0 collective-permute-done.2.q_near
  83.0 1.7 %copy-done.2 = f32[1,384,1536]{2,1,0:T(8,128)S(1)} copy-done((f32[1,384,1536]{2,1,0:T(8,128)S(1)}, f32[1,384,1536]{2,1,0:T(8,128)}, u32[]{:S(2)}) %copy-start.2) | copy-done | bytes 2359320
  84.7 8.2 %shard_map.113 = (f32[1,384,1536]{2,1,0:T(8,128)}, f32[1,384,1536]{2,1,0:T(8,128)}) custom-call(f32[2]{0:T(128)S(1)} %pad_maximum_fusion.2.scal, f32[1,384,1536]{2,1,0:T(8,128)S(1)} %copy-done, f32[1,384,1536]{2,1,0:T(8,128)S(1)} %copy-done, f32[1,384,1536]{2,1,0:T(8,128)S(1)} %copy-done, f32[1,384,1536]{2,1,0:T(8,128)} %collective-permute-done.2.q_near, ...), custom_call_target="tpu_custom_call" | custom-call | flops 29491200 | bytes 16515072 | tf_op jit(solution)/shard_map/pallas_call | solution.py:147
  92.9 1.1 %slice.36.base = f32[1,88,1536]{2,1,0:T(8,128)S(1)} slice(f32[1,384,1536]{2,1,0:T(8,128)} %get-tuple-element.24.base), slice={[0:1], [264:352], [0:1536]} | slice | bytes 1081344 | tf_op jit(solution)/shard_map/slice | solution.py:265
  94.0 0.9 slice.37.base
  94.9 3.2 %collective-permute-done.11.far = f32[1,264,1536]{2,1,0:T(8,128)} collective-permute-done((f32[1,264,1536]{2,1,0:T(8,128)}, f32[1,264,1536]{2,1,0:T(8,128)}, u32[]{:S(2)}, u32[]{:S(2)}) %collective-permute-start.11) | collective-permute-done | bytes 1622048 | tf_op jit(solution)/shard_map/ppermute | solution.py:244
  98.1 4.0 %shard_map.114.before = f32[1,384,1536]{2,1,0:T(8,128)} custom-call(f32[1,384,1536]{2,1,0:T(8,128)} %get-tuple-element.24.base, f32[1,264,1536]{2,1,0:T(8,128)} %collective-permute-done.11.far, f32[384,2]{1,0:T(8,128)S(1)} %stack.31.weight), custom_call_target="tpu_custom_call", output_to_operand_aliasing={{}: (0, {})} | custom-call | flops 4055040 | bytes 4866048 | tf_op jit(solution)/shard_map/pallas_call | solution.py:177
  102.1 1.7 %collective-permute-done.10.far = f32[1,88,1536]{2,1,0:T(8,128)S(1)} collective-permute-done((f32[1,88,1536]{2,1,0:T(8,128)}, f32[1,88,1536]{2,1,0:T(8,128)S(1)}, u32[]{:S(2)}, u32[]{:S(2)}) %collective-permute-start.10) | collective-permute-done | bytes 540704 | tf_op jit(solution)/shard_map/ppermute | solution.py:244
  103.8 1.0 shard_map.115.before
  104.8 1.1 %collective-permute-done.9.far = f32[1,32,1536]{2,1,0:T(8,128)S(1)} collective-permute-done((f32[1,32,1536]{2,1,0:T(8,128)S(1)}, f32[1,32,1536]{2,1,0:T(8,128)S(1)}, u32[]{:S(2)}, u32[]{:S(2)}) %collective-permute-start.9) | collective-permute-done | bytes 196640 | tf_op jit(solution)/shard_map/ppermute | solution.py:244
  105.9 0.8 shard_map.116
  (27 shorter events, 0.1 us)
Async XLA Ops:
  0.6 34.4 %copy-start = (f32[1,384,1536]{2,1,0:T(8,128)S(1)}, f32[1,384,1536]{2,1,0:T(8,128)}, u32[]{:S(2)}) copy-start(f32[1,384,1536]{2,1,0:T(8,128)} %q_down.1) | copy-start | bytes 7077892
  0.6 80.1 %collective-permute-start = (f32[1,384,1536]{2,1,0:T(8,128)}, f32[1,384,1536]{2,1,0:T(8,128)}, u32[]{:S(2)}, u32[]{:S(2)}) collective-permute-start(f32[1,384,1536]{2,1,0:T(8,128)} %c_down.1), channel_id=1, source_target_pairs={{0,15},{1,2},{2,1},{3,4},{4,3},{5,6},{6,5},{7,8},{8,7},{9,10},{10,... | collective-permute-start | bytes 7077896 | tf_op jit(solution)/shard_map/ppermute | solution.py:231
  3.3 79.7 %collective-permute-start.1 = (f32[1,384,1536]{2,1,0:T(8,128)}, f32[1,384,1536]{2,1,0:T(8,128)}, u32[]{:S(2)}, u32[]{:S(2)}) collective-permute-start(f32[1,384,1536]{2,1,0:T(8,128)} %c_down.1), channel_id=1, source_target_pairs={{0,1},{1,0},{2,3},{3,2},{4,5},{5,4},{6,7},{7,6},{8,9},{9,8},{10,11... | collective-permute-start | bytes 7077896 | tf_op jit(solution)/shard_map/ppermute | solution.py:232
  6.2 76.9 %collective-permute-start.2 = (f32[1,384,1536]{2,1,0:T(8,128)}, f32[1,384,1536]{2,1,0:T(8,128)}, u32[]{:S(2)}, u32[]{:S(2)}) collective-permute-start(f32[1,384,1536]{2,1,0:T(8,128)} %q_down.1), channel_id=1, source_target_pairs={{0,1},{1,0},{2,3},{3,2},{4,5},{5,4},{6,7},{7,6},{8,9},{9,8},{10,11... | collective-permute-start | bytes 7077896 | tf_op jit(solution)/shard_map/ppermute | solution.py:233
  6.2 1.7 %copy-start.1 = (f32[1,384,1536]{2,1,0:T(8,128)S(1)}, f32[1,384,1536]{2,1,0:T(8,128)}, u32[]{:S(2)}) copy-start(f32[1,384,1536]{2,1,0:T(8,128)} %c_down.1) | copy-start | bytes 7077892
  7.9 0.7 copy-start.3
  8.5 0.7 copy-start.4
  9.2 27.2 %copy-start.5 = (f32[384]{0:T(512)S(1)}, f32[384]{0:T(512)}, u32[]{:S(2)}) copy-start(f32[384]{0:T(512)} %param.15) | copy-start | bytes 4612
  9.2 29.2 %copy-start.6 = (f32[384]{0:T(512)S(1)}, f32[384]{0:T(512)}, u32[]{:S(2)}) copy-start(f32[384]{0:T(512)} %param.14) | copy-start | bytes 4612
  9.2 29.2 %copy-start.7 = (f32[384]{0:T(512)S(1)}, f32[384]{0:T(512)}, u32[]{:S(2)}) copy-start(f32[384]{0:T(512)} %param.16) | copy-start | bytes 4612
  11.4 27.2 %copy-start.8 = (f32[3]{0:T(128)S(1)}, f32[3]{0:T(128)}, u32[]{:S(2)}) copy-start(f32[3]{0:T(128)} %constant.51) | copy-start | bytes 40
  11.4 2.3 %collective-permute-start.3 = (f32[1,256]{1,0:T(1,128)S(1)}, f32[1,256]{1,0:T(1,128)S(1)}, u32[]{:S(2)}, u32[]{:S(2)}) collective-permute-start(f32[1,256]{1,0:T(1,128)S(1)} %get-tuple-element.21), channel_id=1, source_target_pairs={{0,1},{1,0},{2,3},{3,2},{4,5},{5,4},{6,7},{7,6},{8,9},{9,8},{10,11... | collective-permute-start | bytes 3080 | tf_op jit(solution)/shard_map/ppermute | solution.py:40
  13.7 4.8 %collective-permute-start.4 = (f32[1,256]{1,0:T(1,128)S(1)}, f32[1,256]{1,0:T(1,128)S(1)}, u32[]{:S(2)}, u32[]{:S(2)}) collective-permute-start(f32[1,256]{1,0:T(1,128)S(1)} %add.29), channel_id=1, source_target_pairs={{1,5},{2,6},{5,1},{6,2},{9,13},{10,14},{13,9},{14,10},{17,21},{18,... | collective-permute-start | bytes 3080 | tf_op jit(solution)/shard_map/ppermute | solution.py:42
  18.5 5.7 %collective-permute-start.5 = (f32[1,256]{1,0:T(1,128)S(1)}, f32[1,256]{1,0:T(1,128)S(1)}, u32[]{:S(2)}, u32[]{:S(2)}) collective-permute-start(f32[1,256]{1,0:T(1,128)S(1)} %add.30), channel_id=1, source_target_pairs={{1,9},{2,10},{5,13},{6,14},{9,1},{10,2},{13,5},{14,6},{17,25},{18,... | collective-permute-start | bytes 3080 | tf_op jit(solution)/shard_map/ppermute | solution.py:42
  24.2 2.1 %collective-permute-start.6 = (f32[1,256]{1,0:T(1,128)S(1)}, f32[1,256]{1,0:T(1,128)S(1)}, u32[]{:S(2)}, u32[]{:S(2)}) collective-permute-start(f32[1,256]{1,0:T(1,128)S(1)} %add.31), channel_id=1, source_target_pairs={{1,0},{2,3},{5,4},{6,7},{9,8},{10,11},{13,12},{14,15},{17,16},{18,... | collective-permute-start | bytes 3080 | tf_op jit(solution)/shard_map/ppermute | solution.py:43
  26.3 0.7 collective-permute-start.7
  27.0 8.1 %collective-permute-start.8 = (f32[1,256]{1,0:T(1,128)S(1)}, f32[1,256]{1,0:T(1,128)S(1)}, u32[]{:S(2)}, u32[]{:S(2)}) collective-permute-start(f32[1,256]{1,0:T(1,128)S(1)} %add.32), channel_id=1, source_target_pairs={{0,1},{3,2},{4,5},{7,6},{8,9},{11,10},{12,13},{15,14},{16,17},{19,... | collective-permute-start | bytes 3080 | tf_op jit(solution)/shard_map/ppermute | solution.py:45
  36.4 61.7 %collective-permute-start.11 = (f32[1,264,1536]{2,1,0:T(8,128)}, f32[1,264,1536]{2,1,0:T(8,128)}, u32[]{:S(2)}, u32[]{:S(2)}) collective-permute-start(f32[1,264,1536]{2,1,0:T(8,128)} %slice.40), channel_id=1, source_target_pairs={{0,15},{1,2},{2,1},{3,4},{4,3},{5,6},{6,5},{7,8},{8,7},{9,10},{10,... | collective-permute-start | bytes 4866056 | tf_op jit(solution)/shard_map/ppermute | solution.py:244
  40.8 63.0 %collective-permute-start.10 = (f32[1,88,1536]{2,1,0:T(8,128)}, f32[1,88,1536]{2,1,0:T(8,128)S(1)}, u32[]{:S(2)}, u32[]{:S(2)}) collective-permute-start(f32[1,88,1536]{2,1,0:T(8,128)} %slice.39), channel_id=1, source_target_pairs={{0,15},{1,2},{2,1},{3,4},{4,3},{5,6},{6,5},{7,8},{8,7},{9,10},{10,... | collective-permute-start | bytes 1622024 | tf_op jit(solution)/shard_map/ppermute | solution.py:244
  80.7 25.2 %collective-permute-start.9 = (f32[1,32,1536]{2,1,0:T(8,128)S(1)}, f32[1,32,1536]{2,1,0:T(8,128)S(1)}, u32[]{:S(2)}, u32[]{:S(2)}) collective-permute-start(f32[1,32,1536]{2,1,0:T(8,128)S(1)} %slice.38), channel_id=1, source_target_pairs={{0,15},{1,2},{2,1},{3,4},{4,3},{5,6},{6,5},{7,8},{8,7},{9,10},{10,... | collective-permute-start | bytes 589832 | tf_op jit(solution)/shard_map/ppermute | solution.py:244
  83.0 1.7 %copy-start.2 = (f32[1,384,1536]{2,1,0:T(8,128)S(1)}, f32[1,384,1536]{2,1,0:T(8,128)}, u32[]{:S(2)}) copy-start(f32[1,384,1536]{2,1,0:T(8,128)} %c_down.1) | copy-start | bytes 7077892

commit v3 on v2

--- a/solution.py
+++ b/solution.py
@@ -12,7 +12,8 @@
 
 STATE_PARTS = 48
 STATE_CUTS = (0, 33, 44, 48)
-LOCAL_ROWS = 64
+LOCAL_ROWS = 96
+FAR_WEIGHT = 100000
 ADD_ROWS = 88
 SUB = 8
 
@@ -89,7 +90,7 @@
     )(patch_ids, amplitudes[None], cotangent)
 
 
-def local_kernel(scal, q, q_up, q_down, q_near, c, c_up, c_down, c_near, c_far, wall, coef, q_out, c_out):
+def local_kernel(scal, q, q_up, q_down, q_one, q_two, c, c_up, c_down, c_one, c_two, far, wall, coef, q_out, c_out):
     block, width = q.shape[1:]
     step, side = scal[0], scal[1]
     here, last = pl.program_id(0), pl.num_programs(0) - 1
@@ -109,7 +110,7 @@
     up = jnp.where(here == 0, first_row, q_up[0, SUB - 1 :])
     down = jnp.where(here == last, wall[...], q_down[0, :1])
     above, below = around(x, up, down)
-    near = q_near[0]
+    near = q_one[0] + q_two[0]
     axial = near - (0.5 * side) * (near * (u + 0.5 * near)) - dissipation * x
     q_out[0] = x + step * (
         axial + rd * (above + below - 2.0 * x) + ad * (sides(x) - 2.0 * x)
@@ -123,8 +124,8 @@
     down = jnp.where(here == last, 0.0, after * c_down[0, :1])
     above, below = around(weighted, up, down)
     slope = (0.5 * side) * (u + x)
-    axial = c_near[0] * (1.0 + slope) + c_far[0] * (1.0 - slope) - dissipation * y
-    c_out[0] = y + step * (
+    axial = (c_one[0] + c_two[0]) * (1.0 + slope) - dissipation * y
+    c_out[0] = y + far[0] + step * (
         axial + (above + below - 2.0 * weighted) + ad * (sides(y) - 2.0 * y)
     )
 
@@ -133,7 +134,7 @@
     return coef[0:1, 3:4], coef[0:1, 4:5]
 
 
-def local_parts(scal, q, q_near, c, c_near, c_far, wall, coef):
+def local_parts(scal, q, q_near, c, c_near, far, wall, coef):
     rows, width = q.shape[1:]
     block = math.gcd(LOCAL_ROWS, rows)
     tiles, total = block // SUB, rows // SUB
@@ -149,7 +150,7 @@
         grid=(rows // block,),
         out_shape=(shape, shape),
         in_specs=[pl.BlockSpec(memory_space=pltpu.SMEM)]
-        + [full, up, down, full] * 2
+        + [full, up, down, full, full] * 2
         + [full]
         + [pl.BlockSpec((1, width), lambda i: (0, 0))]
         + [pl.BlockSpec((block, coef.shape[1]), lambda i: (i, 0))],
@@ -158,7 +159,29 @@
         cost_estimate=pl.CostEstimate(
             flops=50 * rows * width, bytes_accessed=4 * rows * width * 7, transcendentals=0
         ),
-    )(scal, q, q, q, q_near, c, c, c, c_near, c_far, wall, coef)
+    )(scal, q, q, q, *q_near, c, c, c, *c_near, far, wall, coef)
+
+
+def cot_kernel(scal, far, state, coef, out):
+    out[0] = scal[0] * far[0] * (1.0 - (0.5 * scal[1]) * (coef[:, 0:1] + state[0]))
+
+
+def cot_term(scal, far, state, coef):
+    rows, width = far.shape[1:]
+    block = math.gcd(128, rows)
+    full = pl.BlockSpec((1, block, width), lambda i: (0, i, 0))
+    return pl.pallas_call(
+        cot_kernel,
+        grid=(rows // block,),
+        out_shape=jax.ShapeDtypeStruct(far.shape, far.dtype),
+        in_specs=[pl.BlockSpec(memory_space=pltpu.SMEM), full, full]
+        + [pl.BlockSpec((block, coef.shape[1]), lambda i: (i, 0))],
+        out_specs=full,
+        compiler_params=pltpu.CompilerParams(vmem_limit_bytes=40 << 20),
+        cost_estimate=pl.CostEstimate(
+            flops=FAR_WEIGHT * rows * width, bytes_accessed=4 * rows * width * 3, transcendentals=0
+        ),
+    )(scal, far, state, coef)
 
 
 def state_far(base, far, weight, out):
@@ -227,10 +250,12 @@
     count = lax.axis_size("ax")
     rows = checkpoint.shape[1]
     patches = amplitudes.shape[0]
-    near, far = on_pairs(count), off_pairs(count)
+    far = off_pairs(count)
+    toward = [(i, i ^ 1) for i in range(count) if i % 4 in (1, 2)]
+    back = [(i, i ^ 1) for i in range(count) if i % 4 not in (1, 2)]
     cot_far_rows = lax.ppermute(cotangent, "ax", far)
-    cot_near_rows = lax.ppermute(cotangent, "ax", near)
-    state_near_rows = lax.ppermute(checkpoint, "ax", near)
+    cot_near = [lax.ppermute(cotangent, "ax", toward)]
+    state_near = [lax.ppermute(checkpoint, "ax", toward)]
 
     wall, binned = wall_and_bins(patch_ids, amplitudes, cotangent)
     if count & (count - 1) or count < 4:
@@ -238,7 +263,11 @@
     else:
         binned = cell_sum(binned, "ax")
 
-    late, binned = lax.optimization_barrier((checkpoint, binned))
+    late, cot_late, binned, *first = lax.optimization_barrier(
+        (checkpoint, cotangent, binned, *cot_near, *state_near)
+    )
+    cot_near = [first[0], lax.ppermute(cot_late, "ax", back)]
+    state_near = [first[1], lax.ppermute(late, "ax", back)]
     edges = [rows * n // STATE_PARTS for n in STATE_CUTS]
     state_far_rows = [
         lax.ppermute(late[:, low:high], "ax", far) for low, high in zip(edges, edges[1:])
@@ -256,11 +285,10 @@
         [step_size + half * axial_speed, jnp.broadcast_to(0.5 * half, axial_speed.shape)], axis=1
     )
 
-    cot_far_rows, cot_near_rows, state_near_rows = lax.optimization_barrier(
-        (cot_far_rows, cot_near_rows, state_near_rows)
-    )
+    term = cot_term(scal, cot_far_rows, checkpoint, coef)
+    term, cot_near, state_near = lax.optimization_barrier((term, cot_near, state_near))
     advanced, adjoint = local_parts(
-        scal, checkpoint, state_near_rows, cotangent, cot_near_rows, cot_far_rows, wall, coef
+        scal, checkpoint, state_near, cotangent, cot_near, term, wall, coef
     )
     bases = [advanced[:, low:high] for low, high in zip(edges[1:], edges[2:])]
     advanced, *bases = lax.optimization_barrier((advanced, *bases))

time: 107 us -> 112 us (1.047)
  starting transfers between devices: 16.6 us -> 24.4 us
  waiting for transfers between devices: 57.3 us -> 54.2 us
  local copies, waits for them, and re-layouts: 9.94 us -> 7.83 us
  Pallas kernels: 16.2 us -> 18.3 us
    ppermute x1, waiting for transfers between devices: 35.5 us -> 43.1 us  [local(): cot_far_rows = lax.ppermute(cotangent, 'ax', far)]
    ppermute x2 -> x4, starting transfers between devices: 2.87 us -> 8.97 us  [the longest x1 3.54 us: local(): cot_near = [lax.ppermute(cotangent, 'ax', toward)]]
    ppermute x2, waiting for transfers between devices: 6.62 us -> 1.64 us  [cell_sum(): value = value + lax.ppermute(value, axis, [(i, i ^ 1 << n) for i in direct])]
    ppermute x2, starting transfers between devices: 3.82 us -> 7.41 us  [cell_sum(): value = value + lax.ppermute(value, axis, [(i, i ^ 1 << n) for i in direct])]
    ppermute x1, waiting for transfers between devices: 6.74 us -> 3.37 us  [cell_sum(): lax.ppermute(value, axis, [(i, i ^ 1) for i in turning])]
    pallas_call x0 -> x1, Pallas kernels: none -> 2.7 us  [cot_term(): pl.pallas_call(cot_kernel, grid=(rows // block,), out_shape=jax.ShapeDtyp...]
    slice x3, local copies, waits for them, and re-layouts: 2.24 us -> 0.16 us  [local(): late[:, low:high]]
    ppermute x1, waiting for transfers between devices: 1.76 us -> 0.01 us  [cell_sum(): lax.ppermute(value, axis, [(i, i ^ 1) for i in range(count)])]
  transfers between devices with their start and end apart: 12 -> 14, of which waited for: 9 -> 8; matrix products, arithmetic and copies ran while one was open for 8% -> 6% of each run, Pallas kernels for 14% -> 16%
where the time goes in v3:
time: 112 us
  waiting for transfers between devices  54.2 us (48%)
  starting transfers between devices  24.4 us (22%)
  Pallas kernels  18.3 us (16%)
  local copies, waits for them, and re-layouts  7.83 us (7%)
  between operations  3.59 us (3%)
  other arithmetic  3.36 us (3%)
    ppermute x1, waiting for transfers between devices, local(): cot_far_rows = lax.ppermute(cotangent, 'ax', far)  43.1 us
    pallas_call x1, Pallas kernels, local_parts(): pl.pallas_call(local_kernel, grid=(rows // block,), out_shape=(shape, sha...  7.97 us
    ppermute x2, starting transfers between devices, cell_sum(): value = value + lax.ppermute(value, axis, [(i, i ^ 1 << n) for i in direct])  7.41 us
    ppermute x3, waiting for transfers between devices, local(): lax.ppermute(late[:, low:high], 'ax', far)  5.32 us
    unnamed x20, local copies, waits for them, and re-layouts  4.54 us
    pallas_call x1, Pallas kernels, add_rows(): pl.pallas_call(state_far, grid=(rows // block,), out_shape=jax.ShapeDtype...  3.66 us
    ppermute x1, starting transfers between devices, local(): cot_near = [lax.ppermute(cotangent, 'ax', toward)]  3.54 us
    ppermute x1, waiting for transfers between devices, cell_sum(): lax.ppermute(value, axis, [(i, i ^ 1) for i in turning])  3.37 us
  transfers between devices with their start and end apart: 14, of which 8 were waited for; matrix products, arithmetic and copies ran while one was open for 6% of the time, Pallas kernels for 16%

profile of v3, /device:TPU:1, one launch (start us, length us, event | category | flops | bytes accessed | tf_op | source)
XLA Modules:
  0.0 111.6 jit_solution(5746916792337709483)
XLA Ops:
  0.6 0.0 copy-start.9
  0.7 3.5 %collective-permute-start.7 = (f32[1,384,1536]{2,1,0:T(8,128)}, f32[1,384,1536]{2,1,0:T(8,128)}, u32[]{:S(2)}, u32[]{:S(2)}) collective-permute-start(f32[1,384,1536]{2,1,0:T(8,128)} %c_down.1), channel_id=1, source_target_pairs={{1,0},{2,3},{5,4},{6,7},{9,8},{10,11},{13,12},{14,15},{17,16},{18,... | collective-permute-start | bytes 7077896 | tf_op jit(solution)/shard_map/ppermute | solution.py:257
  4.2 2.7 %collective-permute-start.8 = (f32[1,384,1536]{2,1,0:T(8,128)}, f32[1,384,1536]{2,1,0:T(8,128)}, u32[]{:S(2)}, u32[]{:S(2)}) collective-permute-start(f32[1,384,1536]{2,1,0:T(8,128)} %q_down.1), channel_id=1, source_target_pairs={{1,0},{2,3},{5,4},{6,7},{9,8},{10,11},{13,12},{14,15},{17,16},{18,... | collective-permute-start | bytes 7077896 | tf_op jit(solution)/shard_map/ppermute | solution.py:258
  6.9 2.4 %collective-permute-start = (f32[1,384,1536]{2,1,0:T(8,128)}, f32[1,384,1536]{2,1,0:T(8,128)}, u32[]{:S(2)}, u32[]{:S(2)}) collective-permute-start(f32[1,384,1536]{2,1,0:T(8,128)} %c_down.1), channel_id=1, source_target_pairs={{0,15},{1,2},{2,1},{3,4},{4,3},{5,6},{6,5},{7,8},{8,7},{9,10},{10,... | collective-permute-start | bytes 7077896 | tf_op jit(solution)/shard_map/ppermute | solution.py:256
  9.3 1.7 %copy-done.1 = f32[1,384,1536]{2,1,0:T(8,128)S(1)} copy-done((f32[1,384,1536]{2,1,0:T(8,128)S(1)}, f32[1,384,1536]{2,1,0:T(8,128)}, u32[]{:S(2)}) %copy-start.1) | copy-done | bytes 2359320
  11.0 0.7 copy-done.4
  11.7 0.7 copy-done.5
  12.4 2.2 %shard_map.113 = (f32[1,1536]{1,0:T(1,128)S(1)}, f32[1,256]{1,0:T(1,128)S(1)}) custom-call(s32[1,1536]{1,0:T(1,128)S(1)} %copy-done.4, f32[1,256]{1,0:T(1,128)S(1)} %bitcast.8, f32[1,384,1536]{2,1,0:T(8,128)S(1)} %copy-done.1), custom_call_target="tpu_custom_call" | custom-call | tf_op jit(solution)/shard_map/pallas_call | solution.py:73
  14.6 0.0 collective-permute-start.1
  15.3 0.6 fusion
  16.5 0.6 multiply_add_fusion
  17.3 3.2 %collective-permute-start.2 = (f32[1,256]{1,0:T(1,128)S(1)}, f32[1,256]{1,0:T(1,128)S(1)}, u32[]{:S(2)}, u32[]{:S(2)}) collective-permute-start(f32[1,256]{1,0:T(1,128)S(1)} %add.29), channel_id=1, source_target_pairs={{1,5},{2,6},{5,1},{6,2},{9,13},{10,14},{13,9},{14,10},{17,21},{18,... | collective-permute-start | bytes 3080 | tf_op jit(solution)/shard_map/ppermute | solution.py:43
  20.5 0.6 slice.32
  21.1 1.0 collective-permute-done.2
  22.1 4.2 %collective-permute-start.3 = (f32[1,256]{1,0:T(1,128)S(1)}, f32[1,256]{1,0:T(1,128)S(1)}, u32[]{:S(2)}, u32[]{:S(2)}) collective-permute-start(f32[1,256]{1,0:T(1,128)S(1)} %add.30), channel_id=1, source_target_pairs={{1,9},{2,10},{5,13},{6,14},{9,1},{10,2},{13,5},{14,6},{17,25},{18,... | collective-permute-start | bytes 3080 | tf_op jit(solution)/shard_map/ppermute | solution.py:43
  26.3 0.7 pad_maximum_fusion.1
  27.0 0.1 slice.34
  27.1 0.7 collective-permute-done.3
  27.7 1.3 %collective-permute-start.4 = (f32[1,256]{1,0:T(1,128)S(1)}, f32[1,256]{1,0:T(1,128)S(1)}, u32[]{:S(2)}, u32[]{:S(2)}) collective-permute-start(f32[1,256]{1,0:T(1,128)S(1)} %add.31), channel_id=1, source_target_pairs={{1,0},{2,3},{5,4},{6,7},{9,8},{10,11},{13,12},{14,15},{17,16},{18,... | collective-permute-start | bytes 3080 | tf_op jit(solution)/shard_map/ppermute | solution.py:44
  29.0 0.1 pad_maximum_fusion.2
  29.1 0.7 collective-permute-done.4
  29.8 0.6 collective-permute-start.5
  30.5 0.7 pad_maximum_fusion.3.scal
  31.2 1.3 %collective-permute-start.6 = (f32[1,256]{1,0:T(1,128)S(1)}, f32[1,256]{1,0:T(1,128)S(1)}, u32[]{:S(2)}, u32[]{:S(2)}) collective-permute-start(f32[1,256]{1,0:T(1,128)S(1)} %add.32), channel_id=1, source_target_pairs={{0,1},{3,2},{4,5},{7,6},{8,9},{11,10},{12,13},{15,14},{16,17},{19,... | collective-permute-start | bytes 3080 | tf_op jit(solution)/shard_map/ppermute | solution.py:46
  32.5 0.1 copy.24.coef
  32.7 0.1 copy.25.coef
  32.9 0.1 stack.36
  34.3 3.4 %collective-permute-done.6 = f32[1,256]{1,0:T(1,128)S(1)} collective-permute-done((f32[1,256]{1,0:T(1,128)S(1)}, f32[1,256]{1,0:T(1,128)S(1)}, u32[]{:S(2)}, u32[]{:S(2)}) %collective-permute-start.6) | collective-permute-done | bytes 1056 | tf_op jit(solution)/shard_map/ppermute | solution.py:46
  37.7 1.4 %collective-permute-start.10 = (f32[1,384,1536]{2,1,0:T(8,128)S(1)}, f32[1,384,1536]{2,1,0:T(8,128)S(1)}, u32[]{:S(2)}, u32[]{:S(2)}) collective-permute-start(f32[1,384,1536]{2,1,0:T(8,128)S(1)} %copy-done), channel_id=1, source_target_pairs={{0,1},{3,2},{4,5},{7,6},{8,9},{11,10},{12,13},{15,14},{16,17},{19,... | collective-permute-start | bytes 7077896 | tf_op jit(solution)/shard_map/ppermute | solution.py:270
  39.2 0.1 slice.40
  39.3 0.0 copy-done.2
  39.4 1.3 %collective-permute-start.9 = (f32[1,384,1536]{2,1,0:T(8,128)S(1)}, f32[1,384,1536]{2,1,0:T(8,128)S(1)}, u32[]{:S(2)}, u32[]{:S(2)}) collective-permute-start(f32[1,384,1536]{2,1,0:T(8,128)S(1)} %copy-done.2), channel_id=1, source_target_pairs={{0,1},{3,2},{4,5},{7,6},{8,9},{11,10},{12,13},{15,14},{16,17},{19,... | collective-permute-start | bytes 7077896 | tf_op jit(solution)/shard_map/ppermute | solution.py:269
  40.7 1.8 %collective-permute-start.13 = (f32[1,264,1536]{2,1,0:T(8,128)S(1)}, f32[1,264,1536]{2,1,0:T(8,128)S(1)}, u32[]{:S(2)}, u32[]{:S(2)}) collective-permute-start(f32[1,264,1536]{2,1,0:T(8,128)S(1)} %slice.40), channel_id=1, source_target_pairs={{0,15},{1,2},{2,1},{3,4},{4,3},{5,6},{6,5},{7,8},{8,7},{9,10},{10,... | collective-permute-start | bytes 4866056 | tf_op jit(solution)/shard_map/ppermute | solution.py:273
  42.5 0.1 collective-permute-start.12
  42.6 43.1 %collective-permute-done.far = f32[1,384,1536]{2,1,0:T(8,128)} collective-permute-done((f32[1,384,1536]{2,1,0:T(8,128)}, f32[1,384,1536]{2,1,0:T(8,128)}, u32[]{:S(2)}, u32[]{:S(2)}) %collective-permute-start) | collective-permute-done | bytes 2359328 | tf_op jit(solution)/shard_map/ppermute | solution.py:256
  85.7 0.5 collective-permute-start.11
  86.1 2.7 %shard_map.112.far = f32[1,384,1536]{2,1,0:T(8,128)S(1)} custom-call(f32[2]{0:T(128)S(1)} %pad_maximum_fusion.3.scal, f32[1,384,1536]{2,1,0:T(8,128)} %collective-permute-done.far, f32[1,384,1536]{2,1,0:T(8,128)S(1)} %copy-done, f32[384,3]{1,0:T(8,128)S(1)} %copy.24.coef), custom_call_target="tpu_custom_call" | custom-call | flops 58982400000 | bytes 7077888 | tf_op jit(solution)/shard_map/pallas_call | solution.py:173
  88.8 1.4 %copy-done.3 = f32[1,384,1536]{2,1,0:T(8,128)} copy-done((f32[1,384,1536]{2,1,0:T(8,128)}, f32[1,384,1536]{2,1,0:T(8,128)S(1)}, u32[]{:S(2)}) %copy-start.3) | copy-done | bytes 2359320
  90.3 0.6 broadcast_multiply_fusion
  90.8 8.0 %shard_map.114 = (f32[1,384,1536]{2,1,0:T(8,128)}, f32[1,384,1536]{2,1,0:T(8,128)}) custom-call(f32[2]{0:T(128)S(1)} %pad_maximum_fusion.3.scal, f32[1,384,1536]{2,1,0:T(8,128)S(1)} %copy-done, f32[1,384,1536]{2,1,0:T(8,128)S(1)} %copy-done, f32[1,384,1536]{2,1,0:T(8,128)S(1)} %copy-done, f32[1,384,1536]{2,1,0:T(8,128)} %collective-permute-done.8.q_one, ...), custom_call_target="tpu_custom_call" | custom-call | flops 29491200 | bytes 16515072 | tf_op jit(solution)/shard_map/pallas_call | solution.py:148
  98.8 1.1 slice.36.base
  99.9 0.9 slice.37.base
  100.8 2.1 %collective-permute-done.13.far = f32[1,264,1536]{2,1,0:T(8,128)S(1)} collective-permute-done((f32[1,264,1536]{2,1,0:T(8,128)S(1)}, f32[1,264,1536]{2,1,0:T(8,128)S(1)}, u32[]{:S(2)}, u32[]{:S(2)}) %collective-permute-start.13) | collective-permute-done | bytes 1622048 | tf_op jit(solution)/shard_map/ppermute | solution.py:273
  102.9 3.7 %shard_map.115.before = f32[1,384,1536]{2,1,0:T(8,128)} custom-call(f32[1,384,1536]{2,1,0:T(8,128)} %get-tuple-element.34.base, f32[1,264,1536]{2,1,0:T(8,128)S(1)} %collective-permute-done.13.far, f32[384,2]{1,0:T(8,128)S(1)} %stack.35.weight), custom_call_target="tpu_custom_call", output_to_operand_aliasing={{}: (0, {})} | custom-call | flops 4055040 | bytes 4866048 | tf_op jit(solution)/shard_map/pallas_call | solution.py:200
  106.6 2.1 %collective-permute-done.12.far = f32[1,88,1536]{2,1,0:T(8,128)S(1)} collective-permute-done((f32[1,88,1536]{2,1,0:T(8,128)S(1)}, f32[1,88,1536]{2,1,0:T(8,128)S(1)}, u32[]{:S(2)}, u32[]{:S(2)}) %collective-permute-start.12) | collective-permute-done | bytes 540704 | tf_op jit(solution)/shard_map/ppermute | solution.py:273
  108.7 1.0 shard_map.116.before
  109.7 1.1 collective-permute-done.11.far
  110.8 0.8 shard_map.117
  (36 shorter events, 0.2 us)
Async XLA Ops:
  0.6 14.6 %copy-start.9 = (f32[3]{0:T(128)S(1)}, f32[3]{0:T(128)}, u32[]{:S(2)}) copy-start(f32[3]{0:T(128)} %constant.51) | copy-start | bytes 40
  0.6 37.1 %copy-start = (f32[1,384,1536]{2,1,0:T(8,128)S(1)}, f32[1,384,1536]{2,1,0:T(8,128)}, u32[]{:S(2)}) copy-start(f32[1,384,1536]{2,1,0:T(8,128)} %q_down.1) | copy-start | bytes 7077892
  0.7 37.0 %collective-permute-start.7 = (f32[1,384,1536]{2,1,0:T(8,128)}, f32[1,384,1536]{2,1,0:T(8,128)}, u32[]{:S(2)}, u32[]{:S(2)}) collective-permute-start(f32[1,384,1536]{2,1,0:T(8,128)} %c_down.1), channel_id=1, source_target_pairs={{1,0},{2,3},{5,4},{6,7},{9,8},{10,11},{13,12},{14,15},{17,16},{18,... | collective-permute-start | bytes 7077896 | tf_op jit(solution)/shard_map/ppermute | solution.py:257
  4.2 33.5 %collective-permute-start.8 = (f32[1,384,1536]{2,1,0:T(8,128)}, f32[1,384,1536]{2,1,0:T(8,128)}, u32[]{:S(2)}, u32[]{:S(2)}) collective-permute-start(f32[1,384,1536]{2,1,0:T(8,128)} %q_down.1), channel_id=1, source_target_pairs={{1,0},{2,3},{5,4},{6,7},{9,8},{10,11},{13,12},{14,15},{17,16},{18,... | collective-permute-start | bytes 7077896 | tf_op jit(solution)/shard_map/ppermute | solution.py:258
  6.9 78.7 %collective-permute-start = (f32[1,384,1536]{2,1,0:T(8,128)}, f32[1,384,1536]{2,1,0:T(8,128)}, u32[]{:S(2)}, u32[]{:S(2)}) collective-permute-start(f32[1,384,1536]{2,1,0:T(8,128)} %c_down.1), channel_id=1, source_target_pairs={{0,15},{1,2},{2,1},{3,4},{4,3},{5,6},{6,5},{7,8},{8,7},{9,10},{10,... | collective-permute-start | bytes 7077896 | tf_op jit(solution)/shard_map/ppermute | solution.py:256
  9.3 1.7 %copy-start.1 = (f32[1,384,1536]{2,1,0:T(8,128)S(1)}, f32[1,384,1536]{2,1,0:T(8,128)}, u32[]{:S(2)}) copy-start(f32[1,384,1536]{2,1,0:T(8,128)} %c_down.1) | copy-start | bytes 7077892
  11.0 0.7 copy-start.4
  11.7 0.7 copy-start.5
  12.4 4.2 %copy-start.7 = (f32[384]{0:T(512)S(1)}, f32[384]{0:T(512)}, u32[]{:S(2)}) copy-start(f32[384]{0:T(512)} %param.14) | copy-start | bytes 4612
  12.4 4.8 %copy-start.6 = (f32[384]{0:T(512)S(1)}, f32[384]{0:T(512)}, u32[]{:S(2)}) copy-start(f32[384]{0:T(512)} %param.15) | copy-start | bytes 4612
  12.4 4.8 %copy-start.8 = (f32[384]{0:T(512)S(1)}, f32[384]{0:T(512)}, u32[]{:S(2)}) copy-start(f32[384]{0:T(512)} %param.16) | copy-start | bytes 4612
  14.6 2.7 %collective-permute-start.1 = (f32[1,256]{1,0:T(1,128)S(1)}, f32[1,256]{1,0:T(1,128)S(1)}, u32[]{:S(2)}, u32[]{:S(2)}) collective-permute-start(f32[1,256]{1,0:T(1,128)S(1)} %get-tuple-element.20), channel_id=1, source_target_pairs={{0,1},{1,0},{2,3},{3,2},{4,5},{5,4},{6,7},{7,6},{8,9},{9,8},{10,11... | collective-permute-start | bytes 3080 | tf_op jit(solution)/shard_map/ppermute | solution.py:41
  17.3 4.8 %collective-permute-start.2 = (f32[1,256]{1,0:T(1,128)S(1)}, f32[1,256]{1,0:T(1,128)S(1)}, u32[]{:S(2)}, u32[]{:S(2)}) collective-permute-start(f32[1,256]{1,0:T(1,128)S(1)} %add.29), channel_id=1, source_target_pairs={{1,5},{2,6},{5,1},{6,2},{9,13},{10,14},{13,9},{14,10},{17,21},{18,... | collective-permute-start | bytes 3080 | tf_op jit(solution)/shard_map/ppermute | solution.py:43
  22.1 5.7 %collective-permute-start.3 = (f32[1,256]{1,0:T(1,128)S(1)}, f32[1,256]{1,0:T(1,128)S(1)}, u32[]{:S(2)}, u32[]{:S(2)}) collective-permute-start(f32[1,256]{1,0:T(1,128)S(1)} %add.30), channel_id=1, source_target_pairs={{1,9},{2,10},{5,13},{6,14},{9,1},{10,2},{13,5},{14,6},{17,25},{18,... | collective-permute-start | bytes 3080 | tf_op jit(solution)/shard_map/ppermute | solution.py:43
  27.7 2.1 %collective-permute-start.4 = (f32[1,256]{1,0:T(1,128)S(1)}, f32[1,256]{1,0:T(1,128)S(1)}, u32[]{:S(2)}, u32[]{:S(2)}) collective-permute-start(f32[1,256]{1,0:T(1,128)S(1)} %add.31), channel_id=1, source_target_pairs={{1,0},{2,3},{5,4},{6,7},{9,8},{10,11},{13,12},{14,15},{17,16},{18,... | collective-permute-start | bytes 3080 | tf_op jit(solution)/shard_map/ppermute | solution.py:44
  29.8 1.4 %collective-permute-start.5 = (f32[1,256]{1,0:T(1,128)S(1)}, f32[1,256]{1,0:T(1,128)S(1)}, u32[]{:S(2)}, u32[]{:S(2)}) collective-permute-start(f32[1,256]{1,0:T(1,128)S(1)} %collective-permute-done.4), channel_id=1, source_target_pairs={{0,3},{3,0},{4,7},{7,4},{8,11},{11,8},{12,15},{15,12},{16,19},{19,... | collective-permute-start | bytes 3080 | tf_op jit(solution)/shard_map/ppermute | solution.py:45
  31.2 6.5 %collective-permute-start.6 = (f32[1,256]{1,0:T(1,128)S(1)}, f32[1,256]{1,0:T(1,128)S(1)}, u32[]{:S(2)}, u32[]{:S(2)}) collective-permute-start(f32[1,256]{1,0:T(1,128)S(1)} %add.32), channel_id=1, source_target_pairs={{0,1},{3,2},{4,5},{7,6},{8,9},{11,10},{12,13},{15,14},{16,17},{19,... | collective-permute-start | bytes 3080 | tf_op jit(solution)/shard_map/ppermute | solution.py:46
  37.7 1.7 %copy-start.2 = (f32[1,384,1536]{2,1,0:T(8,128)S(1)}, f32[1,384,1536]{2,1,0:T(8,128)}, u32[]{:S(2)}) copy-start(f32[1,384,1536]{2,1,0:T(8,128)} %c_down.1) | copy-start | bytes 7077892
  37.7 53.1 %collective-permute-start.10 = (f32[1,384,1536]{2,1,0:T(8,128)S(1)}, f32[1,384,1536]{2,1,0:T(8,128)S(1)}, u32[]{:S(2)}, u32[]{:S(2)}) collective-permute-start(f32[1,384,1536]{2,1,0:T(8,128)S(1)} %copy-done), channel_id=1, source_target_pairs={{0,1},{3,2},{4,5},{7,6},{8,9},{11,10},{12,13},{15,14},{16,17},{19,... | collective-permute-start | bytes 7077896 | tf_op jit(solution)/shard_map/ppermute | solution.py:270
  39.4 51.5 %collective-permute-start.9 = (f32[1,384,1536]{2,1,0:T(8,128)S(1)}, f32[1,384,1536]{2,1,0:T(8,128)S(1)}, u32[]{:S(2)}, u32[]{:S(2)}) collective-permute-start(f32[1,384,1536]{2,1,0:T(8,128)S(1)} %copy-done.2), channel_id=1, source_target_pairs={{0,1},{3,2},{4,5},{7,6},{8,9},{11,10},{12,13},{15,14},{16,17},{19,... | collective-permute-start | bytes 7077896 | tf_op jit(solution)/shard_map/ppermute | solution.py:269
  40.7 62.3 %collective-permute-start.13 = (f32[1,264,1536]{2,1,0:T(8,128)S(1)}, f32[1,264,1536]{2,1,0:T(8,128)S(1)}, u32[]{:S(2)}, u32[]{:S(2)}) collective-permute-start(f32[1,264,1536]{2,1,0:T(8,128)S(1)} %slice.40), channel_id=1, source_target_pairs={{0,15},{1,2},{2,1},{3,4},{4,3},{5,6},{6,5},{7,8},{8,7},{9,10},{10,... | collective-permute-start | bytes 4866056 | tf_op jit(solution)/shard_map/ppermute | solution.py:273
  42.5 66.2 %collective-permute-start.12 = (f32[1,88,1536]{2,1,0:T(8,128)S(1)}, f32[1,88,1536]{2,1,0:T(8,128)S(1)}, u32[]{:S(2)}, u32[]{:S(2)}) collective-permute-start(f32[1,88,1536]{2,1,0:T(8,128)S(1)} %slice.39), channel_id=1, source_target_pairs={{0,15},{1,2},{2,1},{3,4},{4,3},{5,6},{6,5},{7,8},{8,7},{9,10},{10,... | collective-permute-start | bytes 1622024 | tf_op jit(solution)/shard_map/ppermute | solution.py:273
  85.7 25.2 %collective-permute-start.11 = (f32[1,32,1536]{2,1,0:T(8,128)S(1)}, f32[1,32,1536]{2,1,0:T(8,128)S(1)}, u32[]{:S(2)}, u32[]{:S(2)}) collective-permute-start(f32[1,32,1536]{2,1,0:T(8,128)S(1)} %slice.38), channel_id=1, source_target_pairs={{0,15},{1,2},{2,1},{3,4},{4,3},{5,6},{6,5},{7,8},{8,7},{9,10},{10,... | collective-permute-start | bytes 589832 | tf_op jit(solution)/shard_map/ppermute | solution.py:273
  88.8 1.4 %copy-start.3 = (f32[1,384,1536]{2,1,0:T(8,128)}, f32[1,384,1536]{2,1,0:T(8,128)S(1)}, u32[]{:S(2)}) copy-start(f32[1,384,1536]{2,1,0:T(8,128)S(1)} %shard_map.112.far) | copy-start | bytes 7077892

commit v4 on v3

--- a/solution.py
+++ b/solution.py
@@ -90,7 +90,7 @@
     )(patch_ids, amplitudes[None], cotangent)
 
 
-def local_kernel(scal, q, q_up, q_down, q_one, q_two, c, c_up, c_down, c_one, c_two, far, wall, coef, q_out, c_out):
+def local_kernel(scal, q, q_up, q_down, q_near, c, c_up, c_down, c_near, far, wall, coef, q_out, c_out):
     block, width = q.shape[1:]
     step, side = scal[0], scal[1]
     here, last = pl.program_id(0), pl.num_programs(0) - 1
@@ -110,7 +110,7 @@
     up = jnp.where(here == 0, first_row, q_up[0, SUB - 1 :])
     down = jnp.where(here == last, wall[...], q_down[0, :1])
     above, below = around(x, up, down)
-    near = q_one[0] + q_two[0]
+    near = q_near[0]
     axial = near - (0.5 * side) * (near * (u + 0.5 * near)) - dissipation * x
     q_out[0] = x + step * (
         axial + rd * (above + below - 2.0 * x) + ad * (sides(x) - 2.0 * x)
@@ -124,7 +124,7 @@
     down = jnp.where(here == last, 0.0, after * c_down[0, :1])
     above, below = around(weighted, up, down)
     slope = (0.5 * side) * (u + x)
-    axial = (c_one[0] + c_two[0]) * (1.0 + slope) - dissipation * y
+    axial = c_near[0] * (1.0 + slope) - dissipation * y
     c_out[0] = y + far[0] + step * (
         axial + (above + below - 2.0 * weighted) + ad * (sides(y) - 2.0 * y)
     )
@@ -150,7 +150,7 @@
         grid=(rows // block,),
         out_shape=(shape, shape),
         in_specs=[pl.BlockSpec(memory_space=pltpu.SMEM)]
-        + [full, up, down, full, full] * 2
+        + [full, up, down, full] * 2
         + [full]
         + [pl.BlockSpec((1, width), lambda i: (0, 0))]
         + [pl.BlockSpec((block, coef.shape[1]), lambda i: (i, 0))],
@@ -159,7 +159,7 @@
         cost_estimate=pl.CostEstimate(
             flops=50 * rows * width, bytes_accessed=4 * rows * width * 7, transcendentals=0
         ),
-    )(scal, q, q, q, *q_near, c, c, c, *c_near, far, wall, coef)
+    )(scal, q, q, q, q_near, c, c, c, c_near, far, wall, coef)
 
 
 def cot_kernel(scal, far, state, coef, out):
@@ -251,11 +251,7 @@
     rows = checkpoint.shape[1]
     patches = amplitudes.shape[0]
     far = off_pairs(count)
-    toward = [(i, i ^ 1) for i in range(count) if i % 4 in (1, 2)]
-    back = [(i, i ^ 1) for i in range(count) if i % 4 not in (1, 2)]
     cot_far_rows = lax.ppermute(cotangent, "ax", far)
-    cot_near = [lax.ppermute(cotangent, "ax", toward)]
-    state_near = [lax.ppermute(checkpoint, "ax", toward)]
 
     wall, binned = wall_and_bins(patch_ids, amplitudes, cotangent)
     if count & (count - 1) or count < 4:
@@ -263,11 +259,9 @@
     else:
         binned = cell_sum(binned, "ax")
 
-    late, cot_late, binned, *first = lax.optimization_barrier(
-        (checkpoint, cotangent, binned, *cot_near, *state_near)
-    )
-    cot_near = [first[0], lax.ppermute(cot_late, "ax", back)]
-    state_near = [first[1], lax.ppermute(late, "ax", back)]
+    late, cot_late, binned = lax.optimization_barrier((checkpoint, cotangent, binned))
+    cot_near = lax.ppermute(cot_late, "ax", on_pairs(count))
+    state_near = lax.ppermute(late, "ax", on_pairs(count))
     edges = [rows * n // STATE_PARTS for n in STATE_CUTS]
     state_far_rows = [
         lax.ppermute(late[:, low:high], "ax", far) for low, high in zip(edges, edges[1:])

time: 112 us -> 107 us (0.955)
  starting transfers between devices: 24.4 us -> 18.6 us
  waiting for transfers between devices: 54.2 us -> 57.7 us
  Pallas kernels: 18.3 us -> 16.9 us
  local copies, waits for them, and re-layouts: 7.83 us -> 6.55 us
    ppermute x4 -> x2, starting transfers between devices: 8.97 us -> 2.55 us  [the longest x1 1.31 us: local(): state_near = lax.ppermute(late, 'ax', on_pairs(count))]
    ppermute x2, waiting for transfers between devices: 1.64 us -> 5.22 us  [cell_sum(): value = value + lax.ppermute(value, axis, [(i, i ^ 1 << n) for i in direct])]
    ppermute x2, starting transfers between devices: 7.41 us -> 3.83 us  [cell_sum(): value = value + lax.ppermute(value, axis, [(i, i ^ 1 << n) for i in direct])]
    ppermute x1, starting transfers between devices: 0.01 us -> 2.89 us  [cell_sum(): lax.ppermute(value, axis, [(i, i ^ 1) for i in range(count)])]
    ppermute x1, waiting for transfers between devices: 43.1 us -> 40.5 us  [local(): cot_far_rows = lax.ppermute(cotangent, 'ax', far)]
    ppermute x3, waiting for transfers between devices: 5.32 us -> 7.44 us  [local(): lax.ppermute(late[:, low:high], 'ax', far)]
    pallas_call x1, Pallas kernels: 7.97 us -> 6.58 us  [local_parts(): pl.pallas_call(local_kernel, grid=(rows // block,), out_shape=(shape, sha...]
    unnamed x20 -> x18, local copies, waits for them, and re-layouts: 4.54 us -> 3.27 us
  transfers between devices with their start and end apart: 14 -> 12, of which waited for: 8 -> 8; matrix products, arithmetic and copies ran while one was open for 6% -> 6% of each run, Pallas kernels for 16% -> 15%
where the time goes in v4:
time: 107 us
  waiting for transfers between devices  57.7 us (54%)
  starting transfers between devices  18.6 us (17%)
  Pallas kernels  16.9 us (16%)
  local copies, waits for them, and re-layouts  6.55 us (6%)
  between operations  3.54 us (3%)
  other arithmetic  3.36 us (3%)
    ppermute x1, waiting for transfers between devices, local(): cot_far_rows = lax.ppermute(cotangent, 'ax', far)  40.5 us
    ppermute x3, waiting for transfers between devices, local(): lax.ppermute(late[:, low:high], 'ax', far)  7.44 us
    pallas_call x1, Pallas kernels, local_parts(): pl.pallas_call(local_kernel, grid=(rows // block,), out_shape=(shape, sha...  6.58 us
    ppermute x2, waiting for transfers between devices, cell_sum(): value = value + lax.ppermute(value, axis, [(i, i ^ 1 << n) for i in direct])  5.22 us
    ppermute x2, starting transfers between devices, cell_sum(): value = value + lax.ppermute(value, axis, [(i, i ^ 1 << n) for i in direct])  3.83 us
    ppermute x1, waiting for transfers between devices, cell_sum(): lax.ppermute(value, axis, [(i, i ^ 1) for i in turning])  3.82 us
    pallas_call x1, Pallas kernels, add_rows(): pl.pallas_call(state_far, grid=(rows // block,), out_shape=jax.ShapeDtype...  3.66 us
    ppermute x3, starting transfers between devices, local(): lax.ppermute(late[:, low:high], 'ax', far)  3.48 us
  transfers between devices with their start and end apart: 12, of which 8 were waited for; matrix products, arithmetic and copies ran while one was open for 6% of the time, Pallas kernels for 15%

profile of v4, /device:TPU:1, one launch (start us, length us, event | category | flops | bytes accessed | tf_op | source)
XLA Modules:
  0.0 106.7 jit_solution(5086600058768677375)
XLA Ops:
  0.6 0.0 copy-start.8
  0.7 2.7 %collective-permute-start = (f32[1,384,1536]{2,1,0:T(8,128)}, f32[1,384,1536]{2,1,0:T(8,128)}, u32[]{:S(2)}, u32[]{:S(2)}) collective-permute-start(f32[1,384,1536]{2,1,0:T(8,128)} %c_down.1), channel_id=1, source_target_pairs={{0,15},{1,2},{2,1},{3,4},{4,3},{5,6},{6,5},{7,8},{8,7},{9,10},{10,... | collective-permute-start | bytes 7077896 | tf_op jit(solution)/shard_map/ppermute | solution.py:254
  3.3 1.7 %copy-done.1 = f32[1,384,1536]{2,1,0:T(8,128)S(1)} copy-done((f32[1,384,1536]{2,1,0:T(8,128)S(1)}, f32[1,384,1536]{2,1,0:T(8,128)}, u32[]{:S(2)}) %copy-start.1) | copy-done | bytes 2359320
  5.0 0.7 copy-done.3
  5.7 0.7 copy-done.4
  6.4 2.2 %shard_map.113 = (f32[1,1536]{1,0:T(1,128)S(1)}, f32[1,256]{1,0:T(1,128)S(1)}) custom-call(s32[1,1536]{1,0:T(1,128)S(1)} %copy-done.3, f32[1,256]{1,0:T(1,128)S(1)} %bitcast.8, f32[1,384,1536]{2,1,0:T(8,128)S(1)} %copy-done.1), custom_call_target="tpu_custom_call" | custom-call | tf_op jit(solution)/shard_map/pallas_call | solution.py:73
  8.6 2.9 %collective-permute-start.1 = (f32[1,256]{1,0:T(1,128)S(1)}, f32[1,256]{1,0:T(1,128)S(1)}, u32[]{:S(2)}, u32[]{:S(2)}) collective-permute-start(f32[1,256]{1,0:T(1,128)S(1)} %get-tuple-element.16), channel_id=1, source_target_pairs={{0,1},{1,0},{2,3},{3,2},{4,5},{5,4},{6,7},{7,6},{8,9},{9,8},{10,11... | collective-permute-start | bytes 3080 | tf_op jit(solution)/shard_map/ppermute | solution.py:41
  12.2 0.6 fusion
  13.4 0.6 multiply_add_fusion
  14.1 0.0 collective-permute-done.1
  14.2 1.9 %collective-permute-start.2 = (f32[1,256]{1,0:T(1,128)S(1)}, f32[1,256]{1,0:T(1,128)S(1)}, u32[]{:S(2)}, u32[]{:S(2)}) collective-permute-start(f32[1,256]{1,0:T(1,128)S(1)} %add.29), channel_id=1, source_target_pairs={{1,5},{2,6},{5,1},{6,2},{9,13},{10,14},{13,9},{14,10},{17,21},{18,... | collective-permute-start | bytes 3080 | tf_op jit(solution)/shard_map/ppermute | solution.py:43
  16.1 0.6 slice.32
  16.7 2.3 %collective-permute-done.2 = f32[1,256]{1,0:T(1,128)S(1)} collective-permute-done((f32[1,256]{1,0:T(1,128)S(1)}, f32[1,256]{1,0:T(1,128)S(1)}, u32[]{:S(2)}, u32[]{:S(2)}) %collective-permute-start.2) | collective-permute-done | bytes 1056 | tf_op jit(solution)/shard_map/ppermute | solution.py:43
  18.9 1.9 %collective-permute-start.3 = (f32[1,256]{1,0:T(1,128)S(1)}, f32[1,256]{1,0:T(1,128)S(1)}, u32[]{:S(2)}, u32[]{:S(2)}) collective-permute-start(f32[1,256]{1,0:T(1,128)S(1)} %add.30), channel_id=1, source_target_pairs={{1,9},{2,10},{5,13},{6,14},{9,1},{10,2},{13,5},{14,6},{17,25},{18,... | collective-permute-start | bytes 3080 | tf_op jit(solution)/shard_map/ppermute | solution.py:43
  20.9 0.7 pad_maximum_fusion.1
  21.6 0.1 slice.34
  21.7 3.0 %collective-permute-done.3 = f32[1,256]{1,0:T(1,128)S(1)} collective-permute-done((f32[1,256]{1,0:T(1,128)S(1)}, f32[1,256]{1,0:T(1,128)S(1)}, u32[]{:S(2)}, u32[]{:S(2)}) %collective-permute-start.3) | collective-permute-done | bytes 1056 | tf_op jit(solution)/shard_map/ppermute | solution.py:43
  24.6 1.3 %collective-permute-start.4 = (f32[1,256]{1,0:T(1,128)S(1)}, f32[1,256]{1,0:T(1,128)S(1)}, u32[]{:S(2)}, u32[]{:S(2)}) collective-permute-start(f32[1,256]{1,0:T(1,128)S(1)} %add.31), channel_id=1, source_target_pairs={{1,0},{2,3},{5,4},{6,7},{9,8},{10,11},{13,12},{14,15},{17,16},{18,... | collective-permute-start | bytes 3080 | tf_op jit(solution)/shard_map/ppermute | solution.py:44
  25.9 0.1 pad_maximum_fusion.2
  26.0 0.7 collective-permute-done.4
  26.7 0.6 collective-permute-start.5
  27.4 0.7 pad_maximum_fusion.3.scal
  28.1 0.0 collective-permute-done.5
  28.1 1.3 %collective-permute-start.6 = (f32[1,256]{1,0:T(1,128)S(1)}, f32[1,256]{1,0:T(1,128)S(1)}, u32[]{:S(2)}, u32[]{:S(2)}) collective-permute-start(f32[1,256]{1,0:T(1,128)S(1)} %add.32), channel_id=1, source_target_pairs={{0,1},{3,2},{4,5},{7,6},{8,9},{11,10},{12,13},{15,14},{16,17},{19,... | collective-permute-start | bytes 3080 | tf_op jit(solution)/shard_map/ppermute | solution.py:46
  29.4 0.1 copy.24.coef
  29.6 0.1 copy.25.coef
  29.7 0.1 stack.36
  31.2 3.8 %collective-permute-done.6 = f32[1,256]{1,0:T(1,128)S(1)} collective-permute-done((f32[1,256]{1,0:T(1,128)S(1)}, f32[1,256]{1,0:T(1,128)S(1)}, u32[]{:S(2)}, u32[]{:S(2)}) %collective-permute-start.6) | collective-permute-done | bytes 1056 | tf_op jit(solution)/shard_map/ppermute | solution.py:46
  35.0 1.3 %collective-permute-start.8 = (f32[1,384,1536]{2,1,0:T(8,128)S(1)}, f32[1,384,1536]{2,1,0:T(8,128)S(1)}, u32[]{:S(2)}, u32[]{:S(2)}) collective-permute-start(f32[1,384,1536]{2,1,0:T(8,128)S(1)} %copy-done), channel_id=1, source_target_pairs={{0,1},{1,0},{2,3},{3,2},{4,5},{5,4},{6,7},{7,6},{8,9},{9,8},{10,11... | collective-permute-start | bytes 7077896 | tf_op jit(solution)/shard_map/ppermute | solution.py:264
  36.4 0.1 slice.40
  36.5 0.2 copy-done.2
  36.7 1.2 %collective-permute-start.7 = (f32[1,384,1536]{2,1,0:T(8,128)S(1)}, f32[1,384,1536]{2,1,0:T(8,128)S(1)}, u32[]{:S(2)}, u32[]{:S(2)}) collective-permute-start(f32[1,384,1536]{2,1,0:T(8,128)S(1)} %copy-done.2), channel_id=1, source_target_pairs={{0,1},{1,0},{2,3},{3,2},{4,5},{5,4},{6,7},{7,6},{8,9},{9,8},{10,11... | collective-permute-start | bytes 7077896 | tf_op jit(solution)/shard_map/ppermute | solution.py:263
  37.9 0.0 collective-permute-start.11
  37.9 1.7 %collective-permute-start.10 = (f32[1,88,1536]{2,1,0:T(8,128)S(1)}, f32[1,88,1536]{2,1,0:T(8,128)S(1)}, u32[]{:S(2)}, u32[]{:S(2)}) collective-permute-start(f32[1,88,1536]{2,1,0:T(8,128)S(1)} %slice.39), channel_id=1, source_target_pairs={{0,15},{1,2},{2,1},{3,4},{4,3},{5,6},{6,5},{7,8},{8,7},{9,10},{10,... | collective-permute-start | bytes 1622024 | tf_op jit(solution)/shard_map/ppermute | solution.py:267
  39.7 0.6 broadcast_multiply_fusion
  40.3 40.5 %collective-permute-done.far = f32[1,384,1536]{2,1,0:T(8,128)} collective-permute-done((f32[1,384,1536]{2,1,0:T(8,128)}, f32[1,384,1536]{2,1,0:T(8,128)}, u32[]{:S(2)}, u32[]{:S(2)}) %collective-permute-start) | collective-permute-done | bytes 2359328 | tf_op jit(solution)/shard_map/ppermute | solution.py:254
  80.7 1.7 %collective-permute-start.9 = (f32[1,32,1536]{2,1,0:T(8,128)S(1)}, f32[1,32,1536]{2,1,0:T(8,128)S(1)}, u32[]{:S(2)}, u32[]{:S(2)}) collective-permute-start(f32[1,32,1536]{2,1,0:T(8,128)S(1)} %slice.38), channel_id=1, source_target_pairs={{0,15},{1,2},{2,1},{3,4},{4,3},{5,6},{6,5},{7,8},{8,7},{9,10},{10,... | collective-permute-start | bytes 589832 | tf_op jit(solution)/shard_map/ppermute | solution.py:267
  82.5 2.7 %shard_map.112.far = f32[1,384,1536]{2,1,0:T(8,128)S(1)} custom-call(f32[2]{0:T(128)S(1)} %pad_maximum_fusion.3.scal, f32[1,384,1536]{2,1,0:T(8,128)} %collective-permute-done.far, f32[1,384,1536]{2,1,0:T(8,128)S(1)} %copy-done, f32[384,3]{1,0:T(8,128)S(1)} %copy.24.coef), custom_call_target="tpu_custom_call" | custom-call | flops 58982400000 | bytes 7077888 | tf_op jit(solution)/shard_map/pallas_call | solution.py:173
  85.2 0.0 collective-permute-done.7.c_near
  85.2 6.6 %shard_map.114 = (f32[1,384,1536]{2,1,0:T(8,128)}, f32[1,384,1536]{2,1,0:T(8,128)}) custom-call(f32[2]{0:T(128)S(1)} %pad_maximum_fusion.3.scal, f32[1,384,1536]{2,1,0:T(8,128)S(1)} %copy-done, f32[1,384,1536]{2,1,0:T(8,128)S(1)} %copy-done, f32[1,384,1536]{2,1,0:T(8,128)S(1)} %copy-done, f32[1,384,1536]{2,1,0:T(8,128)S(1)} %collective-permute-done.8.q_near, ...), custom_call_target="tpu_custom_call" | custom-call | flops 29491200 | bytes 16515072 | tf_op jit(solution)/shard_map/pallas_call | solution.py:148
  91.8 1.1 %slice.36.base = f32[1,88,1536]{2,1,0:T(8,128)S(1)} slice(f32[1,384,1536]{2,1,0:T(8,128)} %get-tuple-element.26.base), slice={[0:1], [264:352], [0:1536]} | slice | bytes 1081344 | tf_op jit(solution)/shard_map/slice | solution.py:287
  92.9 0.9 slice.37.base
  93.8 4.2 %collective-permute-done.11.far = f32[1,264,1536]{2,1,0:T(8,128)S(1)} collective-permute-done((f32[1,264,1536]{2,1,0:T(8,128)S(1)}, f32[1,264,1536]{2,1,0:T(8,128)S(1)}, u32[]{:S(2)}, u32[]{:S(2)}) %collective-permute-start.11) | collective-permute-done | bytes 1622048 | tf_op jit(solution)/shard_map/ppermute | solution.py:267
  98.0 3.7 %shard_map.115.before = f32[1,384,1536]{2,1,0:T(8,128)} custom-call(f32[1,384,1536]{2,1,0:T(8,128)} %get-tuple-element.26.base, f32[1,264,1536]{2,1,0:T(8,128)S(1)} %collective-permute-done.11.far, f32[384,2]{1,0:T(8,128)S(1)} %stack.35.weight), custom_call_target="tpu_custom_call", output_to_operand_aliasing={{}: (0, {})} | custom-call | flops 4055040 | bytes 4866048 | tf_op jit(solution)/shard_map/pallas_call | solution.py:200
  101.7 2.1 %collective-permute-done.10.far = f32[1,88,1536]{2,1,0:T(8,128)S(1)} collective-permute-done((f32[1,88,1536]{2,1,0:T(8,128)S(1)}, f32[1,88,1536]{2,1,0:T(8,128)S(1)}, u32[]{:S(2)}, u32[]{:S(2)}) %collective-permute-start.10) | collective-permute-done | bytes 540704 | tf_op jit(solution)/shard_map/ppermute | solution.py:267
  103.8 1.0 shard_map.116.before
  104.8 1.1 %collective-permute-done.9.far = f32[1,32,1536]{2,1,0:T(8,128)S(1)} collective-permute-done((f32[1,32,1536]{2,1,0:T(8,128)S(1)}, f32[1,32,1536]{2,1,0:T(8,128)S(1)}, u32[]{:S(2)}, u32[]{:S(2)}) %collective-permute-start.9) | collective-permute-done | bytes 196640 | tf_op jit(solution)/shard_map/ppermute | solution.py:267
  105.9 0.8 shard_map.117
  (30 shorter events, 0.2 us)
Async XLA Ops:
  0.6 11.5 %copy-start.8 = (f32[3]{0:T(128)S(1)}, f32[3]{0:T(128)}, u32[]{:S(2)}) copy-start(f32[3]{0:T(128)} %constant.51) | copy-start | bytes 40
  0.6 34.4 %copy-start = (f32[1,384,1536]{2,1,0:T(8,128)S(1)}, f32[1,384,1536]{2,1,0:T(8,128)}, u32[]{:S(2)}) copy-start(f32[1,384,1536]{2,1,0:T(8,128)} %q_down.1) | copy-start | bytes 7077892
  0.7 80.1 %collective-permute-start = (f32[1,384,1536]{2,1,0:T(8,128)}, f32[1,384,1536]{2,1,0:T(8,128)}, u32[]{:S(2)}, u32[]{:S(2)}) collective-permute-start(f32[1,384,1536]{2,1,0:T(8,128)} %c_down.1), channel_id=1, source_target_pairs={{0,15},{1,2},{2,1},{3,4},{4,3},{5,6},{6,5},{7,8},{8,7},{9,10},{10,... | collective-permute-start | bytes 7077896 | tf_op jit(solution)/shard_map/ppermute | solution.py:254
  3.3 1.7 %copy-start.1 = (f32[1,384,1536]{2,1,0:T(8,128)S(1)}, f32[1,384,1536]{2,1,0:T(8,128)}, u32[]{:S(2)}) copy-start(f32[1,384,1536]{2,1,0:T(8,128)} %c_down.1) | copy-start | bytes 7077892
  5.0 0.7 copy-start.3
  5.7 0.7 copy-start.4
  6.4 7.0 %copy-start.6 = (f32[384]{0:T(512)S(1)}, f32[384]{0:T(512)}, u32[]{:S(2)}) copy-start(f32[384]{0:T(512)} %param.14) | copy-start | bytes 4612
  6.4 7.7 %copy-start.5 = (f32[384]{0:T(512)S(1)}, f32[384]{0:T(512)}, u32[]{:S(2)}) copy-start(f32[384]{0:T(512)} %param.15) | copy-start | bytes 4612
  6.4 7.7 %copy-start.7 = (f32[384]{0:T(512)S(1)}, f32[384]{0:T(512)}, u32[]{:S(2)}) copy-start(f32[384]{0:T(512)} %param.16) | copy-start | bytes 4612
  8.6 5.5 %collective-permute-start.1 = (f32[1,256]{1,0:T(1,128)S(1)}, f32[1,256]{1,0:T(1,128)S(1)}, u32[]{:S(2)}, u32[]{:S(2)}) collective-permute-start(f32[1,256]{1,0:T(1,128)S(1)} %get-tuple-element.16), channel_id=1, source_target_pairs={{0,1},{1,0},{2,3},{3,2},{4,5},{5,4},{6,7},{7,6},{8,9},{9,8},{10,11... | collective-permute-start | bytes 3080 | tf_op jit(solution)/shard_map/ppermute | solution.py:41
  14.2 4.8 %collective-permute-start.2 = (f32[1,256]{1,0:T(1,128)S(1)}, f32[1,256]{1,0:T(1,128)S(1)}, u32[]{:S(2)}, u32[]{:S(2)}) collective-permute-start(f32[1,256]{1,0:T(1,128)S(1)} %add.29), channel_id=1, source_target_pairs={{1,5},{2,6},{5,1},{6,2},{9,13},{10,14},{13,9},{14,10},{17,21},{18,... | collective-permute-start | bytes 3080 | tf_op jit(solution)/shard_map/ppermute | solution.py:43
  18.9 5.7 %collective-permute-start.3 = (f32[1,256]{1,0:T(1,128)S(1)}, f32[1,256]{1,0:T(1,128)S(1)}, u32[]{:S(2)}, u32[]{:S(2)}) collective-permute-start(f32[1,256]{1,0:T(1,128)S(1)} %add.30), channel_id=1, source_target_pairs={{1,9},{2,10},{5,13},{6,14},{9,1},{10,2},{13,5},{14,6},{17,25},{18,... | collective-permute-start | bytes 3080 | tf_op jit(solution)/shard_map/ppermute | solution.py:43
  24.6 2.1 %collective-permute-start.4 = (f32[1,256]{1,0:T(1,128)S(1)}, f32[1,256]{1,0:T(1,128)S(1)}, u32[]{:S(2)}, u32[]{:S(2)}) collective-permute-start(f32[1,256]{1,0:T(1,128)S(1)} %add.31), channel_id=1, source_target_pairs={{1,0},{2,3},{5,4},{6,7},{9,8},{10,11},{13,12},{14,15},{17,16},{18,... | collective-permute-start | bytes 3080 | tf_op jit(solution)/shard_map/ppermute | solution.py:44
  26.7 1.4 %collective-permute-start.5 = (f32[1,256]{1,0:T(1,128)S(1)}, f32[1,256]{1,0:T(1,128)S(1)}, u32[]{:S(2)}, u32[]{:S(2)}) collective-permute-start(f32[1,256]{1,0:T(1,128)S(1)} %collective-permute-done.4), channel_id=1, source_target_pairs={{0,3},{3,0},{4,7},{7,4},{8,11},{11,8},{12,15},{15,12},{16,19},{19,... | collective-permute-start | bytes 3080 | tf_op jit(solution)/shard_map/ppermute | solution.py:45
  28.1 6.9 %collective-permute-start.6 = (f32[1,256]{1,0:T(1,128)S(1)}, f32[1,256]{1,0:T(1,128)S(1)}, u32[]{:S(2)}, u32[]{:S(2)}) collective-permute-start(f32[1,256]{1,0:T(1,128)S(1)} %add.32), channel_id=1, source_target_pairs={{0,1},{3,2},{4,5},{7,6},{8,9},{11,10},{12,13},{15,14},{16,17},{19,... | collective-permute-start | bytes 3080 | tf_op jit(solution)/shard_map/ppermute | solution.py:46
  35.0 1.7 %copy-start.2 = (f32[1,384,1536]{2,1,0:T(8,128)S(1)}, f32[1,384,1536]{2,1,0:T(8,128)}, u32[]{:S(2)}) copy-start(f32[1,384,1536]{2,1,0:T(8,128)} %c_down.1) | copy-start | bytes 7077892
  35.0 50.2 %collective-permute-start.8 = (f32[1,384,1536]{2,1,0:T(8,128)S(1)}, f32[1,384,1536]{2,1,0:T(8,128)S(1)}, u32[]{:S(2)}, u32[]{:S(2)}) collective-permute-start(f32[1,384,1536]{2,1,0:T(8,128)S(1)} %copy-done), channel_id=1, source_target_pairs={{0,1},{1,0},{2,3},{3,2},{4,5},{5,4},{6,7},{7,6},{8,9},{9,8},{10,11... | collective-permute-start | bytes 7077896 | tf_op jit(solution)/shard_map/ppermute | solution.py:264
  36.7 48.5 %collective-permute-start.7 = (f32[1,384,1536]{2,1,0:T(8,128)S(1)}, f32[1,384,1536]{2,1,0:T(8,128)S(1)}, u32[]{:S(2)}, u32[]{:S(2)}) collective-permute-start(f32[1,384,1536]{2,1,0:T(8,128)S(1)} %copy-done.2), channel_id=1, source_target_pairs={{0,1},{1,0},{2,3},{3,2},{4,5},{5,4},{6,7},{7,6},{8,9},{9,8},{10,11... | collective-permute-start | bytes 7077896 | tf_op jit(solution)/shard_map/ppermute | solution.py:263
  37.9 60.1 %collective-permute-start.11 = (f32[1,264,1536]{2,1,0:T(8,128)S(1)}, f32[1,264,1536]{2,1,0:T(8,128)S(1)}, u32[]{:S(2)}, u32[]{:S(2)}) collective-permute-start(f32[1,264,1536]{2,1,0:T(8,128)S(1)} %slice.40), channel_id=1, source_target_pairs={{0,15},{1,2},{2,1},{3,4},{4,3},{5,6},{6,5},{7,8},{8,7},{9,10},{10,... | collective-permute-start | bytes 4866056 | tf_op jit(solution)/shard_map/ppermute | solution.py:267
  37.9 65.9 %collective-permute-start.10 = (f32[1,88,1536]{2,1,0:T(8,128)S(1)}, f32[1,88,1536]{2,1,0:T(8,128)S(1)}, u32[]{:S(2)}, u32[]{:S(2)}) collective-permute-start(f32[1,88,1536]{2,1,0:T(8,128)S(1)} %slice.39), channel_id=1, source_target_pairs={{0,15},{1,2},{2,1},{3,4},{4,3},{5,6},{6,5},{7,8},{8,7},{9,10},{10,... | collective-permute-start | bytes 1622024 | tf_op jit(solution)/shard_map/ppermute | solution.py:267
  80.7 25.2 %collective-permute-start.9 = (f32[1,32,1536]{2,1,0:T(8,128)S(1)}, f32[1,32,1536]{2,1,0:T(8,128)S(1)}, u32[]{:S(2)}, u32[]{:S(2)}) collective-permute-start(f32[1,32,1536]{2,1,0:T(8,128)S(1)} %slice.38), channel_id=1, source_target_pairs={{0,15},{1,2},{2,1},{3,4},{4,3},{5,6},{6,5},{7,8},{8,7},{9,10},{10,... | collective-permute-start | bytes 589832 | tf_op jit(solution)/shard_map/ppermute | solution.py:267

commit v5 on v2

--- a/solution.py
+++ b/solution.py
@@ -10,8 +10,8 @@
 time_step = 0.6
 dissipation = 2.0
 
-STATE_PARTS = 48
-STATE_CUTS = (0, 33, 44, 48)
+STATE_PARTS = 16
+STATE_CUTS = (0, 11, 15, 16)
 LOCAL_ROWS = 64
 ADD_ROWS = 88
 SUB = 8

time: 107 us -> 107 us (level)
  no operation moved by 1% of the time
where the time goes in v5:
time: 107 us
  waiting for transfers between devices  57.1 us (53%)
  starting transfers between devices  16.6 us (16%)
  Pallas kernels  16.2 us (15%)
  local copies, waits for them, and re-layouts  9.97 us (9%)
  between operations  3.45 us (3%)
  other arithmetic  3.35 us (3%)
    ppermute x1, waiting for transfers between devices, local(): cot_far_rows = lax.ppermute(cotangent, 'ax', far)  35.3 us
    pallas_call x1, Pallas kernels, local_parts(): pl.pallas_call(local_kernel, grid=(rows // block,), out_shape=(shape, sha...  8.21 us
    ppermute x1, waiting for transfers between devices, cell_sum(): lax.ppermute(value, axis, [(i, i ^ 1) for i in turning])  6.74 us
    ppermute x2, waiting for transfers between devices, cell_sum(): value = value + lax.ppermute(value, axis, [(i, i ^ 1 << n) for i in direct])  6.62 us
    ppermute x3, waiting for transfers between devices, local(): lax.ppermute(late[:, low:high], 'ax', far)  5.92 us
    unnamed x18, local copies, waits for them, and re-layouts  4.73 us
    pallas_call x1, Pallas kernels, add_rows(): pl.pallas_call(state_far, grid=(rows // block,), out_shape=jax.ShapeDtype...  4.02 us
    ppermute x2, starting transfers between devices, cell_sum(): value = value + lax.ppermute(value, axis, [(i, i ^ 1 << n) for i in direct])  3.82 us
  transfers between devices with their start and end apart: 12, of which 9 were waited for; matrix products, arithmetic and copies ran while one was open for 8% of the time, Pallas kernels for 14%

profile of v5, /device:TPU:1, one launch (start us, length us, event | category | flops | bytes accessed | tf_op | source)
XLA Modules:
  0.0 106.7 jit_solution(12892695909432634500)
XLA Ops:
  0.6 2.7 %collective-permute-start = (f32[1,384,1536]{2,1,0:T(8,128)}, f32[1,384,1536]{2,1,0:T(8,128)}, u32[]{:S(2)}, u32[]{:S(2)}) collective-permute-start(f32[1,384,1536]{2,1,0:T(8,128)} %c_down.1), channel_id=1, source_target_pairs={{0,15},{1,2},{2,1},{3,4},{4,3},{5,6},{6,5},{7,8},{8,7},{9,10},{10,... | collective-permute-start | bytes 7077896 | tf_op jit(solution)/shard_map/ppermute | solution.py:231
  3.3 2.9 %collective-permute-start.1 = (f32[1,384,1536]{2,1,0:T(8,128)}, f32[1,384,1536]{2,1,0:T(8,128)}, u32[]{:S(2)}, u32[]{:S(2)}) collective-permute-start(f32[1,384,1536]{2,1,0:T(8,128)} %c_down.1), channel_id=1, source_target_pairs={{0,1},{1,0},{2,3},{3,2},{4,5},{5,4},{6,7},{7,6},{8,9},{9,8},{10,11... | collective-permute-start | bytes 7077896 | tf_op jit(solution)/shard_map/ppermute | solution.py:232
  6.2 0.0 collective-permute-start.2
  6.2 1.7 %copy-done.1 = f32[1,384,1536]{2,1,0:T(8,128)S(1)} copy-done((f32[1,384,1536]{2,1,0:T(8,128)S(1)}, f32[1,384,1536]{2,1,0:T(8,128)}, u32[]{:S(2)}) %copy-start.1) | copy-done | bytes 2359320
  7.9 0.7 copy-done.3
  8.5 0.7 copy-done.4
  9.2 2.2 %shard_map.112 = (f32[1,1536]{1,0:T(1,128)S(1)}, f32[1,256]{1,0:T(1,128)S(1)}) custom-call(s32[1,1536]{1,0:T(1,128)S(1)} %copy-done.3, f32[1,256]{1,0:T(1,128)S(1)} %bitcast.8, f32[1,384,1536]{2,1,0:T(8,128)S(1)} %copy-done.1), custom_call_target="tpu_custom_call" | custom-call | tf_op jit(solution)/shard_map/pallas_call | solution.py:72
  11.4 0.0 copy-start.7
  11.4 0.6 collective-permute-start.3
  12.0 1.7 %collective-permute-done.3 = f32[1,256]{1,0:T(1,128)S(1)} collective-permute-done((f32[1,256]{1,0:T(1,128)S(1)}, f32[1,256]{1,0:T(1,128)S(1)}, u32[]{:S(2)}, u32[]{:S(2)}) %collective-permute-start.3) | collective-permute-done | bytes 1056 | tf_op jit(solution)/shard_map/ppermute | solution.py:40
  13.7 1.9 %collective-permute-start.4 = (f32[1,256]{1,0:T(1,128)S(1)}, f32[1,256]{1,0:T(1,128)S(1)}, u32[]{:S(2)}, u32[]{:S(2)}) collective-permute-start(f32[1,256]{1,0:T(1,128)S(1)} %add.29), channel_id=1, source_target_pairs={{1,5},{2,6},{5,1},{6,2},{9,13},{10,14},{13,9},{14,10},{17,21},{18,... | collective-permute-start | bytes 3080 | tf_op jit(solution)/shard_map/ppermute | solution.py:42
  15.6 2.9 %collective-permute-done.4 = f32[1,256]{1,0:T(1,128)S(1)} collective-permute-done((f32[1,256]{1,0:T(1,128)S(1)}, f32[1,256]{1,0:T(1,128)S(1)}, u32[]{:S(2)}, u32[]{:S(2)}) %collective-permute-start.4) | collective-permute-done | bytes 1056 | tf_op jit(solution)/shard_map/ppermute | solution.py:42
  18.5 1.9 %collective-permute-start.5 = (f32[1,256]{1,0:T(1,128)S(1)}, f32[1,256]{1,0:T(1,128)S(1)}, u32[]{:S(2)}, u32[]{:S(2)}) collective-permute-start(f32[1,256]{1,0:T(1,128)S(1)} %add.30), channel_id=1, source_target_pairs={{1,9},{2,10},{5,13},{6,14},{9,1},{10,2},{13,5},{14,6},{17,25},{18,... | collective-permute-start | bytes 3080 | tf_op jit(solution)/shard_map/ppermute | solution.py:42
  20.4 3.8 %collective-permute-done.5 = f32[1,256]{1,0:T(1,128)S(1)} collective-permute-done((f32[1,256]{1,0:T(1,128)S(1)}, f32[1,256]{1,0:T(1,128)S(1)}, u32[]{:S(2)}, u32[]{:S(2)}) %collective-permute-start.5) | collective-permute-done | bytes 1056 | tf_op jit(solution)/shard_map/ppermute | solution.py:42
  24.2 1.3 %collective-permute-start.6 = (f32[1,256]{1,0:T(1,128)S(1)}, f32[1,256]{1,0:T(1,128)S(1)}, u32[]{:S(2)}, u32[]{:S(2)}) collective-permute-start(f32[1,256]{1,0:T(1,128)S(1)} %add.31), channel_id=1, source_target_pairs={{1,0},{2,3},{5,4},{6,7},{9,8},{10,11},{13,12},{14,15},{17,16},{18,... | collective-permute-start | bytes 3080 | tf_op jit(solution)/shard_map/ppermute | solution.py:43
  25.5 0.8 collective-permute-done.6
  26.3 0.6 collective-permute-start.7
  26.9 0.0 collective-permute-done.7
  27.0 1.3 %collective-permute-start.8 = (f32[1,256]{1,0:T(1,128)S(1)}, f32[1,256]{1,0:T(1,128)S(1)}, u32[]{:S(2)}, u32[]{:S(2)}) collective-permute-start(f32[1,256]{1,0:T(1,128)S(1)} %add.32), channel_id=1, source_target_pairs={{0,1},{3,2},{4,5},{7,6},{8,9},{11,10},{12,13},{15,14},{16,17},{19,... | collective-permute-start | bytes 3080 | tf_op jit(solution)/shard_map/ppermute | solution.py:45
  28.3 6.7 %collective-permute-done.8 = f32[1,256]{1,0:T(1,128)S(1)} collective-permute-done((f32[1,256]{1,0:T(1,128)S(1)}, f32[1,256]{1,0:T(1,128)S(1)}, u32[]{:S(2)}, u32[]{:S(2)}) %collective-permute-start.8) | collective-permute-done | bytes 1056 | tf_op jit(solution)/shard_map/ppermute | solution.py:45
  35.0 1.4 %slice.40 = f32[1,264,1536]{2,1,0:T(8,128)} slice(f32[1,384,1536]{2,1,0:T(8,128)S(1)} %copy-done), slice={[0:1], [0:264], [0:1536]} | slice | bytes 3244032 | tf_op jit(solution)/shard_map/slice | solution.py:244
  36.4 0.0 collective-permute-start.11
  36.4 0.6 slice.32
  37.0 0.1 slice.34
  37.7 0.7 pad_maximum_fusion
  38.4 0.6 fusion
  39.0 0.9 slice.39
  39.9 1.7 %collective-permute-start.10 = (f32[1,96,1536]{2,1,0:T(8,128)}, f32[1,96,1536]{2,1,0:T(8,128)S(1)}, u32[]{:S(2)}, u32[]{:S(2)}) collective-permute-start(f32[1,96,1536]{2,1,0:T(8,128)} %slice.39), channel_id=1, source_target_pairs={{0,15},{1,2},{2,1},{3,4},{4,3},{5,6},{6,5},{7,8},{8,7},{9,10},{10,... | collective-permute-start | bytes 1769480 | tf_op jit(solution)/shard_map/ppermute | solution.py:244
  41.6 0.1 pad_maximum_fusion.1
  41.8 0.1 copy.21.coef
  42.6 0.6 multiply_add_fusion
  43.3 0.1 stack.32
  44.7 0.7 pad_maximum_fusion.2.scal
  45.4 35.3 %collective-permute-done.c_far = f32[1,384,1536]{2,1,0:T(8,128)} collective-permute-done((f32[1,384,1536]{2,1,0:T(8,128)}, f32[1,384,1536]{2,1,0:T(8,128)}, u32[]{:S(2)}, u32[]{:S(2)}) %collective-permute-start) | collective-permute-done | bytes 2359328 | tf_op jit(solution)/shard_map/ppermute | solution.py:231
  80.7 1.7 %collective-permute-start.9 = (f32[1,24,1536]{2,1,0:T(8,128)S(1)}, f32[1,24,1536]{2,1,0:T(8,128)S(1)}, u32[]{:S(2)}, u32[]{:S(2)}) collective-permute-start(f32[1,24,1536]{2,1,0:T(8,128)S(1)} %slice.38), channel_id=1, source_target_pairs={{0,15},{1,2},{2,1},{3,4},{4,3},{5,6},{6,5},{7,8},{8,7},{9,10},{10,... | collective-permute-start | bytes 442376 | tf_op jit(solution)/shard_map/ppermute | solution.py:244
  82.5 0.6 broadcast_multiply_fusion
  83.0 0.0 collective-permute-done.1.c_near
  83.0 0.0 collective-permute-done.2.q_near
  83.0 1.7 %copy-done.2 = f32[1,384,1536]{2,1,0:T(8,128)S(1)} copy-done((f32[1,384,1536]{2,1,0:T(8,128)S(1)}, f32[1,384,1536]{2,1,0:T(8,128)}, u32[]{:S(2)}) %copy-start.2) | copy-done | bytes 2359320
  84.7 8.2 %shard_map.113 = (f32[1,384,1536]{2,1,0:T(8,128)}, f32[1,384,1536]{2,1,0:T(8,128)}) custom-call(f32[2]{0:T(128)S(1)} %pad_maximum_fusion.2.scal, f32[1,384,1536]{2,1,0:T(8,128)S(1)} %copy-done, f32[1,384,1536]{2,1,0:T(8,128)S(1)} %copy-done, f32[1,384,1536]{2,1,0:T(8,128)S(1)} %copy-done, f32[1,384,1536]{2,1,0:T(8,128)} %collective-permute-done.2.q_near, ...), custom_call_target="tpu_custom_call" | custom-call | flops 29491200 | bytes 16515072 | tf_op jit(solution)/shard_map/pallas_call | solution.py:147
  92.9 1.1 %slice.36.base = f32[1,96,1536]{2,1,0:T(8,128)S(1)} slice(f32[1,384,1536]{2,1,0:T(8,128)} %get-tuple-element.24.base), slice={[0:1], [264:360], [0:1536]} | slice | bytes 1179648 | tf_op jit(solution)/shard_map/slice | solution.py:265
  94.0 0.9 slice.37.base
  94.9 3.2 %collective-permute-done.11.far = f32[1,264,1536]{2,1,0:T(8,128)} collective-permute-done((f32[1,264,1536]{2,1,0:T(8,128)}, f32[1,264,1536]{2,1,0:T(8,128)}, u32[]{:S(2)}, u32[]{:S(2)}) %collective-permute-start.11) | collective-permute-done | bytes 1622048 | tf_op jit(solution)/shard_map/ppermute | solution.py:244
  98.1 4.0 %shard_map.114.before = f32[1,384,1536]{2,1,0:T(8,128)} custom-call(f32[1,384,1536]{2,1,0:T(8,128)} %get-tuple-element.24.base, f32[1,264,1536]{2,1,0:T(8,128)} %collective-permute-done.11.far, f32[384,2]{1,0:T(8,128)S(1)} %stack.31.weight), custom_call_target="tpu_custom_call", output_to_operand_aliasing={{}: (0, {})} | custom-call | flops 4055040 | bytes 4866048 | tf_op jit(solution)/shard_map/pallas_call | solution.py:177
  102.1 2.2 %collective-permute-done.10.far = f32[1,96,1536]{2,1,0:T(8,128)S(1)} collective-permute-done((f32[1,96,1536]{2,1,0:T(8,128)}, f32[1,96,1536]{2,1,0:T(8,128)S(1)}, u32[]{:S(2)}, u32[]{:S(2)}) %collective-permute-start.10) | collective-permute-done | bytes 589856 | tf_op jit(solution)/shard_map/ppermute | solution.py:244
  104.3 1.0 shard_map.115.before
  105.3 0.6 collective-permute-done.9.far
  105.9 0.8 shard_map.116
  (27 shorter events, 0.1 us)
Async XLA Ops:
  0.6 34.4 %copy-start = (f32[1,384,1536]{2,1,0:T(8,128)S(1)}, f32[1,384,1536]{2,1,0:T(8,128)}, u32[]{:S(2)}) copy-start(f32[1,384,1536]{2,1,0:T(8,128)} %q_down.1) | copy-start | bytes 7077892
  0.6 80.1 %collective-permute-start = (f32[1,384,1536]{2,1,0:T(8,128)}, f32[1,384,1536]{2,1,0:T(8,128)}, u32[]{:S(2)}, u32[]{:S(2)}) collective-permute-start(f32[1,384,1536]{2,1,0:T(8,128)} %c_down.1), channel_id=1, source_target_pairs={{0,15},{1,2},{2,1},{3,4},{4,3},{5,6},{6,5},{7,8},{8,7},{9,10},{10,... | collective-permute-start | bytes 7077896 | tf_op jit(solution)/shard_map/ppermute | solution.py:231
  3.3 79.7 %collective-permute-start.1 = (f32[1,384,1536]{2,1,0:T(8,128)}, f32[1,384,1536]{2,1,0:T(8,128)}, u32[]{:S(2)}, u32[]{:S(2)}) collective-permute-start(f32[1,384,1536]{2,1,0:T(8,128)} %c_down.1), channel_id=1, source_target_pairs={{0,1},{1,0},{2,3},{3,2},{4,5},{5,4},{6,7},{7,6},{8,9},{9,8},{10,11... | collective-permute-start | bytes 7077896 | tf_op jit(solution)/shard_map/ppermute | solution.py:232
  6.2 76.9 %collective-permute-start.2 = (f32[1,384,1536]{2,1,0:T(8,128)}, f32[1,384,1536]{2,1,0:T(8,128)}, u32[]{:S(2)}, u32[]{:S(2)}) collective-permute-start(f32[1,384,1536]{2,1,0:T(8,128)} %q_down.1), channel_id=1, source_target_pairs={{0,1},{1,0},{2,3},{3,2},{4,5},{5,4},{6,7},{7,6},{8,9},{9,8},{10,11... | collective-permute-start | bytes 7077896 | tf_op jit(solution)/shard_map/ppermute | solution.py:233
  6.2 1.7 %copy-start.1 = (f32[1,384,1536]{2,1,0:T(8,128)S(1)}, f32[1,384,1536]{2,1,0:T(8,128)}, u32[]{:S(2)}) copy-start(f32[1,384,1536]{2,1,0:T(8,128)} %c_down.1) | copy-start | bytes 7077892
  7.8 0.7 copy-start.3
  8.5 0.7 copy-start.4
  9.2 27.2 %copy-start.5 = (f32[384]{0:T(512)S(1)}, f32[384]{0:T(512)}, u32[]{:S(2)}) copy-start(f32[384]{0:T(512)} %param.15) | copy-start | bytes 4612
  9.2 29.2 %copy-start.8 = (f32[3]{0:T(128)S(1)}, f32[3]{0:T(128)}, u32[]{:S(2)}) copy-start(f32[3]{0:T(128)} %constant.51) | copy-start | bytes 40
  11.4 30.3 %copy-start.6 = (f32[384]{0:T(512)S(1)}, f32[384]{0:T(512)}, u32[]{:S(2)}) copy-start(f32[384]{0:T(512)} %param.14) | copy-start | bytes 4612
  11.4 30.3 %copy-start.7 = (f32[384]{0:T(512)S(1)}, f32[384]{0:T(512)}, u32[]{:S(2)}) copy-start(f32[384]{0:T(512)} %param.16) | copy-start | bytes 4612
  11.4 2.3 %collective-permute-start.3 = (f32[1,256]{1,0:T(1,128)S(1)}, f32[1,256]{1,0:T(1,128)S(1)}, u32[]{:S(2)}, u32[]{:S(2)}) collective-permute-start(f32[1,256]{1,0:T(1,128)S(1)} %get-tuple-element.21), channel_id=1, source_target_pairs={{0,1},{1,0},{2,3},{3,2},{4,5},{5,4},{6,7},{7,6},{8,9},{9,8},{10,11... | collective-permute-start | bytes 3080 | tf_op jit(solution)/shard_map/ppermute | solution.py:40
  13.7 4.8 %collective-permute-start.4 = (f32[1,256]{1,0:T(1,128)S(1)}, f32[1,256]{1,0:T(1,128)S(1)}, u32[]{:S(2)}, u32[]{:S(2)}) collective-permute-start(f32[1,256]{1,0:T(1,128)S(1)} %add.29), channel_id=1, source_target_pairs={{1,5},{2,6},{5,1},{6,2},{9,13},{10,14},{13,9},{14,10},{17,21},{18,... | collective-permute-start | bytes 3080 | tf_op jit(solution)/shard_map/ppermute | solution.py:42
  18.5 5.7 %collective-permute-start.5 = (f32[1,256]{1,0:T(1,128)S(1)}, f32[1,256]{1,0:T(1,128)S(1)}, u32[]{:S(2)}, u32[]{:S(2)}) collective-permute-start(f32[1,256]{1,0:T(1,128)S(1)} %add.30), channel_id=1, source_target_pairs={{1,9},{2,10},{5,13},{6,14},{9,1},{10,2},{13,5},{14,6},{17,25},{18,... | collective-permute-start | bytes 3080 | tf_op jit(solution)/shard_map/ppermute | solution.py:42
  24.2 2.1 %collective-permute-start.6 = (f32[1,256]{1,0:T(1,128)S(1)}, f32[1,256]{1,0:T(1,128)S(1)}, u32[]{:S(2)}, u32[]{:S(2)}) collective-permute-start(f32[1,256]{1,0:T(1,128)S(1)} %add.31), channel_id=1, source_target_pairs={{1,0},{2,3},{5,4},{6,7},{9,8},{10,11},{13,12},{14,15},{17,16},{18,... | collective-permute-start | bytes 3080 | tf_op jit(solution)/shard_map/ppermute | solution.py:43
  26.3 0.7 collective-permute-start.7
  27.0 8.1 %collective-permute-start.8 = (f32[1,256]{1,0:T(1,128)S(1)}, f32[1,256]{1,0:T(1,128)S(1)}, u32[]{:S(2)}, u32[]{:S(2)}) collective-permute-start(f32[1,256]{1,0:T(1,128)S(1)} %add.32), channel_id=1, source_target_pairs={{0,1},{3,2},{4,5},{7,6},{8,9},{11,10},{12,13},{15,14},{16,17},{19,... | collective-permute-start | bytes 3080 | tf_op jit(solution)/shard_map/ppermute | solution.py:45
  36.4 61.7 %collective-permute-start.11 = (f32[1,264,1536]{2,1,0:T(8,128)}, f32[1,264,1536]{2,1,0:T(8,128)}, u32[]{:S(2)}, u32[]{:S(2)}) collective-permute-start(f32[1,264,1536]{2,1,0:T(8,128)} %slice.40), channel_id=1, source_target_pairs={{0,15},{1,2},{2,1},{3,4},{4,3},{5,6},{6,5},{7,8},{8,7},{9,10},{10,... | collective-permute-start | bytes 4866056 | tf_op jit(solution)/shard_map/ppermute | solution.py:244
  39.9 64.4 %collective-permute-start.10 = (f32[1,96,1536]{2,1,0:T(8,128)}, f32[1,96,1536]{2,1,0:T(8,128)S(1)}, u32[]{:S(2)}, u32[]{:S(2)}) collective-permute-start(f32[1,96,1536]{2,1,0:T(8,128)} %slice.39), channel_id=1, source_target_pairs={{0,15},{1,2},{2,1},{3,4},{4,3},{5,6},{6,5},{7,8},{8,7},{9,10},{10,... | collective-permute-start | bytes 1769480 | tf_op jit(solution)/shard_map/ppermute | solution.py:244
  80.7 25.2 %collective-permute-start.9 = (f32[1,24,1536]{2,1,0:T(8,128)S(1)}, f32[1,24,1536]{2,1,0:T(8,128)S(1)}, u32[]{:S(2)}, u32[]{:S(2)}) collective-permute-start(f32[1,24,1536]{2,1,0:T(8,128)S(1)} %slice.38), channel_id=1, source_target_pairs={{0,15},{1,2},{2,1},{3,4},{4,3},{5,6},{6,5},{7,8},{8,7},{9,10},{10,... | collective-permute-start | bytes 442376 | tf_op jit(solution)/shard_map/ppermute | solution.py:244
  83.0 1.7 %copy-start.2 = (f32[1,384,1536]{2,1,0:T(8,128)S(1)}, f32[1,384,1536]{2,1,0:T(8,128)}, u32[]{:S(2)}) copy-start(f32[1,384,1536]{2,1,0:T(8,128)} %c_down.1) | copy-start | bytes 7077892

commit v6 on v5

--- a/solution.py
+++ b/solution.py
@@ -10,10 +10,9 @@
 time_step = 0.6
 dissipation = 2.0
 
-STATE_PARTS = 16
-STATE_CUTS = (0, 11, 15, 16)
+STATE_PARTS = 12
+STATE_CUTS = (0, 11, 12)
 LOCAL_ROWS = 64
-ADD_ROWS = 88
 SUB = 8
 
 
@@ -161,33 +160,6 @@
     )(scal, q, q, q, q_near, c, c, c, c_near, c_far, wall, coef)
 
 
-def state_far(base, far, weight, out):
-    x = far[0]
-    out[0] = base[0] + x * (weight[:, 0:1] + weight[:, 1:2] * x)
-
-
-def add_rows(base, part, weight, start):
-    rows, width = part.shape[1:]
-    whole = rows <= ADD_ROWS and start % rows == 0
-    block = rows if whole else math.gcd(ADD_ROWS, rows, start)
-    first = start // block
-    full = pl.BlockSpec((1, block, width), lambda i: (0, first + i, 0))
-    piece = pl.BlockSpec((1, block, width), lambda i: (0, i, 0))
-    column = pl.BlockSpec((block, weight.shape[1]), lambda i: (first + i, 0))
-    return pl.pallas_call(
-        state_far,
-        grid=(rows // block,),
-        out_shape=jax.ShapeDtypeStruct(base.shape, base.dtype),
-        in_specs=[full, piece, column],
-        out_specs=full,
-        input_output_aliases={0: 0},
-        compiler_params=pltpu.CompilerParams(vmem_limit_bytes=40 << 20),
-        cost_estimate=pl.CostEstimate(
-            flops=10 * rows * width, bytes_accessed=4 * rows * width * 3, transcendentals=0
-        ),
-    )(base, part, weight)
-
-
 def put_rows(out, base, part, weight, start):
     rows, width = part.shape[1:]
 
@@ -262,10 +234,9 @@
     advanced, adjoint = local_parts(
         scal, checkpoint, state_near_rows, cotangent, cot_near_rows, cot_far_rows, wall, coef
     )
-    bases = [advanced[:, low:high] for low, high in zip(edges[1:], edges[2:])]
+    bases = [advanced[:, low:high] for low, high in zip(edges, edges[1:])]
     advanced, *bases = lax.optimization_barrier((advanced, *bases))
-    advanced = add_rows(advanced, state_far_rows[0], weight, 0)
-    for low, base, part in zip(edges[1:], bases, state_far_rows[1:]):
+    for low, base, part in zip(edges, bases, state_far_rows):
         advanced = put_rows(advanced, base, part, weight, low)
     return (advanced, adjoint, gradient)
 

time: 107 us -> 129 us (1.21)
  waiting for transfers between devices: 57.1 us -> 76.7 us
  starting transfers between devices: 16.6 us -> 22.3 us
  local copies, waits for them, and re-layouts: 9.97 us -> 6.75 us
    ppermute x1, waiting for transfers between devices: 35.3 us -> 58.6 us  [local(): cot_far_rows = lax.ppermute(cotangent, 'ax', far)]
    ppermute x3 -> x2, waiting for transfers between devices: 5.92 us -> 11.7 us  [local(): lax.ppermute(late[:, low:high], 'ax', far)]
    ppermute x2, starting transfers between devices: 3.82 us -> 8.74 us  [cell_sum(): value = value + lax.ppermute(value, axis, [(i, i ^ 1 << n) for i in direct])]
    ppermute x2, waiting for transfers between devices: 6.62 us -> 1.89 us  [cell_sum(): value = value + lax.ppermute(value, axis, [(i, i ^ 1 << n) for i in direct])]
    ppermute x1, waiting for transfers between devices: 6.74 us -> 2.67 us  [cell_sum(): lax.ppermute(value, axis, [(i, i ^ 1) for i in turning])]
    pallas_call x1 -> x0, Pallas kernels: 4.02 us -> none  [add_rows(): pl.pallas_call(state_far, grid=(rows // block,), out_shape=jax.ShapeDtype...]
    unnamed x18 -> x14, local copies, waits for them, and re-layouts: 4.73 us -> 1.55 us
    pallas_call x2, Pallas kernels: 1.77 us -> 4.25 us  [put_rows(): pl.pallas_call(kernel, out_shape=jax.ShapeDtypeStruct(out.shape, out.dtyp...]
  transfers between devices with their start and end apart: 12 -> 11, of which waited for: 9 -> 7; matrix products, arithmetic and copies ran while one was open for 8% -> 7% of each run, Pallas kernels for 14% -> 10%
where the time goes in v6:
time: 129 us
  waiting for transfers between devices  76.7 us (59%)
  starting transfers between devices  22.3 us (17%)
  Pallas kernels  16.1 us (12%)
  local copies, waits for them, and re-layouts  6.75 us (5%)
  between operations  3.38 us (3%)
  other arithmetic  3.27 us (3%)
    ppermute x1, waiting for transfers between devices, local(): cot_far_rows = lax.ppermute(cotangent, 'ax', far)  58.6 us
    ppermute x2, waiting for transfers between devices, local(): lax.ppermute(late[:, low:high], 'ax', far)  11.7 us
    pallas_call x1, Pallas kernels, local_parts(): pl.pallas_call(local_kernel, grid=(rows // block,), out_shape=(shape, sha...  8.8 us
    ppermute x2, starting transfers between devices, cell_sum(): value = value + lax.ppermute(value, axis, [(i, i ^ 1 << n) for i in direct])  8.74 us
    ppermute x1, starting transfers between devices, local(): cot_near_rows = lax.ppermute(cotangent, 'ax', near)  4.62 us
    pallas_call x2, Pallas kernels, put_rows(): pl.pallas_call(kernel, out_shape=jax.ShapeDtypeStruct(out.shape, out.dtyp...  4.25 us
    ppermute x1, starting transfers between devices, local(): cot_far_rows = lax.ppermute(cotangent, 'ax', far)  3.82 us
    pallas_call x1, Pallas kernels, wall_and_bins(): pl.pallas_call(wall_kernel, grid=(1,), out_shape=(jax.ShapeDtypeStruct((1...  3 us
  transfers between devices with their start and end apart: 11, of which 7 were waited for; matrix products, arithmetic and copies ran while one was open for 7% of the time, Pallas kernels for 10%

profile of v6, /device:TPU:1, one launch (start us, length us, event | category | flops | bytes accessed | tf_op | source)
XLA Modules:
  0.0 128.5 jit_solution(13610224995410940245)
XLA Ops:
  0.6 0.0 copy-start
  0.6 0.0 copy-start.1
  0.7 0.8 copy-done.1
  1.5 0.7 copy-done.2
  2.2 3.0 %shard_map.112 = (f32[1,1536]{1,0:T(1,128)S(1)}, f32[1,256]{1,0:T(1,128)S(1)}) custom-call(s32[1,1536]{1,0:T(1,128)S(1)} %copy-done.1, f32[1,256]{1,0:T(1,128)S(1)} %bitcast.8, f32[1,384,1536]{2,1,0:T(8,128)} %c_down.1), custom_call_target="tpu_custom_call" | custom-call | tf_op jit(solution)/shard_map/pallas_call | solution.py:71
  5.2 0.0 copy-start.4
  5.2 0.0 copy-start.5
  5.2 0.0 copy-start.6
  5.2 0.1 collective-permute-start.3
  5.3 1.1 collective-permute-done.3
  6.4 4.4 %collective-permute-start.4 = (f32[1,256]{1,0:T(1,128)S(1)}, f32[1,256]{1,0:T(1,128)S(1)}, u32[]{:S(2)}, u32[]{:S(2)}) collective-permute-start(f32[1,256]{1,0:T(1,128)S(1)} %add.29), channel_id=1, source_target_pairs={{1,5},{2,6},{5,1},{6,2},{9,13},{10,14},{13,9},{14,10},{17,21},{18,... | collective-permute-start | bytes 3080 | tf_op jit(solution)/shard_map/ppermute | solution.py:41
  10.8 0.9 collective-permute-done.4
  11.8 4.4 %collective-permute-start.5 = (f32[1,256]{1,0:T(1,128)S(1)}, f32[1,256]{1,0:T(1,128)S(1)}, u32[]{:S(2)}, u32[]{:S(2)}) collective-permute-start(f32[1,256]{1,0:T(1,128)S(1)} %add.30), channel_id=1, source_target_pairs={{1,9},{2,10},{5,13},{6,14},{9,1},{10,2},{13,5},{14,6},{17,25},{18,... | collective-permute-start | bytes 3080 | tf_op jit(solution)/shard_map/ppermute | solution.py:41
  16.1 0.9 collective-permute-done.5
  17.1 1.3 collective-permute-start.6
  18.4 0.8 collective-permute-done.6
  19.2 0.6 collective-permute-start.7
  19.8 3.8 %collective-permute-start = (f32[1,384,1536]{2,1,0:T(8,128)}, f32[1,384,1536]{2,1,0:T(8,128)}, u32[]{:S(2)}, u32[]{:S(2)}) collective-permute-start(f32[1,384,1536]{2,1,0:T(8,128)} %c_down.1), channel_id=1, source_target_pairs={{0,15},{1,2},{2,1},{3,4},{4,3},{5,6},{6,5},{7,8},{8,7},{9,10},{10,... | collective-permute-start | bytes 7077896 | tf_op jit(solution)/shard_map/ppermute | solution.py:203
  23.6 4.6 %collective-permute-start.1 = (f32[1,384,1536]{2,1,0:T(8,128)}, f32[1,384,1536]{2,1,0:T(8,128)}, u32[]{:S(2)}, u32[]{:S(2)}) collective-permute-start(f32[1,384,1536]{2,1,0:T(8,128)} %c_down.1), channel_id=1, source_target_pairs={{0,1},{1,0},{2,3},{3,2},{4,5},{5,4},{6,7},{7,6},{8,9},{9,8},{10,11... | collective-permute-start | bytes 7077896 | tf_op jit(solution)/shard_map/ppermute | solution.py:204
  28.3 0.0 copy-done
  28.3 0.0 collective-permute-start.2
  28.3 0.0 collective-permute-done.7
  28.3 1.3 %collective-permute-start.8 = (f32[1,256]{1,0:T(1,128)S(1)}, f32[1,256]{1,0:T(1,128)S(1)}, u32[]{:S(2)}, u32[]{:S(2)}) collective-permute-start(f32[1,256]{1,0:T(1,128)S(1)} %add.32), channel_id=1, source_target_pairs={{0,1},{3,2},{4,5},{7,6},{8,9},{11,10},{12,13},{15,14},{16,17},{19,... | collective-permute-start | bytes 3080 | tf_op jit(solution)/shard_map/ppermute | solution.py:44
  29.6 2.7 %collective-permute-done.8 = f32[1,256]{1,0:T(1,128)S(1)} collective-permute-done((f32[1,256]{1,0:T(1,128)S(1)}, f32[1,256]{1,0:T(1,128)S(1)}, u32[]{:S(2)}, u32[]{:S(2)}) %collective-permute-start.8) | collective-permute-done | bytes 1056 | tf_op jit(solution)/shard_map/ppermute | solution.py:44
  32.3 1.5 %slice.36 = f32[1,352,1536]{2,1,0:T(8,128)} slice(f32[1,384,1536]{2,1,0:T(8,128)S(1)} %copy-done), slice={[0:1], [0:352], [0:1536]} | slice | bytes 4325376 | tf_op jit(solution)/shard_map/slice | solution.py:216
  33.8 0.0 collective-permute-start.10
  33.8 0.0 copy-done.3
  33.8 0.6 slice.29
  34.4 0.1 slice.31
  35.1 0.6 pad_maximum_fusion
  35.8 0.1 pad_maximum_fusion.1
  35.9 0.1 copy.20.coef
  36.1 0.6 fusion
  37.3 0.6 multiply_add_fusion
  38.0 0.1 stack.32
  39.3 0.7 pad_maximum_fusion.2.scal
  40.1 1.8 %collective-permute-start.9 = (f32[1,32,1536]{2,1,0:T(8,128)S(1)}, f32[1,32,1536]{2,1,0:T(8,128)S(1)}, u32[]{:S(2)}, u32[]{:S(2)}) collective-permute-start(f32[1,32,1536]{2,1,0:T(8,128)S(1)} %slice.35), channel_id=1, source_target_pairs={{0,15},{1,2},{2,1},{3,4},{4,3},{5,6},{6,5},{7,8},{8,7},{9,10},{10,... | collective-permute-start | bytes 589832 | tf_op jit(solution)/shard_map/ppermute | solution.py:216
  41.9 0.6 broadcast_multiply_fusion
  42.5 58.6 %collective-permute-done.c_far = f32[1,384,1536]{2,1,0:T(8,128)} collective-permute-done((f32[1,384,1536]{2,1,0:T(8,128)}, f32[1,384,1536]{2,1,0:T(8,128)}, u32[]{:S(2)}, u32[]{:S(2)}) %collective-permute-start) | collective-permute-done | bytes 2359328 | tf_op jit(solution)/shard_map/ppermute | solution.py:203
  101.1 0.0 collective-permute-done.1.c_near
  101.1 0.0 collective-permute-done.2.q_near
  101.1 8.8 %shard_map.113 = (f32[1,384,1536]{2,1,0:T(8,128)}, f32[1,384,1536]{2,1,0:T(8,128)}) custom-call(f32[2]{0:T(128)S(1)} %pad_maximum_fusion.2.scal, f32[1,384,1536]{2,1,0:T(8,128)S(1)} %copy-done, f32[1,384,1536]{2,1,0:T(8,128)S(1)} %copy-done, f32[1,384,1536]{2,1,0:T(8,128)S(1)} %copy-done, f32[1,384,1536]{2,1,0:T(8,128)} %collective-permute-done.2.q_near, ...), custom_call_target="tpu_custom_call" | custom-call | flops 29491200 | bytes 16515072 | tf_op jit(solution)/shard_map/pallas_call | solution.py:146
  109.9 1.7 %slice.33.base = f32[1,352,1536]{2,1,0:T(8,128)S(1)} slice(f32[1,384,1536]{2,1,0:T(8,128)} %get-tuple-element.24.before), slice={[0:1], [0:352], [0:1536]} | slice | bytes 4325376 | tf_op jit(solution)/shard_map/slice | solution.py:237
  111.6 0.9 slice.34.base
  112.6 11.7 %collective-permute-done.10.far = f32[1,352,1536]{2,1,0:T(8,128)} collective-permute-done((f32[1,352,1536]{2,1,0:T(8,128)}, f32[1,352,1536]{2,1,0:T(8,128)}, u32[]{:S(2)}, u32[]{:S(2)}) %collective-permute-start.10) | collective-permute-done | bytes 2162720 | tf_op jit(solution)/shard_map/ppermute | solution.py:216
  124.2 3.5 %shard_map.114.before = f32[1,384,1536]{2,1,0:T(8,128)} custom-call(f32[1,352,1536]{2,1,0:T(8,128)S(1)} %slice.33.base, f32[1,352,1536]{2,1,0:T(8,128)} %collective-permute-done.10.far, f32[384,2]{1,0:T(8,128)S(1)} %stack.31.weight, f32[1,384,1536]{2,1,0:T(8,128)} %get-tuple-element.24.before), custom_call_target="tpu_custom_call", output_to_operand_aliasing={{}: (3, {})} | custom-call | flops 5406720 | bytes 6488064 | tf_op jit(solution)/shard_map/pallas_call | solution.py:175
  127.7 0.0 collective-permute-done.9.far
  127.7 0.8 shard_map.115
  (19 shorter events, 0.1 us)
Async XLA Ops:
  0.6 27.6 %copy-start = (f32[1,384,1536]{2,1,0:T(8,128)S(1)}, f32[1,384,1536]{2,1,0:T(8,128)}, u32[]{:S(2)}) copy-start(f32[1,384,1536]{2,1,0:T(8,128)} %q_down.1) | copy-start | bytes 7077892
  0.6 0.8 copy-start.1
  1.5 0.7 copy-start.2
  5.2 28.7 %copy-start.3 = (f32[384]{0:T(512)S(1)}, f32[384]{0:T(512)}, u32[]{:S(2)}) copy-start(f32[384]{0:T(512)} %param.15) | copy-start | bytes 4612
  5.2 30.7 %copy-start.4 = (f32[384]{0:T(512)S(1)}, f32[384]{0:T(512)}, u32[]{:S(2)}) copy-start(f32[384]{0:T(512)} %param.14) | copy-start | bytes 4612
  5.2 30.7 %copy-start.5 = (f32[384]{0:T(512)S(1)}, f32[384]{0:T(512)}, u32[]{:S(2)}) copy-start(f32[384]{0:T(512)} %param.16) | copy-start | bytes 4612
  5.2 30.9 %copy-start.6 = (f32[3]{0:T(128)S(1)}, f32[3]{0:T(128)}, u32[]{:S(2)}) copy-start(f32[3]{0:T(128)} %constant.51) | copy-start | bytes 40
  5.2 1.2 collective-permute-start.3
  6.4 5.3 %collective-permute-start.4 = (f32[1,256]{1,0:T(1,128)S(1)}, f32[1,256]{1,0:T(1,128)S(1)}, u32[]{:S(2)}, u32[]{:S(2)}) collective-permute-start(f32[1,256]{1,0:T(1,128)S(1)} %add.29), channel_id=1, source_target_pairs={{1,5},{2,6},{5,1},{6,2},{9,13},{10,14},{13,9},{14,10},{17,21},{18,... | collective-permute-start | bytes 3080 | tf_op jit(solution)/shard_map/ppermute | solution.py:41
  11.8 5.3 %collective-permute-start.5 = (f32[1,256]{1,0:T(1,128)S(1)}, f32[1,256]{1,0:T(1,128)S(1)}, u32[]{:S(2)}, u32[]{:S(2)}) collective-permute-start(f32[1,256]{1,0:T(1,128)S(1)} %add.30), channel_id=1, source_target_pairs={{1,9},{2,10},{5,13},{6,14},{9,1},{10,2},{13,5},{14,6},{17,25},{18,... | collective-permute-start | bytes 3080 | tf_op jit(solution)/shard_map/ppermute | solution.py:41
  17.1 2.1 %collective-permute-start.6 = (f32[1,256]{1,0:T(1,128)S(1)}, f32[1,256]{1,0:T(1,128)S(1)}, u32[]{:S(2)}, u32[]{:S(2)}) collective-permute-start(f32[1,256]{1,0:T(1,128)S(1)} %add.31), channel_id=1, source_target_pairs={{1,0},{2,3},{5,4},{6,7},{9,8},{10,11},{13,12},{14,15},{17,16},{18,... | collective-permute-start | bytes 3080 | tf_op jit(solution)/shard_map/ppermute | solution.py:42
  19.2 9.1 %collective-permute-start.7 = (f32[1,256]{1,0:T(1,128)S(1)}, f32[1,256]{1,0:T(1,128)S(1)}, u32[]{:S(2)}, u32[]{:S(2)}) collective-permute-start(f32[1,256]{1,0:T(1,128)S(1)} %collective-permute-done.6), channel_id=1, source_target_pairs={{0,3},{3,0},{4,7},{7,4},{8,11},{11,8},{12,15},{15,12},{16,19},{19,... | collective-permute-start | bytes 3080 | tf_op jit(solution)/shard_map/ppermute | solution.py:43
  19.8 81.2 %collective-permute-start = (f32[1,384,1536]{2,1,0:T(8,128)}, f32[1,384,1536]{2,1,0:T(8,128)}, u32[]{:S(2)}, u32[]{:S(2)}) collective-permute-start(f32[1,384,1536]{2,1,0:T(8,128)} %c_down.1), channel_id=1, source_target_pairs={{0,15},{1,2},{2,1},{3,4},{4,3},{5,6},{6,5},{7,8},{8,7},{9,10},{10,... | collective-permute-start | bytes 7077896 | tf_op jit(solution)/shard_map/ppermute | solution.py:203
  23.6 77.4 %collective-permute-start.1 = (f32[1,384,1536]{2,1,0:T(8,128)}, f32[1,384,1536]{2,1,0:T(8,128)}, u32[]{:S(2)}, u32[]{:S(2)}) collective-permute-start(f32[1,384,1536]{2,1,0:T(8,128)} %c_down.1), channel_id=1, source_target_pairs={{0,1},{1,0},{2,3},{3,2},{4,5},{5,4},{6,7},{7,6},{8,9},{9,8},{10,11... | collective-permute-start | bytes 7077896 | tf_op jit(solution)/shard_map/ppermute | solution.py:204
  28.3 72.8 %collective-permute-start.2 = (f32[1,384,1536]{2,1,0:T(8,128)S(1)}, f32[1,384,1536]{2,1,0:T(8,128)}, u32[]{:S(2)}, u32[]{:S(2)}) collective-permute-start(f32[1,384,1536]{2,1,0:T(8,128)S(1)} %copy-done), channel_id=1, source_target_pairs={{0,1},{1,0},{2,3},{3,2},{4,5},{5,4},{6,7},{7,6},{8,9},{9,8},{10,11... | collective-permute-start | bytes 7077896 | tf_op jit(solution)/shard_map/ppermute | solution.py:205
  28.3 4.0 %collective-permute-start.8 = (f32[1,256]{1,0:T(1,128)S(1)}, f32[1,256]{1,0:T(1,128)S(1)}, u32[]{:S(2)}, u32[]{:S(2)}) collective-permute-start(f32[1,256]{1,0:T(1,128)S(1)} %add.32), channel_id=1, source_target_pairs={{0,1},{3,2},{4,5},{7,6},{8,9},{11,10},{12,13},{15,14},{16,17},{19,... | collective-permute-start | bytes 3080 | tf_op jit(solution)/shard_map/ppermute | solution.py:44
  33.8 90.4 %collective-permute-start.10 = (f32[1,352,1536]{2,1,0:T(8,128)}, f32[1,352,1536]{2,1,0:T(8,128)}, u32[]{:S(2)}, u32[]{:S(2)}) collective-permute-start(f32[1,352,1536]{2,1,0:T(8,128)} %slice.36), channel_id=1, source_target_pairs={{0,15},{1,2},{2,1},{3,4},{4,3},{5,6},{6,5},{7,8},{8,7},{9,10},{10,... | collective-permute-start | bytes 6488072 | tf_op jit(solution)/shard_map/ppermute | solution.py:216
  40.1 87.6 %collective-permute-start.9 = (f32[1,32,1536]{2,1,0:T(8,128)S(1)}, f32[1,32,1536]{2,1,0:T(8,128)S(1)}, u32[]{:S(2)}, u32[]{:S(2)}) collective-permute-start(f32[1,32,1536]{2,1,0:T(8,128)S(1)} %slice.35), channel_id=1, source_target_pairs={{0,15},{1,2},{2,1},{3,4},{4,3},{5,6},{6,5},{7,8},{8,7},{9,10},{10,... | collective-permute-start | bytes 589832 | tf_op jit(solution)/shard_map/ppermute | solution.py:216

commit v7 on v2

--- a/solution.py
+++ b/solution.py
@@ -191,13 +191,19 @@
 def put_rows(out, base, part, weight, start):
     rows, width = part.shape[1:]
 
-    def kernel(base, far, weight, before, out, fresh, sem):
-        x = far[0]
-        of_row = weight[pl.ds(start, rows), :]
-        fresh[...] = base[0] + x * (of_row[:, 0:1] + of_row[:, 1:2] * x)
-        store = pltpu.make_async_copy(fresh, out.at[0, pl.ds(start, rows)], sem)
-        store.start()
-        store.wait()
+    def kernel(base, far, weight, before, out, fresh, sems):
+        stores = []
+        for n in range(rows // SUB):
+            here = pl.ds(n * SUB, SUB)
+            there = pl.ds(start + n * SUB, SUB)
+            x = far[0, here]
+            of_row = weight[there, :]
+            fresh[here] = base[0, here] + x * (of_row[:, 0:1] + of_row[:, 1:2] * x)
+            store = pltpu.make_async_copy(fresh.at[here], out.at[0, there], sems.at[n])
+            store.start()
+            stores.append(store)
+        for store in stores:
+            store.wait()
 
     anywhere = pl.BlockSpec(memory_space=pl.ANY)
     return pl.pallas_call(
@@ -205,7 +211,10 @@
         out_shape=jax.ShapeDtypeStruct(out.shape, out.dtype),
         in_specs=[pl.BlockSpec(memory_space=pltpu.VMEM)] * 3 + [anywhere],
         out_specs=anywhere,
-        scratch_shapes=[pltpu.VMEM((rows, width), jnp.float32), pltpu.SemaphoreType.DMA],
+        scratch_shapes=[
+            pltpu.VMEM((rows, width), jnp.float32),
+            pltpu.SemaphoreType.DMA((rows // SUB,)),
+        ],
         input_output_aliases={3: 0},
         compiler_params=pltpu.CompilerParams(vmem_limit_bytes=40 << 20),
         cost_estimate=pl.CostEstimate(

time: 107 us -> 107 us (level)
  no operation moved by 1% of the time
where the time goes in v7:
time: 107 us
  waiting for transfers between devices  57.4 us (54%)
  starting transfers between devices  16.6 us (16%)
  Pallas kernels  16.2 us (15%)
  local copies, waits for them, and re-layouts  9.94 us (9%)
  between operations  3.35 us (3%)
  other arithmetic  3.26 us (3%)
    ppermute x1, waiting for transfers between devices, local(): cot_far_rows = lax.ppermute(cotangent, 'ax', far)  35.5 us
    pallas_call x1, Pallas kernels, local_parts(): pl.pallas_call(local_kernel, grid=(rows // block,), out_shape=(shape, sha...  8.21 us
    ppermute x1, waiting for transfers between devices, cell_sum(): lax.ppermute(value, axis, [(i, i ^ 1) for i in turning])  6.74 us
    ppermute x2, waiting for transfers between devices, cell_sum(): value = value + lax.ppermute(value, axis, [(i, i ^ 1 << n) for i in direct])  6.62 us
    ppermute x3, waiting for transfers between devices, local(): lax.ppermute(late[:, low:high], 'ax', far)  5.97 us
    unnamed x18, local copies, waits for them, and re-layouts  4.72 us
    pallas_call x1, Pallas kernels, add_rows(): pl.pallas_call(state_far, grid=(rows // block,), out_shape=jax.ShapeDtype...  4.02 us
    ppermute x2, starting transfers between devices, cell_sum(): value = value + lax.ppermute(value, axis, [(i, i ^ 1 << n) for i in direct])  3.82 us
  transfers between devices with their start and end apart: 12, of which 9 were waited for; matrix products, arithmetic and copies ran while one was open for 8% of the time, Pallas kernels for 14%

profile of v7, /device:TPU:1, one launch (start us, length us, event | category | flops | bytes accessed | tf_op | source)
XLA Modules:
  0.0 106.7 jit_solution(1222725745736222939)
XLA Ops:
  0.6 0.0 copy-start
  0.6 2.7 %collective-permute-start = (f32[1,384,1536]{2,1,0:T(8,128)}, f32[1,384,1536]{2,1,0:T(8,128)}, u32[]{:S(2)}, u32[]{:S(2)}) collective-permute-start(f32[1,384,1536]{2,1,0:T(8,128)} %c_down.1), channel_id=1, source_target_pairs={{0,15},{1,2},{2,1},{3,4},{4,3},{5,6},{6,5},{7,8},{8,7},{9,10},{10,... | collective-permute-start | bytes 7077896 | tf_op jit(solution)/shard_map/ppermute | solution.py:240
  3.3 2.9 %collective-permute-start.1 = (f32[1,384,1536]{2,1,0:T(8,128)}, f32[1,384,1536]{2,1,0:T(8,128)}, u32[]{:S(2)}, u32[]{:S(2)}) collective-permute-start(f32[1,384,1536]{2,1,0:T(8,128)} %c_down.1), channel_id=1, source_target_pairs={{0,1},{1,0},{2,3},{3,2},{4,5},{5,4},{6,7},{7,6},{8,9},{9,8},{10,11... | collective-permute-start | bytes 7077896 | tf_op jit(solution)/shard_map/ppermute | solution.py:241
  6.2 0.0 collective-permute-start.2
  6.2 1.7 %copy-done.1 = f32[1,384,1536]{2,1,0:T(8,128)S(1)} copy-done((f32[1,384,1536]{2,1,0:T(8,128)S(1)}, f32[1,384,1536]{2,1,0:T(8,128)}, u32[]{:S(2)}) %copy-start.1) | copy-done | bytes 2359320
  7.9 0.7 copy-done.3
  8.5 0.7 copy-done.4
  9.2 2.2 %shard_map.112 = (f32[1,1536]{1,0:T(1,128)S(1)}, f32[1,256]{1,0:T(1,128)S(1)}) custom-call(s32[1,1536]{1,0:T(1,128)S(1)} %copy-done.3, f32[1,256]{1,0:T(1,128)S(1)} %bitcast.8, f32[1,384,1536]{2,1,0:T(8,128)S(1)} %copy-done.1), custom_call_target="tpu_custom_call" | custom-call | tf_op jit(solution)/shard_map/pallas_call | solution.py:72
  11.4 0.5 collective-permute-start.3
  12.0 1.8 %collective-permute-done.3 = f32[1,256]{1,0:T(1,128)S(1)} collective-permute-done((f32[1,256]{1,0:T(1,128)S(1)}, f32[1,256]{1,0:T(1,128)S(1)}, u32[]{:S(2)}, u32[]{:S(2)}) %collective-permute-start.3) | collective-permute-done | bytes 1056 | tf_op jit(solution)/shard_map/ppermute | solution.py:40
  13.7 1.9 %collective-permute-start.4 = (f32[1,256]{1,0:T(1,128)S(1)}, f32[1,256]{1,0:T(1,128)S(1)}, u32[]{:S(2)}, u32[]{:S(2)}) collective-permute-start(f32[1,256]{1,0:T(1,128)S(1)} %add.29), channel_id=1, source_target_pairs={{1,5},{2,6},{5,1},{6,2},{9,13},{10,14},{13,9},{14,10},{17,21},{18,... | collective-permute-start | bytes 3080 | tf_op jit(solution)/shard_map/ppermute | solution.py:42
  15.6 2.9 %collective-permute-done.4 = f32[1,256]{1,0:T(1,128)S(1)} collective-permute-done((f32[1,256]{1,0:T(1,128)S(1)}, f32[1,256]{1,0:T(1,128)S(1)}, u32[]{:S(2)}, u32[]{:S(2)}) %collective-permute-start.4) | collective-permute-done | bytes 1056 | tf_op jit(solution)/shard_map/ppermute | solution.py:42
  18.5 1.9 %collective-permute-start.5 = (f32[1,256]{1,0:T(1,128)S(1)}, f32[1,256]{1,0:T(1,128)S(1)}, u32[]{:S(2)}, u32[]{:S(2)}) collective-permute-start(f32[1,256]{1,0:T(1,128)S(1)} %add.30), channel_id=1, source_target_pairs={{1,9},{2,10},{5,13},{6,14},{9,1},{10,2},{13,5},{14,6},{17,25},{18,... | collective-permute-start | bytes 3080 | tf_op jit(solution)/shard_map/ppermute | solution.py:42
  20.4 3.8 %collective-permute-done.5 = f32[1,256]{1,0:T(1,128)S(1)} collective-permute-done((f32[1,256]{1,0:T(1,128)S(1)}, f32[1,256]{1,0:T(1,128)S(1)}, u32[]{:S(2)}, u32[]{:S(2)}) %collective-permute-start.5) | collective-permute-done | bytes 1056 | tf_op jit(solution)/shard_map/ppermute | solution.py:42
  24.2 1.3 %collective-permute-start.6 = (f32[1,256]{1,0:T(1,128)S(1)}, f32[1,256]{1,0:T(1,128)S(1)}, u32[]{:S(2)}, u32[]{:S(2)}) collective-permute-start(f32[1,256]{1,0:T(1,128)S(1)} %add.31), channel_id=1, source_target_pairs={{1,0},{2,3},{5,4},{6,7},{9,8},{10,11},{13,12},{14,15},{17,16},{18,... | collective-permute-start | bytes 3080 | tf_op jit(solution)/shard_map/ppermute | solution.py:43
  25.5 0.8 collective-permute-done.6
  26.3 0.6 collective-permute-start.7
  26.9 0.0 collective-permute-done.7
  27.0 1.3 %collective-permute-start.8 = (f32[1,256]{1,0:T(1,128)S(1)}, f32[1,256]{1,0:T(1,128)S(1)}, u32[]{:S(2)}, u32[]{:S(2)}) collective-permute-start(f32[1,256]{1,0:T(1,128)S(1)} %add.32), channel_id=1, source_target_pairs={{0,1},{3,2},{4,5},{7,6},{8,9},{11,10},{12,13},{15,14},{16,17},{19,... | collective-permute-start | bytes 3080 | tf_op jit(solution)/shard_map/ppermute | solution.py:45
  28.3 6.7 %collective-permute-done.8 = f32[1,256]{1,0:T(1,128)S(1)} collective-permute-done((f32[1,256]{1,0:T(1,128)S(1)}, f32[1,256]{1,0:T(1,128)S(1)}, u32[]{:S(2)}, u32[]{:S(2)}) %collective-permute-start.8) | collective-permute-done | bytes 1056 | tf_op jit(solution)/shard_map/ppermute | solution.py:45
  35.0 1.4 %slice.40 = f32[1,264,1536]{2,1,0:T(8,128)} slice(f32[1,384,1536]{2,1,0:T(8,128)S(1)} %copy-done), slice={[0:1], [0:264], [0:1536]} | slice | bytes 3244032 | tf_op jit(solution)/shard_map/slice | solution.py:253
  36.4 0.0 collective-permute-start.11
  36.4 0.6 slice.32
  37.0 0.1 slice.34
  37.7 0.6 pad_maximum_fusion
  38.3 0.1 pad_maximum_fusion.1
  38.5 0.1 copy.21.coef
  38.6 0.6 fusion
  39.9 0.9 slice.39
  40.8 1.7 %collective-permute-start.10 = (f32[1,88,1536]{2,1,0:T(8,128)}, f32[1,88,1536]{2,1,0:T(8,128)S(1)}, u32[]{:S(2)}, u32[]{:S(2)}) collective-permute-start(f32[1,88,1536]{2,1,0:T(8,128)} %slice.39), channel_id=1, source_target_pairs={{0,15},{1,2},{2,1},{3,4},{4,3},{5,6},{6,5},{7,8},{8,7},{9,10},{10,... | collective-permute-start | bytes 1622024 | tf_op jit(solution)/shard_map/ppermute | solution.py:253
  42.5 0.6 multiply_add_fusion
  43.2 0.1 stack.32
  44.5 0.7 pad_maximum_fusion.2.scal
  45.3 35.5 %collective-permute-done.c_far = f32[1,384,1536]{2,1,0:T(8,128)} collective-permute-done((f32[1,384,1536]{2,1,0:T(8,128)}, f32[1,384,1536]{2,1,0:T(8,128)}, u32[]{:S(2)}, u32[]{:S(2)}) %collective-permute-start) | collective-permute-done | bytes 2359328 | tf_op jit(solution)/shard_map/ppermute | solution.py:240
  80.7 1.7 %collective-permute-start.9 = (f32[1,32,1536]{2,1,0:T(8,128)S(1)}, f32[1,32,1536]{2,1,0:T(8,128)S(1)}, u32[]{:S(2)}, u32[]{:S(2)}) collective-permute-start(f32[1,32,1536]{2,1,0:T(8,128)S(1)} %slice.38), channel_id=1, source_target_pairs={{0,15},{1,2},{2,1},{3,4},{4,3},{5,6},{6,5},{7,8},{8,7},{9,10},{10,... | collective-permute-start | bytes 589832 | tf_op jit(solution)/shard_map/ppermute | solution.py:253
  82.5 0.6 broadcast_multiply_fusion
  83.0 0.0 collective-permute-done.1.c_near
  83.0 0.0 collective-permute-done.2.q_near
  83.0 1.7 %copy-done.2 = f32[1,384,1536]{2,1,0:T(8,128)S(1)} copy-done((f32[1,384,1536]{2,1,0:T(8,128)S(1)}, f32[1,384,1536]{2,1,0:T(8,128)}, u32[]{:S(2)}) %copy-start.2) | copy-done | bytes 2359320
  84.7 8.2 %shard_map.113 = (f32[1,384,1536]{2,1,0:T(8,128)}, f32[1,384,1536]{2,1,0:T(8,128)}) custom-call(f32[2]{0:T(128)S(1)} %pad_maximum_fusion.2.scal, f32[1,384,1536]{2,1,0:T(8,128)S(1)} %copy-done, f32[1,384,1536]{2,1,0:T(8,128)S(1)} %copy-done, f32[1,384,1536]{2,1,0:T(8,128)S(1)} %copy-done, f32[1,384,1536]{2,1,0:T(8,128)} %collective-permute-done.2.q_near, ...), custom_call_target="tpu_custom_call" | custom-call | flops 29491200 | bytes 16515072 | tf_op jit(solution)/shard_map/pallas_call | solution.py:147
  92.9 1.1 %slice.36.base = f32[1,88,1536]{2,1,0:T(8,128)S(1)} slice(f32[1,384,1536]{2,1,0:T(8,128)} %get-tuple-element.24.base), slice={[0:1], [264:352], [0:1536]} | slice | bytes 1081344 | tf_op jit(solution)/shard_map/slice | solution.py:274
  94.0 0.9 slice.37.base
  94.9 3.2 %collective-permute-done.11.far = f32[1,264,1536]{2,1,0:T(8,128)} collective-permute-done((f32[1,264,1536]{2,1,0:T(8,128)}, f32[1,264,1536]{2,1,0:T(8,128)}, u32[]{:S(2)}, u32[]{:S(2)}) %collective-permute-start.11) | collective-permute-done | bytes 1622048 | tf_op jit(solution)/shard_map/ppermute | solution.py:253
  98.1 4.0 %shard_map.114.before = f32[1,384,1536]{2,1,0:T(8,128)} custom-call(f32[1,384,1536]{2,1,0:T(8,128)} %get-tuple-element.24.base, f32[1,264,1536]{2,1,0:T(8,128)} %collective-permute-done.11.far, f32[384,2]{1,0:T(8,128)S(1)} %stack.31.weight), custom_call_target="tpu_custom_call", output_to_operand_aliasing={{}: (0, {})} | custom-call | flops 4055040 | bytes 4866048 | tf_op jit(solution)/shard_map/pallas_call | solution.py:177
  102.1 1.7 %collective-permute-done.10.far = f32[1,88,1536]{2,1,0:T(8,128)S(1)} collective-permute-done((f32[1,88,1536]{2,1,0:T(8,128)}, f32[1,88,1536]{2,1,0:T(8,128)S(1)}, u32[]{:S(2)}, u32[]{:S(2)}) %collective-permute-start.10) | collective-permute-done | bytes 540704 | tf_op jit(solution)/shard_map/ppermute | solution.py:253
  103.8 1.0 shard_map.115.before
  104.8 1.1 %collective-permute-done.9.far = f32[1,32,1536]{2,1,0:T(8,128)S(1)} collective-permute-done((f32[1,32,1536]{2,1,0:T(8,128)S(1)}, f32[1,32,1536]{2,1,0:T(8,128)S(1)}, u32[]{:S(2)}, u32[]{:S(2)}) %collective-permute-start.9) | collective-permute-done | bytes 196640 | tf_op jit(solution)/shard_map/ppermute | solution.py:253
  105.9 0.8 shard_map.116
  (27 shorter events, 0.1 us)
Async XLA Ops:
  0.6 34.4 %copy-start = (f32[1,384,1536]{2,1,0:T(8,128)S(1)}, f32[1,384,1536]{2,1,0:T(8,128)}, u32[]{:S(2)}) copy-start(f32[1,384,1536]{2,1,0:T(8,128)} %q_down.1) | copy-start | bytes 7077892
  0.6 80.1 %collective-permute-start = (f32[1,384,1536]{2,1,0:T(8,128)}, f32[1,384,1536]{2,1,0:T(8,128)}, u32[]{:S(2)}, u32[]{:S(2)}) collective-permute-start(f32[1,384,1536]{2,1,0:T(8,128)} %c_down.1), channel_id=1, source_target_pairs={{0,15},{1,2},{2,1},{3,4},{4,3},{5,6},{6,5},{7,8},{8,7},{9,10},{10,... | collective-permute-start | bytes 7077896 | tf_op jit(solution)/shard_map/ppermute | solution.py:240
  3.3 79.7 %collective-permute-start.1 = (f32[1,384,1536]{2,1,0:T(8,128)}, f32[1,384,1536]{2,1,0:T(8,128)}, u32[]{:S(2)}, u32[]{:S(2)}) collective-permute-start(f32[1,384,1536]{2,1,0:T(8,128)} %c_down.1), channel_id=1, source_target_pairs={{0,1},{1,0},{2,3},{3,2},{4,5},{5,4},{6,7},{7,6},{8,9},{9,8},{10,11... | collective-permute-start | bytes 7077896 | tf_op jit(solution)/shard_map/ppermute | solution.py:241
  6.2 76.9 %collective-permute-start.2 = (f32[1,384,1536]{2,1,0:T(8,128)}, f32[1,384,1536]{2,1,0:T(8,128)}, u32[]{:S(2)}, u32[]{:S(2)}) collective-permute-start(f32[1,384,1536]{2,1,0:T(8,128)} %q_down.1), channel_id=1, source_target_pairs={{0,1},{1,0},{2,3},{3,2},{4,5},{5,4},{6,7},{7,6},{8,9},{9,8},{10,11... | collective-permute-start | bytes 7077896 | tf_op jit(solution)/shard_map/ppermute | solution.py:242
  6.2 1.7 %copy-start.1 = (f32[1,384,1536]{2,1,0:T(8,128)S(1)}, f32[1,384,1536]{2,1,0:T(8,128)}, u32[]{:S(2)}) copy-start(f32[1,384,1536]{2,1,0:T(8,128)} %c_down.1) | copy-start | bytes 7077892
  7.9 0.7 copy-start.3
  8.5 0.7 copy-start.4
  9.2 27.2 %copy-start.5 = (f32[384]{0:T(512)S(1)}, f32[384]{0:T(512)}, u32[]{:S(2)}) copy-start(f32[384]{0:T(512)} %param.15) | copy-start | bytes 4612
  9.2 29.2 %copy-start.6 = (f32[384]{0:T(512)S(1)}, f32[384]{0:T(512)}, u32[]{:S(2)}) copy-start(f32[384]{0:T(512)} %param.14) | copy-start | bytes 4612
  9.2 29.2 %copy-start.7 = (f32[384]{0:T(512)S(1)}, f32[384]{0:T(512)}, u32[]{:S(2)}) copy-start(f32[384]{0:T(512)} %param.16) | copy-start | bytes 4612
  11.4 27.2 %copy-start.8 = (f32[3]{0:T(128)S(1)}, f32[3]{0:T(128)}, u32[]{:S(2)}) copy-start(f32[3]{0:T(128)} %constant.51) | copy-start | bytes 40
  11.4 2.3 %collective-permute-start.3 = (f32[1,256]{1,0:T(1,128)S(1)}, f32[1,256]{1,0:T(1,128)S(1)}, u32[]{:S(2)}, u32[]{:S(2)}) collective-permute-start(f32[1,256]{1,0:T(1,128)S(1)} %get-tuple-element.21), channel_id=1, source_target_pairs={{0,1},{1,0},{2,3},{3,2},{4,5},{5,4},{6,7},{7,6},{8,9},{9,8},{10,11... | collective-permute-start | bytes 3080 | tf_op jit(solution)/shard_map/ppermute | solution.py:40
  13.7 4.8 %collective-permute-start.4 = (f32[1,256]{1,0:T(1,128)S(1)}, f32[1,256]{1,0:T(1,128)S(1)}, u32[]{:S(2)}, u32[]{:S(2)}) collective-permute-start(f32[1,256]{1,0:T(1,128)S(1)} %add.29), channel_id=1, source_target_pairs={{1,5},{2,6},{5,1},{6,2},{9,13},{10,14},{13,9},{14,10},{17,21},{18,... | collective-permute-start | bytes 3080 | tf_op jit(solution)/shard_map/ppermute | solution.py:42
  18.5 5.7 %collective-permute-start.5 = (f32[1,256]{1,0:T(1,128)S(1)}, f32[1,256]{1,0:T(1,128)S(1)}, u32[]{:S(2)}, u32[]{:S(2)}) collective-permute-start(f32[1,256]{1,0:T(1,128)S(1)} %add.30), channel_id=1, source_target_pairs={{1,9},{2,10},{5,13},{6,14},{9,1},{10,2},{13,5},{14,6},{17,25},{18,... | collective-permute-start | bytes 3080 | tf_op jit(solution)/shard_map/ppermute | solution.py:42
  24.2 2.1 %collective-permute-start.6 = (f32[1,256]{1,0:T(1,128)S(1)}, f32[1,256]{1,0:T(1,128)S(1)}, u32[]{:S(2)}, u32[]{:S(2)}) collective-permute-start(f32[1,256]{1,0:T(1,128)S(1)} %add.31), channel_id=1, source_target_pairs={{1,0},{2,3},{5,4},{6,7},{9,8},{10,11},{13,12},{14,15},{17,16},{18,... | collective-permute-start | bytes 3080 | tf_op jit(solution)/shard_map/ppermute | solution.py:43
  26.3 0.7 collective-permute-start.7
  27.0 8.1 %collective-permute-start.8 = (f32[1,256]{1,0:T(1,128)S(1)}, f32[1,256]{1,0:T(1,128)S(1)}, u32[]{:S(2)}, u32[]{:S(2)}) collective-permute-start(f32[1,256]{1,0:T(1,128)S(1)} %add.32), channel_id=1, source_target_pairs={{0,1},{3,2},{4,5},{7,6},{8,9},{11,10},{12,13},{15,14},{16,17},{19,... | collective-permute-start | bytes 3080 | tf_op jit(solution)/shard_map/ppermute | solution.py:45
  36.4 61.7 %collective-permute-start.11 = (f32[1,264,1536]{2,1,0:T(8,128)}, f32[1,264,1536]{2,1,0:T(8,128)}, u32[]{:S(2)}, u32[]{:S(2)}) collective-permute-start(f32[1,264,1536]{2,1,0:T(8,128)} %slice.40), channel_id=1, source_target_pairs={{0,15},{1,2},{2,1},{3,4},{4,3},{5,6},{6,5},{7,8},{8,7},{9,10},{10,... | collective-permute-start | bytes 4866056 | tf_op jit(solution)/shard_map/ppermute | solution.py:253
  40.8 63.0 %collective-permute-start.10 = (f32[1,88,1536]{2,1,0:T(8,128)}, f32[1,88,1536]{2,1,0:T(8,128)S(1)}, u32[]{:S(2)}, u32[]{:S(2)}) collective-permute-start(f32[1,88,1536]{2,1,0:T(8,128)} %slice.39), channel_id=1, source_target_pairs={{0,15},{1,2},{2,1},{3,4},{4,3},{5,6},{6,5},{7,8},{8,7},{9,10},{10,... | collective-permute-start | bytes 1622024 | tf_op jit(solution)/shard_map/ppermute | solution.py:253
  80.7 25.2 %collective-permute-start.9 = (f32[1,32,1536]{2,1,0:T(8,128)S(1)}, f32[1,32,1536]{2,1,0:T(8,128)S(1)}, u32[]{:S(2)}, u32[]{:S(2)}) collective-permute-start(f32[1,32,1536]{2,1,0:T(8,128)S(1)} %slice.38), channel_id=1, source_target_pairs={{0,15},{1,2},{2,1},{3,4},{4,3},{5,6},{6,5},{7,8},{8,7},{9,10},{10,... | collective-permute-start | bytes 589832 | tf_op jit(solution)/shard_map/ppermute | solution.py:253
  83.0 1.7 %copy-start.2 = (f32[1,384,1536]{2,1,0:T(8,128)S(1)}, f32[1,384,1536]{2,1,0:T(8,128)}, u32[]{:S(2)}) copy-start(f32[1,384,1536]{2,1,0:T(8,128)} %c_down.1) | copy-start | bytes 7077892

commit v8 on v2

--- a/solution.py
+++ b/solution.py
@@ -238,7 +238,7 @@
     else:
         binned = cell_sum(binned, "ax")
 
-    late, binned = lax.optimization_barrier((checkpoint, binned))
+    late, cot_near_rows = lax.optimization_barrier((checkpoint, cot_near_rows))
     edges = [rows * n // STATE_PARTS for n in STATE_CUTS]
     state_far_rows = [
         lax.ppermute(late[:, low:high], "ax", far) for low, high in zip(edges, edges[1:])

time: 107 us -> 107 us (level)
  waiting for transfers between devices: 57.3 us -> 51.8 us
  local copies, waits for them, and re-layouts: 9.94 us -> 12.9 us
  starting transfers between devices: 16.6 us -> 19.5 us
    ppermute x1, waiting for transfers between devices: 6.74 us -> 20.9 us  [cell_sum(): lax.ppermute(value, axis, [(i, i ^ 1) for i in turning])]
    ppermute x1, waiting for transfers between devices: 35.5 us -> 21.4 us  [local(): cot_far_rows = lax.ppermute(cotangent, 'ax', far)]
    ppermute x2, waiting for transfers between devices: 6.62 us -> 1.71 us  [cell_sum(): value = value + lax.ppermute(value, axis, [(i, i ^ 1 << n) for i in direct])]
    ppermute x1, starting transfers between devices: 0.01 us -> 3.47 us  [local(): state_near_rows = lax.ppermute(checkpoint, 'ax', near)]
    ppermute x1, starting transfers between devices: 2.87 us -> 0.12 us  [local(): cot_near_rows = lax.ppermute(cotangent, 'ax', near)]
    ppermute x1, starting transfers between devices: 0.52 us -> 3.19 us  [cell_sum(): lax.ppermute(value, axis, [(i, i ^ 1) for i in range(count)])]
    ppermute x1, waiting for transfers between devices: 1.76 us -> 0.01 us  [cell_sum(): lax.ppermute(value, axis, [(i, i ^ 1) for i in range(count)])]
    unnamed x18 -> x22, local copies, waits for them, and re-layouts: 4.72 us -> 6.13 us
  transfers between devices with their start and end apart: 12 -> 12, of which waited for: 9 -> 8; matrix products, arithmetic and copies ran while one was open for 8% -> 9% of each run, Pallas kernels for 14% -> 14%
where the time goes in v8:
time: 107 us
  waiting for transfers between devices  51.8 us (48%)
  starting transfers between devices  19.5 us (18%)
  Pallas kernels  15.8 us (15%)
  local copies, waits for them, and re-layouts  12.9 us (12%)
  between operations  3.54 us (3%)
  other arithmetic  3.39 us (3%)
    ppermute x1, waiting for transfers between devices, local(): cot_far_rows = lax.ppermute(cotangent, 'ax', far)  21.4 us
    ppermute x1, waiting for transfers between devices, cell_sum(): lax.ppermute(value, axis, [(i, i ^ 1) for i in turning])  20.9 us
    pallas_call x1, Pallas kernels, local_parts(): pl.pallas_call(local_kernel, grid=(rows // block,), out_shape=(shape, sha...  7.77 us
    ppermute x3, waiting for transfers between devices, local(): lax.ppermute(late[:, low:high], 'ax', far)  7.02 us
    unnamed x22, local copies, waits for them, and re-layouts  6.13 us
    pallas_call x1, Pallas kernels, add_rows(): pl.pallas_call(state_far, grid=(rows // block,), out_shape=jax.ShapeDtype...  4.02 us
    ppermute x2, starting transfers between devices, cell_sum(): value = value + lax.ppermute(value, axis, [(i, i ^ 1 << n) for i in direct])  3.83 us
    slice x3, local copies, waits for them, and re-layouts, local(): late[:, low:high]  3.65 us
  transfers between devices with their start and end apart: 12, of which 8 were waited for; matrix products, arithmetic and copies ran while one was open for 9% of the time, Pallas kernels for 14%

profile of v8, /device:TPU:1, one launch (start us, length us, event | category | flops | bytes accessed | tf_op | source)
XLA Modules:
  0.0 106.8 jit_solution(3706307947852085350)
XLA Ops:
  0.6 0.0 copy-start.10
  0.6 0.0 copy-start.1
  0.7 0.1 collective-permute-start.1
  0.8 2.6 %collective-permute-start = (f32[1,384,1536]{2,1,0:T(8,128)}, f32[1,384,1536]{2,1,0:T(8,128)}, u32[]{:S(2)}, u32[]{:S(2)}) collective-permute-start(f32[1,384,1536]{2,1,0:T(8,128)} %c_down.1), channel_id=1, source_target_pairs={{0,15},{1,2},{2,1},{3,4},{4,3},{5,6},{6,5},{7,8},{8,7},{9,10},{10,... | collective-permute-start | bytes 7077896 | tf_op jit(solution)/shard_map/ppermute | solution.py:231
  3.4 3.5 %collective-permute-start.2 = (f32[1,384,1536]{2,1,0:T(8,128)}, f32[1,384,1536]{2,1,0:T(8,128)}, u32[]{:S(2)}, u32[]{:S(2)}) collective-permute-start(f32[1,384,1536]{2,1,0:T(8,128)} %q_down.1), channel_id=1, source_target_pairs={{0,1},{1,0},{2,3},{3,2},{4,5},{5,4},{6,7},{7,6},{8,9},{9,8},{10,11... | collective-permute-start | bytes 7077896 | tf_op jit(solution)/shard_map/ppermute | solution.py:233
  6.9 0.0 collective-permute-done.1.c_near
  6.9 1.4 %copy-done.3 = f32[1,384,1536]{2,1,0:T(8,128)} copy-done((f32[1,384,1536]{2,1,0:T(8,128)}, f32[1,384,1536]{2,1,0:T(8,128)S(1)}, u32[]{:S(2)}) %copy-start.3) | copy-done | bytes 2359320
  8.3 2.7 %slice.40 = f32[1,264,1536]{2,1,0:T(8,128)} slice(f32[1,384,1536]{2,1,0:T(8,128)} %q_down.1), slice={[0:1], [0:264], [0:1536]} | slice | bytes 3244032 | tf_op jit(solution)/shard_map/slice | solution.py:244
  11.0 1.2 %collective-permute-start.5 = (f32[1,264,1536]{2,1,0:T(8,128)}, f32[1,264,1536]{2,1,0:T(8,128)}, u32[]{:S(2)}, u32[]{:S(2)}) collective-permute-start(f32[1,264,1536]{2,1,0:T(8,128)} %slice.40), channel_id=1, source_target_pairs={{0,15},{1,2},{2,1},{3,4},{4,3},{5,6},{6,5},{7,8},{8,7},{9,10},{10,... | collective-permute-start | bytes 4866056 | tf_op jit(solution)/shard_map/ppermute | solution.py:244
  12.2 0.7 copy-done.5
  12.9 0.7 copy-done.6
  13.6 2.2 %shard_map.112 = (f32[1,1536]{1,0:T(1,128)S(1)}, f32[1,256]{1,0:T(1,128)S(1)}) custom-call(s32[1,1536]{1,0:T(1,128)S(1)} %copy-done.5, f32[1,256]{1,0:T(1,128)S(1)} %bitcast.8, f32[1,384,1536]{2,1,0:T(8,128)S(1)} %copy-done.1), custom_call_target="tpu_custom_call" | custom-call | tf_op jit(solution)/shard_map/pallas_call | solution.py:72
  15.8 3.2 %collective-permute-start.6 = (f32[1,256]{1,0:T(1,128)S(1)}, f32[1,256]{1,0:T(1,128)S(1)}, u32[]{:S(2)}, u32[]{:S(2)}) collective-permute-start(f32[1,256]{1,0:T(1,128)S(1)} %get-tuple-element.26), channel_id=1, source_target_pairs={{0,1},{1,0},{2,3},{3,2},{4,5},{5,4},{6,7},{7,6},{8,9},{9,8},{10,11... | collective-permute-start | bytes 3080 | tf_op jit(solution)/shard_map/ppermute | solution.py:40
  19.7 0.6 fusion.1
  20.9 0.0 collective-permute-done.6
  20.9 1.9 %collective-permute-start.7 = (f32[1,256]{1,0:T(1,128)S(1)}, f32[1,256]{1,0:T(1,128)S(1)}, u32[]{:S(2)}, u32[]{:S(2)}) collective-permute-start(f32[1,256]{1,0:T(1,128)S(1)} %add.31), channel_id=1, source_target_pairs={{1,5},{2,6},{5,1},{6,2},{9,13},{10,14},{13,9},{14,10},{17,21},{18,... | collective-permute-start | bytes 3080 | tf_op jit(solution)/shard_map/ppermute | solution.py:42
  22.9 0.7 multiply_add_fusion
  23.5 0.7 slice.32
  24.2 1.5 %collective-permute-done.7 = f32[1,256]{1,0:T(1,128)S(1)} collective-permute-done((f32[1,256]{1,0:T(1,128)S(1)}, f32[1,256]{1,0:T(1,128)S(1)}, u32[]{:S(2)}, u32[]{:S(2)}) %collective-permute-start.7) | collective-permute-done | bytes 1056 | tf_op jit(solution)/shard_map/ppermute | solution.py:42
  25.7 1.9 %collective-permute-start.8 = (f32[1,256]{1,0:T(1,128)S(1)}, f32[1,256]{1,0:T(1,128)S(1)}, u32[]{:S(2)}, u32[]{:S(2)}) collective-permute-start(f32[1,256]{1,0:T(1,128)S(1)} %add.32), channel_id=1, source_target_pairs={{1,9},{2,10},{5,13},{6,14},{9,1},{10,2},{13,5},{14,6},{17,25},{18,... | collective-permute-start | bytes 3080 | tf_op jit(solution)/shard_map/ppermute | solution.py:42
  27.6 0.9 slice.39
  28.5 1.8 %collective-permute-start.4 = (f32[1,88,1536]{2,1,0:T(8,128)}, f32[1,88,1536]{2,1,0:T(8,128)S(1)}, u32[]{:S(2)}, u32[]{:S(2)}) collective-permute-start(f32[1,88,1536]{2,1,0:T(8,128)} %slice.39), channel_id=1, source_target_pairs={{0,15},{1,2},{2,1},{3,4},{4,3},{5,6},{6,5},{7,8},{8,7},{9,10},{10,... | collective-permute-start | bytes 1622024 | tf_op jit(solution)/shard_map/ppermute | solution.py:244
  30.4 0.8 pad_maximum_fusion
  31.1 0.1 slice.34
  31.2 0.2 collective-permute-done.8
  31.4 1.3 %collective-permute-start.9 = (f32[1,256]{1,0:T(1,128)S(1)}, f32[1,256]{1,0:T(1,128)S(1)}, u32[]{:S(2)}, u32[]{:S(2)}) collective-permute-start(f32[1,256]{1,0:T(1,128)S(1)} %add.33), channel_id=1, source_target_pairs={{1,0},{2,3},{5,4},{6,7},{9,8},{10,11},{13,12},{14,15},{17,16},{18,... | collective-permute-start | bytes 3080 | tf_op jit(solution)/shard_map/ppermute | solution.py:43
  32.7 0.1 pad_maximum_fusion.1
  32.8 0.7 collective-permute-done.9
  33.5 0.6 collective-permute-start.10
  34.1 0.7 pad_maximum_fusion.2.scal
  34.9 1.3 %collective-permute-start.11 = (f32[1,256]{1,0:T(1,128)S(1)}, f32[1,256]{1,0:T(1,128)S(1)}, u32[]{:S(2)}, u32[]{:S(2)}) collective-permute-start(f32[1,256]{1,0:T(1,128)S(1)} %add.34), channel_id=1, source_target_pairs={{0,1},{3,2},{4,5},{7,6},{8,9},{11,10},{12,13},{15,14},{16,17},{19,... | collective-permute-start | bytes 3080 | tf_op jit(solution)/shard_map/ppermute | solution.py:45
  36.3 0.1 copy.21.coef
  36.4 0.1 stack.32
  38.0 20.9 %collective-permute-done.11 = f32[1,256]{1,0:T(1,128)S(1)} collective-permute-done((f32[1,256]{1,0:T(1,128)S(1)}, f32[1,256]{1,0:T(1,128)S(1)}, u32[]{:S(2)}, u32[]{:S(2)}) %collective-permute-start.11) | collective-permute-done | bytes 1056 | tf_op jit(solution)/shard_map/ppermute | solution.py:45
  58.9 0.0 collective-permute-start.3
  58.9 0.6 fusion
  59.5 21.4 %collective-permute-done.c_far = f32[1,384,1536]{2,1,0:T(8,128)} collective-permute-done((f32[1,384,1536]{2,1,0:T(8,128)}, f32[1,384,1536]{2,1,0:T(8,128)}, u32[]{:S(2)}, u32[]{:S(2)}) %collective-permute-start) | collective-permute-done | bytes 2359328 | tf_op jit(solution)/shard_map/ppermute | solution.py:231
  80.8 1.7 %copy-done.2 = f32[1,384,1536]{2,1,0:T(8,128)S(1)} copy-done((f32[1,384,1536]{2,1,0:T(8,128)S(1)}, f32[1,384,1536]{2,1,0:T(8,128)}, u32[]{:S(2)}) %copy-start.2) | copy-done | bytes 2359320
  82.5 1.7 %copy-done.4 = f32[1,384,1536]{2,1,0:T(8,128)S(1)} copy-done((f32[1,384,1536]{2,1,0:T(8,128)S(1)}, f32[1,384,1536]{2,1,0:T(8,128)}, u32[]{:S(2)}) %copy-start.4) | copy-done | bytes 2359320
  84.2 7.8 %shard_map.113 = (f32[1,384,1536]{2,1,0:T(8,128)}, f32[1,384,1536]{2,1,0:T(8,128)}) custom-call(f32[2]{0:T(128)S(1)} %pad_maximum_fusion.2.scal, f32[1,384,1536]{2,1,0:T(8,128)S(1)} %copy-done, f32[1,384,1536]{2,1,0:T(8,128)S(1)} %copy-done, f32[1,384,1536]{2,1,0:T(8,128)S(1)} %copy-done, f32[1,384,1536]{2,1,0:T(8,128)} %collective-permute-done.2.q_near, ...), custom_call_target="tpu_custom_call" | custom-call | flops 29491200 | bytes 16515072 | tf_op jit(solution)/shard_map/pallas_call | solution.py:147
  91.9 1.1 %slice.36.base = f32[1,88,1536]{2,1,0:T(8,128)S(1)} slice(f32[1,384,1536]{2,1,0:T(8,128)} %get-tuple-element.24.base), slice={[0:1], [264:352], [0:1536]} | slice | bytes 1081344 | tf_op jit(solution)/shard_map/slice | solution.py:265
  93.0 0.9 slice.37.base
  94.0 4.2 %collective-permute-done.5.far = f32[1,264,1536]{2,1,0:T(8,128)} collective-permute-done((f32[1,264,1536]{2,1,0:T(8,128)}, f32[1,264,1536]{2,1,0:T(8,128)}, u32[]{:S(2)}, u32[]{:S(2)}) %collective-permute-start.5) | collective-permute-done | bytes 1622048 | tf_op jit(solution)/shard_map/ppermute | solution.py:244
  98.2 4.0 %shard_map.114.before = f32[1,384,1536]{2,1,0:T(8,128)} custom-call(f32[1,384,1536]{2,1,0:T(8,128)} %get-tuple-element.24.base, f32[1,264,1536]{2,1,0:T(8,128)} %collective-permute-done.5.far, f32[384,2]{1,0:T(8,128)S(1)} %stack.31.weight), custom_call_target="tpu_custom_call", output_to_operand_aliasing={{}: (0, {})} | custom-call | flops 4055040 | bytes 4866048 | tf_op jit(solution)/shard_map/pallas_call | solution.py:177
  102.2 1.7 %collective-permute-done.4.far = f32[1,88,1536]{2,1,0:T(8,128)S(1)} collective-permute-done((f32[1,88,1536]{2,1,0:T(8,128)}, f32[1,88,1536]{2,1,0:T(8,128)S(1)}, u32[]{:S(2)}, u32[]{:S(2)}) %collective-permute-start.4) | collective-permute-done | bytes 540704 | tf_op jit(solution)/shard_map/ppermute | solution.py:244
  103.9 1.0 shard_map.115.before
  104.9 1.1 %collective-permute-done.3.far = f32[1,32,1536]{2,1,0:T(8,128)S(1)} collective-permute-done((f32[1,32,1536]{2,1,0:T(8,128)S(1)}, f32[1,32,1536]{2,1,0:T(8,128)S(1)}, u32[]{:S(2)}, u32[]{:S(2)}) %collective-permute-start.3) | collective-permute-done | bytes 196640 | tf_op jit(solution)/shard_map/ppermute | solution.py:244
  106.0 0.8 shard_map.116
  (30 shorter events, 0.1 us)
Async XLA Ops:
  0.6 19.0 %copy-start.10 = (f32[3]{0:T(128)S(1)}, f32[3]{0:T(128)}, u32[]{:S(2)}) copy-start(f32[3]{0:T(128)} %constant.51) | copy-start | bytes 40
  0.6 11.6 %copy-start.1 = (f32[1,384,1536]{2,1,0:T(8,128)S(1)}, f32[1,384,1536]{2,1,0:T(8,128)}, u32[]{:S(2)}) copy-start(f32[1,384,1536]{2,1,0:T(8,128)} %c_down.1) | copy-start | bytes 7077892
  0.7 27.0 %copy-start = (f32[1,384,1536]{2,1,0:T(8,128)S(1)}, f32[1,384,1536]{2,1,0:T(8,128)}, u32[]{:S(2)}) copy-start(f32[1,384,1536]{2,1,0:T(8,128)} %q_down.1) | copy-start | bytes 7077892
  0.7 6.2 %collective-permute-start.1 = (f32[1,384,1536]{2,1,0:T(8,128)}, f32[1,384,1536]{2,1,0:T(8,128)S(1)}, u32[]{:S(2)}, u32[]{:S(2)}) collective-permute-start(f32[1,384,1536]{2,1,0:T(8,128)} %c_down.1), channel_id=1, source_target_pairs={{0,1},{1,0},{2,3},{3,2},{4,5},{5,4},{6,7},{7,6},{8,9},{9,8},{10,11... | collective-permute-start | bytes 7077896 | tf_op jit(solution)/shard_map/ppermute | solution.py:232
  0.8 80.0 %collective-permute-start = (f32[1,384,1536]{2,1,0:T(8,128)}, f32[1,384,1536]{2,1,0:T(8,128)}, u32[]{:S(2)}, u32[]{:S(2)}) collective-permute-start(f32[1,384,1536]{2,1,0:T(8,128)} %c_down.1), channel_id=1, source_target_pairs={{0,15},{1,2},{2,1},{3,4},{4,3},{5,6},{6,5},{7,8},{8,7},{9,10},{10,... | collective-permute-start | bytes 7077896 | tf_op jit(solution)/shard_map/ppermute | solution.py:231
  3.4 77.4 %collective-permute-start.2 = (f32[1,384,1536]{2,1,0:T(8,128)}, f32[1,384,1536]{2,1,0:T(8,128)}, u32[]{:S(2)}, u32[]{:S(2)}) collective-permute-start(f32[1,384,1536]{2,1,0:T(8,128)} %q_down.1), channel_id=1, source_target_pairs={{0,1},{1,0},{2,3},{3,2},{4,5},{5,4},{6,7},{7,6},{8,9},{9,8},{10,11... | collective-permute-start | bytes 7077896 | tf_op jit(solution)/shard_map/ppermute | solution.py:233
  6.9 1.4 %copy-start.3 = (f32[1,384,1536]{2,1,0:T(8,128)}, f32[1,384,1536]{2,1,0:T(8,128)S(1)}, u32[]{:S(2)}) copy-start(f32[1,384,1536]{2,1,0:T(8,128)S(1)} %collective-permute-done.1.c_near) | copy-start | bytes 7077892
  11.0 87.2 %collective-permute-start.5 = (f32[1,264,1536]{2,1,0:T(8,128)}, f32[1,264,1536]{2,1,0:T(8,128)}, u32[]{:S(2)}, u32[]{:S(2)}) collective-permute-start(f32[1,264,1536]{2,1,0:T(8,128)} %slice.40), channel_id=1, source_target_pairs={{0,15},{1,2},{2,1},{3,4},{4,3},{5,6},{6,5},{7,8},{8,7},{9,10},{10,... | collective-permute-start | bytes 4866056 | tf_op jit(solution)/shard_map/ppermute | solution.py:244
  12.2 0.7 copy-start.5
  12.9 0.7 copy-start.6
  13.6 9.3 %copy-start.8 = (f32[384]{0:T(512)S(1)}, f32[384]{0:T(512)}, u32[]{:S(2)}) copy-start(f32[384]{0:T(512)} %param.14) | copy-start | bytes 4612
  13.6 9.9 %copy-start.7 = (f32[384]{0:T(512)S(1)}, f32[384]{0:T(512)}, u32[]{:S(2)}) copy-start(f32[384]{0:T(512)} %param.15) | copy-start | bytes 4612
  13.6 22.6 %copy-start.9 = (f32[384]{0:T(512)S(1)}, f32[384]{0:T(512)}, u32[]{:S(2)}) copy-start(f32[384]{0:T(512)} %param.16) | copy-start | bytes 4612
  15.8 5.1 %collective-permute-start.6 = (f32[1,256]{1,0:T(1,128)S(1)}, f32[1,256]{1,0:T(1,128)S(1)}, u32[]{:S(2)}, u32[]{:S(2)}) collective-permute-start(f32[1,256]{1,0:T(1,128)S(1)} %get-tuple-element.26), channel_id=1, source_target_pairs={{0,1},{1,0},{2,3},{3,2},{4,5},{5,4},{6,7},{7,6},{8,9},{9,8},{10,11... | collective-permute-start | bytes 3080 | tf_op jit(solution)/shard_map/ppermute | solution.py:40
  20.9 4.8 %collective-permute-start.7 = (f32[1,256]{1,0:T(1,128)S(1)}, f32[1,256]{1,0:T(1,128)S(1)}, u32[]{:S(2)}, u32[]{:S(2)}) collective-permute-start(f32[1,256]{1,0:T(1,128)S(1)} %add.31), channel_id=1, source_target_pairs={{1,5},{2,6},{5,1},{6,2},{9,13},{10,14},{13,9},{14,10},{17,21},{18,... | collective-permute-start | bytes 3080 | tf_op jit(solution)/shard_map/ppermute | solution.py:42
  25.7 5.7 %collective-permute-start.8 = (f32[1,256]{1,0:T(1,128)S(1)}, f32[1,256]{1,0:T(1,128)S(1)}, u32[]{:S(2)}, u32[]{:S(2)}) collective-permute-start(f32[1,256]{1,0:T(1,128)S(1)} %add.32), channel_id=1, source_target_pairs={{1,9},{2,10},{5,13},{6,14},{9,1},{10,2},{13,5},{14,6},{17,25},{18,... | collective-permute-start | bytes 3080 | tf_op jit(solution)/shard_map/ppermute | solution.py:42
  28.5 75.3 %collective-permute-start.4 = (f32[1,88,1536]{2,1,0:T(8,128)}, f32[1,88,1536]{2,1,0:T(8,128)S(1)}, u32[]{:S(2)}, u32[]{:S(2)}) collective-permute-start(f32[1,88,1536]{2,1,0:T(8,128)} %slice.39), channel_id=1, source_target_pairs={{0,15},{1,2},{2,1},{3,4},{4,3},{5,6},{6,5},{7,8},{8,7},{9,10},{10,... | collective-permute-start | bytes 1622024 | tf_op jit(solution)/shard_map/ppermute | solution.py:244
  31.4 2.1 %collective-permute-start.9 = (f32[1,256]{1,0:T(1,128)S(1)}, f32[1,256]{1,0:T(1,128)S(1)}, u32[]{:S(2)}, u32[]{:S(2)}) collective-permute-start(f32[1,256]{1,0:T(1,128)S(1)} %add.33), channel_id=1, source_target_pairs={{1,0},{2,3},{5,4},{6,7},{9,8},{10,11},{13,12},{14,15},{17,16},{18,... | collective-permute-start | bytes 3080 | tf_op jit(solution)/shard_map/ppermute | solution.py:43
  33.5 1.4 %collective-permute-start.10 = (f32[1,256]{1,0:T(1,128)S(1)}, f32[1,256]{1,0:T(1,128)S(1)}, u32[]{:S(2)}, u32[]{:S(2)}) collective-permute-start(f32[1,256]{1,0:T(1,128)S(1)} %collective-permute-done.9), channel_id=1, source_target_pairs={{0,3},{3,0},{4,7},{7,4},{8,11},{11,8},{12,15},{15,12},{16,19},{19,... | collective-permute-start | bytes 3080 | tf_op jit(solution)/shard_map/ppermute | solution.py:44
  34.9 24.0 %collective-permute-start.11 = (f32[1,256]{1,0:T(1,128)S(1)}, f32[1,256]{1,0:T(1,128)S(1)}, u32[]{:S(2)}, u32[]{:S(2)}) collective-permute-start(f32[1,256]{1,0:T(1,128)S(1)} %add.34), channel_id=1, source_target_pairs={{0,1},{3,2},{4,5},{7,6},{8,9},{11,10},{12,13},{15,14},{16,17},{19,... | collective-permute-start | bytes 3080 | tf_op jit(solution)/shard_map/ppermute | solution.py:45
  58.9 47.1 %collective-permute-start.3 = (f32[1,32,1536]{2,1,0:T(8,128)S(1)}, f32[1,32,1536]{2,1,0:T(8,128)S(1)}, u32[]{:S(2)}, u32[]{:S(2)}) collective-permute-start(f32[1,32,1536]{2,1,0:T(8,128)S(1)} %slice.38), channel_id=1, source_target_pairs={{0,15},{1,2},{2,1},{3,4},{4,3},{5,6},{6,5},{7,8},{8,7},{9,10},{10,... | collective-permute-start | bytes 589832 | tf_op jit(solution)/shard_map/ppermute | solution.py:244
  80.8 1.7 %copy-start.2 = (f32[1,384,1536]{2,1,0:T(8,128)S(1)}, f32[1,384,1536]{2,1,0:T(8,128)}, u32[]{:S(2)}) copy-start(f32[1,384,1536]{2,1,0:T(8,128)} %c_down.1) | copy-start | bytes 7077892
  82.5 1.7 %copy-start.4 = (f32[1,384,1536]{2,1,0:T(8,128)S(1)}, f32[1,384,1536]{2,1,0:T(8,128)}, u32[]{:S(2)}) copy-start(f32[1,384,1536]{2,1,0:T(8,128)} %copy-done.3) | copy-start | bytes 7077892

commit v9 on v8

--- a/solution.py
+++ b/solution.py
@@ -238,7 +238,7 @@
     else:
         binned = cell_sum(binned, "ax")
 
-    late, cot_near_rows = lax.optimization_barrier((checkpoint, cot_near_rows))
+    late, wall = lax.optimization_barrier((checkpoint, wall))
     edges = [rows * n // STATE_PARTS for n in STATE_CUTS]
     state_far_rows = [
         lax.ppermute(late[:, low:high], "ax", far) for low, high in zip(edges, edges[1:])

time: 107 us -> 107 us (level)
  waiting for transfers between devices: 51.8 us -> 57.1 us
  starting transfers between devices: 19.5 us -> 15.8 us
  local copies, waits for them, and re-layouts: 12.9 us -> 10.6 us
    ppermute x1, waiting for transfers between devices: 21.4 us -> 25.5 us  [local(): cot_far_rows = lax.ppermute(cotangent, 'ax', far)]
    ppermute x1, starting transfers between devices: 3.47 us -> 0.01 us  [local(): state_near_rows = lax.ppermute(checkpoint, 'ax', near)]
    ppermute x1, starting transfers between devices: 0.12 us -> 2.87 us  [local(): cot_near_rows = lax.ppermute(cotangent, 'ax', near)]
    ppermute x1, starting transfers between devices: 3.19 us -> 0.83 us  [cell_sum(): lax.ppermute(value, axis, [(i, i ^ 1) for i in range(count)])]
    ppermute x2, waiting for transfers between devices: 1.71 us -> 3.97 us  [cell_sum(): value = value + lax.ppermute(value, axis, [(i, i ^ 1 << n) for i in direct])]
    unnamed x22 -> x18, local copies, waits for them, and re-layouts: 6.13 us -> 4.73 us
    ppermute x3, starting transfers between devices: 3.02 us -> 1.74 us  [local(): lax.ppermute(late[:, low:high], 'ax', far)]
    ppermute x3, waiting for transfers between devices: 7.02 us -> 5.84 us  [local(): lax.ppermute(late[:, low:high], 'ax', far)]
  transfers between devices with their start and end apart: 12 -> 12, of which waited for: 8 -> 9; matrix products, arithmetic and copies ran while one was open for 9% -> 9% of each run, Pallas kernels for 14% -> 15%
where the time goes in v9:
time: 107 us
  waiting for transfers between devices  57.1 us (53%)
  Pallas kernels  16.3 us (15%)
  starting transfers between devices  15.8 us (15%)
  local copies, waits for them, and re-layouts  10.6 us (10%)
  between operations  3.48 us (3%)
  other arithmetic  3.35 us (3%)
    ppermute x1, waiting for transfers between devices, local(): cot_far_rows = lax.ppermute(cotangent, 'ax', far)  25.5 us
    ppermute x1, waiting for transfers between devices, cell_sum(): lax.ppermute(value, axis, [(i, i ^ 1) for i in turning])  20.9 us
    pallas_call x1, Pallas kernels, local_parts(): pl.pallas_call(local_kernel, grid=(rows // block,), out_shape=(shape, sha...  8.31 us
    ppermute x3, waiting for transfers between devices, local(): lax.ppermute(late[:, low:high], 'ax', far)  5.84 us
    unnamed x18, local copies, waits for them, and re-layouts  4.73 us
    ppermute x2, starting transfers between devices, cell_sum(): value = value + lax.ppermute(value, axis, [(i, i ^ 1 << n) for i in direct])  4.47 us
    pallas_call x1, Pallas kernels, add_rows(): pl.pallas_call(state_far, grid=(rows // block,), out_shape=jax.ShapeDtype...  4.02 us
    ppermute x2, waiting for transfers between devices, cell_sum(): value = value + lax.ppermute(value, axis, [(i, i ^ 1 << n) for i in direct])  3.97 us
  transfers between devices with their start and end apart: 12, of which 9 were waited for; matrix products, arithmetic and copies ran while one was open for 9% of the time, Pallas kernels for 15%

profile of v9, /device:TPU:1, one launch (start us, length us, event | category | flops | bytes accessed | tf_op | source)
XLA Modules:
  0.0 106.7 jit_solution(13979841828743638943)
XLA Ops:
  0.6 2.7 %collective-permute-start = (f32[1,384,1536]{2,1,0:T(8,128)}, f32[1,384,1536]{2,1,0:T(8,128)}, u32[]{:S(2)}, u32[]{:S(2)}) collective-permute-start(f32[1,384,1536]{2,1,0:T(8,128)} %c_down.1), channel_id=1, source_target_pairs={{0,15},{1,2},{2,1},{3,4},{4,3},{5,6},{6,5},{7,8},{8,7},{9,10},{10,... | collective-permute-start | bytes 7077896 | tf_op jit(solution)/shard_map/ppermute | solution.py:231
  3.3 2.9 %collective-permute-start.1 = (f32[1,384,1536]{2,1,0:T(8,128)}, f32[1,384,1536]{2,1,0:T(8,128)}, u32[]{:S(2)}, u32[]{:S(2)}) collective-permute-start(f32[1,384,1536]{2,1,0:T(8,128)} %c_down.1), channel_id=1, source_target_pairs={{0,1},{1,0},{2,3},{3,2},{4,5},{5,4},{6,7},{7,6},{8,9},{9,8},{10,11... | collective-permute-start | bytes 7077896 | tf_op jit(solution)/shard_map/ppermute | solution.py:232
  6.2 0.0 collective-permute-start.2
  6.2 1.7 %copy-done.1 = f32[1,384,1536]{2,1,0:T(8,128)S(1)} copy-done((f32[1,384,1536]{2,1,0:T(8,128)S(1)}, f32[1,384,1536]{2,1,0:T(8,128)}, u32[]{:S(2)}) %copy-start.1) | copy-done | bytes 2359320
  7.9 0.7 copy-done.3
  8.5 0.7 copy-done.4
  9.2 2.2 %shard_map.112 = (f32[1,1536]{1,0:T(1,128)S(1)}, f32[1,256]{1,0:T(1,128)S(1)}) custom-call(s32[1,1536]{1,0:T(1,128)S(1)} %copy-done.3, f32[1,256]{1,0:T(1,128)S(1)} %bitcast.8, f32[1,384,1536]{2,1,0:T(8,128)S(1)} %copy-done.1), custom_call_target="tpu_custom_call" | custom-call | tf_op jit(solution)/shard_map/pallas_call | solution.py:72
  11.4 0.0 copy-start.6
  11.5 0.0 copy-start.7
  11.5 1.4 %slice.40 = f32[1,264,1536]{2,1,0:T(8,128)} slice(f32[1,384,1536]{2,1,0:T(8,128)S(1)} %copy-done), slice={[0:1], [0:264], [0:1536]} | slice | bytes 3244032 | tf_op jit(solution)/shard_map/slice | solution.py:244
  12.8 0.0 collective-permute-start.5
  12.8 0.8 collective-permute-start.6
  14.3 0.2 collective-permute-done.6
  14.5 1.9 %collective-permute-start.7 = (f32[1,256]{1,0:T(1,128)S(1)}, f32[1,256]{1,0:T(1,128)S(1)}, u32[]{:S(2)}, u32[]{:S(2)}) collective-permute-start(f32[1,256]{1,0:T(1,128)S(1)} %add.31), channel_id=1, source_target_pairs={{1,5},{2,6},{5,1},{6,2},{9,13},{10,14},{13,9},{14,10},{17,21},{18,... | collective-permute-start | bytes 3080 | tf_op jit(solution)/shard_map/ppermute | solution.py:42
  16.4 0.6 fusion.1
  17.0 0.6 slice.32
  17.6 1.7 %collective-permute-done.7 = f32[1,256]{1,0:T(1,128)S(1)} collective-permute-done((f32[1,256]{1,0:T(1,128)S(1)}, f32[1,256]{1,0:T(1,128)S(1)}, u32[]{:S(2)}, u32[]{:S(2)}) %collective-permute-start.7) | collective-permute-done | bytes 1056 | tf_op jit(solution)/shard_map/ppermute | solution.py:42
  19.3 2.6 %collective-permute-start.8 = (f32[1,256]{1,0:T(1,128)S(1)}, f32[1,256]{1,0:T(1,128)S(1)}, u32[]{:S(2)}, u32[]{:S(2)}) collective-permute-start(f32[1,256]{1,0:T(1,128)S(1)} %add.32), channel_id=1, source_target_pairs={{1,9},{2,10},{5,13},{6,14},{9,1},{10,2},{13,5},{14,6},{17,25},{18,... | collective-permute-start | bytes 3080 | tf_op jit(solution)/shard_map/ppermute | solution.py:42
  21.8 0.7 pad_maximum_fusion
  22.6 0.1 slice.34
  22.6 2.3 %collective-permute-done.8 = f32[1,256]{1,0:T(1,128)S(1)} collective-permute-done((f32[1,256]{1,0:T(1,128)S(1)}, f32[1,256]{1,0:T(1,128)S(1)}, u32[]{:S(2)}, u32[]{:S(2)}) %collective-permute-start.8) | collective-permute-done | bytes 1056 | tf_op jit(solution)/shard_map/ppermute | solution.py:42
  24.9 1.3 %collective-permute-start.9 = (f32[1,256]{1,0:T(1,128)S(1)}, f32[1,256]{1,0:T(1,128)S(1)}, u32[]{:S(2)}, u32[]{:S(2)}) collective-permute-start(f32[1,256]{1,0:T(1,128)S(1)} %add.33), channel_id=1, source_target_pairs={{1,0},{2,3},{5,4},{6,7},{9,8},{10,11},{13,12},{14,15},{17,16},{18,... | collective-permute-start | bytes 3080 | tf_op jit(solution)/shard_map/ppermute | solution.py:43
  26.2 0.1 pad_maximum_fusion.1
  26.3 0.7 collective-permute-done.9
  27.0 0.6 collective-permute-start.10
  27.7 0.9 slice.39
  28.6 0.7 slice.38
  29.2 0.0 collective-permute-done.10
  29.3 1.3 %collective-permute-start.11 = (f32[1,256]{1,0:T(1,128)S(1)}, f32[1,256]{1,0:T(1,128)S(1)}, u32[]{:S(2)}, u32[]{:S(2)}) collective-permute-start(f32[1,256]{1,0:T(1,128)S(1)} %add.34), channel_id=1, source_target_pairs={{0,1},{3,2},{4,5},{7,6},{8,9},{11,10},{12,13},{15,14},{16,17},{19,... | collective-permute-start | bytes 3080 | tf_op jit(solution)/shard_map/ppermute | solution.py:45
  30.6 0.1 copy.21.coef
  31.5 20.9 %collective-permute-done.11 = f32[1,256]{1,0:T(1,128)S(1)} collective-permute-done((f32[1,256]{1,0:T(1,128)S(1)}, f32[1,256]{1,0:T(1,128)S(1)}, u32[]{:S(2)}, u32[]{:S(2)}) %collective-permute-start.11) | collective-permute-done | bytes 1056 | tf_op jit(solution)/shard_map/ppermute | solution.py:45
  52.4 0.0 collective-permute-start.4
  52.4 0.6 multiply_add_fusion
  53.1 0.1 stack.32
  54.5 0.7 pad_maximum_fusion.2.scal
  55.2 25.5 %collective-permute-done.c_far = f32[1,384,1536]{2,1,0:T(8,128)} collective-permute-done((f32[1,384,1536]{2,1,0:T(8,128)}, f32[1,384,1536]{2,1,0:T(8,128)}, u32[]{:S(2)}, u32[]{:S(2)}) %collective-permute-start) | collective-permute-done | bytes 2359328 | tf_op jit(solution)/shard_map/ppermute | solution.py:231
  80.7 1.7 %collective-permute-start.3 = (f32[1,32,1536]{2,1,0:T(8,128)}, f32[1,32,1536]{2,1,0:T(8,128)S(1)}, u32[]{:S(2)}, u32[]{:S(2)}) collective-permute-start(f32[1,32,1536]{2,1,0:T(8,128)} %slice.38), channel_id=1, source_target_pairs={{0,15},{1,2},{2,1},{3,4},{4,3},{5,6},{6,5},{7,8},{8,7},{9,10},{10,... | collective-permute-start | bytes 589832 | tf_op jit(solution)/shard_map/ppermute | solution.py:244
  82.5 0.6 fusion
  83.0 1.7 %copy-done.2 = f32[1,384,1536]{2,1,0:T(8,128)S(1)} copy-done((f32[1,384,1536]{2,1,0:T(8,128)S(1)}, f32[1,384,1536]{2,1,0:T(8,128)}, u32[]{:S(2)}) %copy-start.2) | copy-done | bytes 2359320
  84.7 8.3 %shard_map.113 = (f32[1,384,1536]{2,1,0:T(8,128)}, f32[1,384,1536]{2,1,0:T(8,128)}) custom-call(f32[2]{0:T(128)S(1)} %pad_maximum_fusion.2.scal, f32[1,384,1536]{2,1,0:T(8,128)S(1)} %copy-done, f32[1,384,1536]{2,1,0:T(8,128)S(1)} %copy-done, f32[1,384,1536]{2,1,0:T(8,128)S(1)} %copy-done, f32[1,384,1536]{2,1,0:T(8,128)} %collective-permute-done.2.q_near, ...), custom_call_target="tpu_custom_call" | custom-call | flops 29491200 | bytes 16515072 | tf_op jit(solution)/shard_map/pallas_call | solution.py:147
  93.0 1.1 %slice.36.base = f32[1,88,1536]{2,1,0:T(8,128)S(1)} slice(f32[1,384,1536]{2,1,0:T(8,128)} %get-tuple-element.24.base), slice={[0:1], [264:352], [0:1536]} | slice | bytes 1081344 | tf_op jit(solution)/shard_map/slice | solution.py:265
  94.1 0.9 slice.37.base
  95.0 3.1 %collective-permute-done.5.far = f32[1,264,1536]{2,1,0:T(8,128)} collective-permute-done((f32[1,264,1536]{2,1,0:T(8,128)}, f32[1,264,1536]{2,1,0:T(8,128)}, u32[]{:S(2)}, u32[]{:S(2)}) %collective-permute-start.5) | collective-permute-done | bytes 1622048 | tf_op jit(solution)/shard_map/ppermute | solution.py:244
  98.1 4.0 %shard_map.114.before = f32[1,384,1536]{2,1,0:T(8,128)} custom-call(f32[1,384,1536]{2,1,0:T(8,128)} %get-tuple-element.24.base, f32[1,264,1536]{2,1,0:T(8,128)} %collective-permute-done.5.far, f32[384,2]{1,0:T(8,128)S(1)} %stack.31.weight), custom_call_target="tpu_custom_call", output_to_operand_aliasing={{}: (0, {})} | custom-call | flops 4055040 | bytes 4866048 | tf_op jit(solution)/shard_map/pallas_call | solution.py:177
  102.1 1.7 %collective-permute-done.4.far = f32[1,88,1536]{2,1,0:T(8,128)S(1)} collective-permute-done((f32[1,88,1536]{2,1,0:T(8,128)}, f32[1,88,1536]{2,1,0:T(8,128)S(1)}, u32[]{:S(2)}, u32[]{:S(2)}) %collective-permute-start.4) | collective-permute-done | bytes 540704 | tf_op jit(solution)/shard_map/ppermute | solution.py:244
  103.8 1.0 shard_map.115.before
  104.8 1.1 %collective-permute-done.3.far = f32[1,32,1536]{2,1,0:T(8,128)S(1)} collective-permute-done((f32[1,32,1536]{2,1,0:T(8,128)}, f32[1,32,1536]{2,1,0:T(8,128)S(1)}, u32[]{:S(2)}, u32[]{:S(2)}) %collective-permute-start.3) | collective-permute-done | bytes 196640 | tf_op jit(solution)/shard_map/ppermute | solution.py:244
  105.9 0.8 shard_map.116
  (26 shorter events, 0.1 us)
Async XLA Ops:
  0.6 10.8 %copy-start = (f32[1,384,1536]{2,1,0:T(8,128)S(1)}, f32[1,384,1536]{2,1,0:T(8,128)}, u32[]{:S(2)}) copy-start(f32[1,384,1536]{2,1,0:T(8,128)} %q_down.1) | copy-start | bytes 7077892
  0.6 80.1 %collective-permute-start = (f32[1,384,1536]{2,1,0:T(8,128)}, f32[1,384,1536]{2,1,0:T(8,128)}, u32[]{:S(2)}, u32[]{:S(2)}) collective-permute-start(f32[1,384,1536]{2,1,0:T(8,128)} %c_down.1), channel_id=1, source_target_pairs={{0,15},{1,2},{2,1},{3,4},{4,3},{5,6},{6,5},{7,8},{8,7},{9,10},{10,... | collective-permute-start | bytes 7077896 | tf_op jit(solution)/shard_map/ppermute | solution.py:231
  3.3 79.7 %collective-permute-start.1 = (f32[1,384,1536]{2,1,0:T(8,128)}, f32[1,384,1536]{2,1,0:T(8,128)}, u32[]{:S(2)}, u32[]{:S(2)}) collective-permute-start(f32[1,384,1536]{2,1,0:T(8,128)} %c_down.1), channel_id=1, source_target_pairs={{0,1},{1,0},{2,3},{3,2},{4,5},{5,4},{6,7},{7,6},{8,9},{9,8},{10,11... | collective-permute-start | bytes 7077896 | tf_op jit(solution)/shard_map/ppermute | solution.py:232
  6.2 76.9 %collective-permute-start.2 = (f32[1,384,1536]{2,1,0:T(8,128)}, f32[1,384,1536]{2,1,0:T(8,128)}, u32[]{:S(2)}, u32[]{:S(2)}) collective-permute-start(f32[1,384,1536]{2,1,0:T(8,128)} %q_down.1), channel_id=1, source_target_pairs={{0,1},{1,0},{2,3},{3,2},{4,5},{5,4},{6,7},{7,6},{8,9},{9,8},{10,11... | collective-permute-start | bytes 7077896 | tf_op jit(solution)/shard_map/ppermute | solution.py:233
  6.2 1.7 %copy-start.1 = (f32[1,384,1536]{2,1,0:T(8,128)S(1)}, f32[1,384,1536]{2,1,0:T(8,128)}, u32[]{:S(2)}) copy-start(f32[1,384,1536]{2,1,0:T(8,128)} %c_down.1) | copy-start | bytes 7077892
  7.8 0.7 copy-start.3
  8.5 0.7 copy-start.4
  9.2 7.2 %copy-start.8 = (f32[3]{0:T(128)S(1)}, f32[3]{0:T(128)}, u32[]{:S(2)}) copy-start(f32[3]{0:T(128)} %constant.51) | copy-start | bytes 40
  9.2 7.8 %copy-start.5 = (f32[384]{0:T(512)S(1)}, f32[384]{0:T(512)}, u32[]{:S(2)}) copy-start(f32[384]{0:T(512)} %param.15) | copy-start | bytes 4612
  11.4 19.1 %copy-start.6 = (f32[384]{0:T(512)S(1)}, f32[384]{0:T(512)}, u32[]{:S(2)}) copy-start(f32[384]{0:T(512)} %param.14) | copy-start | bytes 4612
  11.5 19.1 %copy-start.7 = (f32[384]{0:T(512)S(1)}, f32[384]{0:T(512)}, u32[]{:S(2)}) copy-start(f32[384]{0:T(512)} %param.16) | copy-start | bytes 4612
  12.8 85.3 %collective-permute-start.5 = (f32[1,264,1536]{2,1,0:T(8,128)}, f32[1,264,1536]{2,1,0:T(8,128)}, u32[]{:S(2)}, u32[]{:S(2)}) collective-permute-start(f32[1,264,1536]{2,1,0:T(8,128)} %slice.40), channel_id=1, source_target_pairs={{0,15},{1,2},{2,1},{3,4},{4,3},{5,6},{6,5},{7,8},{8,7},{9,10},{10,... | collective-permute-start | bytes 4866056 | tf_op jit(solution)/shard_map/ppermute | solution.py:244
  12.8 1.7 %collective-permute-start.6 = (f32[1,256]{1,0:T(1,128)S(1)}, f32[1,256]{1,0:T(1,128)S(1)}, u32[]{:S(2)}, u32[]{:S(2)}) collective-permute-start(f32[1,256]{1,0:T(1,128)S(1)} %get-tuple-element.26), channel_id=1, source_target_pairs={{0,1},{1,0},{2,3},{3,2},{4,5},{5,4},{6,7},{7,6},{8,9},{9,8},{10,11... | collective-permute-start | bytes 3080 | tf_op jit(solution)/shard_map/ppermute | solution.py:40
  14.5 4.8 %collective-permute-start.7 = (f32[1,256]{1,0:T(1,128)S(1)}, f32[1,256]{1,0:T(1,128)S(1)}, u32[]{:S(2)}, u32[]{:S(2)}) collective-permute-start(f32[1,256]{1,0:T(1,128)S(1)} %add.31), channel_id=1, source_target_pairs={{1,5},{2,6},{5,1},{6,2},{9,13},{10,14},{13,9},{14,10},{17,21},{18,... | collective-permute-start | bytes 3080 | tf_op jit(solution)/shard_map/ppermute | solution.py:42
  19.3 5.7 %collective-permute-start.8 = (f32[1,256]{1,0:T(1,128)S(1)}, f32[1,256]{1,0:T(1,128)S(1)}, u32[]{:S(2)}, u32[]{:S(2)}) collective-permute-start(f32[1,256]{1,0:T(1,128)S(1)} %add.32), channel_id=1, source_target_pairs={{1,9},{2,10},{5,13},{6,14},{9,1},{10,2},{13,5},{14,6},{17,25},{18,... | collective-permute-start | bytes 3080 | tf_op jit(solution)/shard_map/ppermute | solution.py:42
  24.9 2.1 %collective-permute-start.9 = (f32[1,256]{1,0:T(1,128)S(1)}, f32[1,256]{1,0:T(1,128)S(1)}, u32[]{:S(2)}, u32[]{:S(2)}) collective-permute-start(f32[1,256]{1,0:T(1,128)S(1)} %add.33), channel_id=1, source_target_pairs={{1,0},{2,3},{5,4},{6,7},{9,8},{10,11},{13,12},{14,15},{17,16},{18,... | collective-permute-start | bytes 3080 | tf_op jit(solution)/shard_map/ppermute | solution.py:43
  27.0 2.2 %collective-permute-start.10 = (f32[1,256]{1,0:T(1,128)S(1)}, f32[1,256]{1,0:T(1,128)S(1)}, u32[]{:S(2)}, u32[]{:S(2)}) collective-permute-start(f32[1,256]{1,0:T(1,128)S(1)} %collective-permute-done.9), channel_id=1, source_target_pairs={{0,3},{3,0},{4,7},{7,4},{8,11},{11,8},{12,15},{15,12},{16,19},{19,... | collective-permute-start | bytes 3080 | tf_op jit(solution)/shard_map/ppermute | solution.py:44
  29.3 23.1 %collective-permute-start.11 = (f32[1,256]{1,0:T(1,128)S(1)}, f32[1,256]{1,0:T(1,128)S(1)}, u32[]{:S(2)}, u32[]{:S(2)}) collective-permute-start(f32[1,256]{1,0:T(1,128)S(1)} %add.34), channel_id=1, source_target_pairs={{0,1},{3,2},{4,5},{7,6},{8,9},{11,10},{12,13},{15,14},{16,17},{19,... | collective-permute-start | bytes 3080 | tf_op jit(solution)/shard_map/ppermute | solution.py:45
  52.4 51.4 %collective-permute-start.4 = (f32[1,88,1536]{2,1,0:T(8,128)}, f32[1,88,1536]{2,1,0:T(8,128)S(1)}, u32[]{:S(2)}, u32[]{:S(2)}) collective-permute-start(f32[1,88,1536]{2,1,0:T(8,128)} %slice.39), channel_id=1, source_target_pairs={{0,15},{1,2},{2,1},{3,4},{4,3},{5,6},{6,5},{7,8},{8,7},{9,10},{10,... | collective-permute-start | bytes 1622024 | tf_op jit(solution)/shard_map/ppermute | solution.py:244
  80.7 25.2 %collective-permute-start.3 = (f32[1,32,1536]{2,1,0:T(8,128)}, f32[1,32,1536]{2,1,0:T(8,128)S(1)}, u32[]{:S(2)}, u32[]{:S(2)}) collective-permute-start(f32[1,32,1536]{2,1,0:T(8,128)} %slice.38), channel_id=1, source_target_pairs={{0,15},{1,2},{2,1},{3,4},{4,3},{5,6},{6,5},{7,8},{8,7},{9,10},{10,... | collective-permute-start | bytes 589832 | tf_op jit(solution)/shard_map/ppermute | solution.py:244
  83.0 1.7 %copy-start.2 = (f32[1,384,1536]{2,1,0:T(8,128)S(1)}, f32[1,384,1536]{2,1,0:T(8,128)}, u32[]{:S(2)}) copy-start(f32[1,384,1536]{2,1,0:T(8,128)} %c_down.1) | copy-start | bytes 7077892
